TPU v7x, 32 devices: a whole 2x2x4 slice. The times are simulated.
32 devices in a mesh: blk: 8 (over y, x, core), narrow: 4 (over z).
Axes of the slice: x: 2, y: 2, z: 4, core: 2. Of those that a mesh axis runs over, the one named last changes fastest.
Arguments:
- student_bytes: bfloat16 [16384, 2048], P(('blk', 'narrow')), may hold values from -6 to 6
- student_weight: bfloat16 [2048, 1024], replicated, may hold values from -0.125 to 0.125
- teacher_rows: bfloat16 [4096, 8192], P('blk', 'narrow'), may hold values from -6 to 6
- teacher_weight: bfloat16 [8192, 1024], P('narrow'), may hold values from -0.0625 to 0.0625
- span_lengths: int32 [8, 512], P('blk'), may hold values from 1 to 16, 2048 in all within a row
- span_scale: float32 [4096], P(('blk', 'narrow')), may hold values from 20 to 4000
- positives: int32 [4096], P(('blk', 'narrow')), may hold values from 0 to 2047
Outputs:
- loss_mean: float32 [], replicated
- grad_bytes: bfloat16 [16384, 2048], P(('blk', 'narrow'))
- grad_teacher_weight: float32 [8192, 1024], P('narrow')
All inputs are finite; a program needn't handle non-finite values.
Results may differ from a plain program's by a relative error of at most 0.007.
The roundings to bfloat16 on the way count: a program that leaves them out, or rounds other values in their place, can miss the bound.
Values may be sent and summed in bfloat16 or wider, within the bound.
No kernel may reach another device: no remote copies, remote signals or barrier semaphores. Data moves between devices by JAX's collectives and lax.ppermute only.
A program may use at most 128 MiB of HBM per device.

v0:
```python
import jax
import jax.numpy as jnp
from jax import lax
from jax.sharding import PartitionSpec as P

STOPS = 4


EPS = 1e-06


def shifted(x, axis, by):
    devices = lax.axis_size(axis)
    return lax.ppermute(x, axis, [(i, (i + by) % devices) for i in range(devices)])


def normalize(values):
    inv_rms = lax.rsqrt(jnp.mean(values * values, axis=-1, keepdims=True) + EPS)
    return (values * inv_rms, inv_rms)


def norm_back(upstream, normed, inv_rms):
    inner_mean = jnp.mean(upstream * normed, axis=-1, keepdims=True)
    return inv_rms * (upstream - normed * inner_mean)


def contract_first(left, right):
    return lax.dot_general(
        left, right, (((0,), (0,)), ((), ())), preferred_element_type=jnp.float32
    )


def shards(
    student_bytes, student_weight, teacher_rows, teacher_weight, span_lengths, span_scale, positives
):
    span_dev = span_scale.shape[0]
    embed_width = student_weight.shape[1]
    lane_count = lax.axis_size("narrow")
    lane_index = lax.axis_index("narrow")
    span_block = span_dev * lane_count
    byte_dev = student_bytes.shape[0]
    byte_lengths = span_lengths[0]
    byte_ends = jnp.cumsum(byte_lengths)
    byte_starts = byte_ends - byte_lengths

    def owner_order(values):
        return values.reshape(span_dev, lane_count).T.reshape(span_block)

    lengths = owner_order(byte_lengths)
    span_ends = owner_order(byte_ends)
    starts = owner_order(byte_starts)
    own_first = lane_index * span_dev
    own_lengths = lax.dynamic_slice_in_dim(lengths, own_first, span_dev).astype(jnp.float32)[
        :, None
    ]
    byte_pos = lane_index * byte_dev + jnp.arange(byte_dev, dtype=jnp.int32)
    span_table = (
        (byte_pos[None, :] >= starts[:, None]) & (byte_pos[None, :] < span_ends[:, None])
    ).astype(jnp.bfloat16)
    projected = jnp.dot(student_bytes, student_weight, preferred_element_type=jnp.float32).astype(
        jnp.bfloat16
    )
    pooled = lax.psum_scatter(
        jnp.dot(span_table, projected, preferred_element_type=jnp.float32),
        "narrow",
        scatter_dimension=0,
        tiled=True,
    )
    span_mean = pooled / own_lengths
    student_full, student_rms = normalize(span_mean)
    student = student_full.astype(jnp.bfloat16)
    row_block = teacher_rows
    teacher_proj = lax.psum_scatter(
        jnp.dot(row_block, teacher_weight, preferred_element_type=jnp.float32),
        "narrow",
        scatter_dimension=0,
        tiled=True,
    )
    teacher_full, teacher_rms = normalize(teacher_proj)
    teacher = teacher_full.astype(jnp.bfloat16)
    blocks = []
    teacher_block = lax.all_gather(teacher, "narrow", axis=0, tiled=True)
    for stop_index in range(STOPS):
        if stop_index > 0:
            teacher_block = shifted(teacher_block, "blk", 1)
        blocks.append(teacher_block)
    factor = span_scale[:, None] / embed_width
    window_keys = jnp.concatenate(blocks, axis=0)
    scores = jnp.dot(student, window_keys.T, preferred_element_type=jnp.float32) * factor
    row_max = jnp.max(scores, axis=1, keepdims=True)
    log_total = row_max[:, 0] + jnp.log(jnp.sum(jnp.exp(scores - row_max), axis=1))
    column = jnp.arange(STOPS * span_block, dtype=jnp.int32)
    positive_mask = column[None, :] == positives[:, None]
    picked = jnp.sum(jnp.where(positive_mask, scores, 0.0), axis=1)
    loss_part = jnp.sum(log_total - picked)
    loss_mean = lax.psum(loss_part, ("blk", "narrow")) / (span_block * lax.axis_size("blk"))
    score_grads = (
        (jnp.exp(scores - log_total[:, None]) - positive_mask.astype(jnp.float32)) * factor
    ).astype(jnp.bfloat16)
    dstudent = jnp.dot(score_grads, window_keys, preferred_element_type=jnp.float32)
    partials = [
        contract_first(
            score_grads[:, stop_index * span_block : (stop_index + 1) * span_block], student
        )
        for stop_index in range(STOPS)
    ]
    carried = partials[STOPS - 1]
    for stop_index in range(STOPS - 2, -1, -1):
        carried = shifted(carried, "blk", -1) + partials[stop_index]
    dteacher = lax.psum_scatter(carried, "narrow", scatter_dimension=0, tiled=True)
    span_grad = (norm_back(dstudent, student_full, student_rms) / own_lengths).astype(jnp.bfloat16)
    block_grads = lax.all_gather(span_grad, "narrow", axis=0, tiled=True)
    byte_grad = contract_first(span_table, block_grads).astype(jnp.bfloat16)
    grad_bytes = lax.dot_general(
        byte_grad, student_weight, (((1,), (1,)), ((), ())), preferred_element_type=jnp.float32
    ).astype(jnp.bfloat16)
    teacher_grad = norm_back(dteacher, teacher_full, teacher_rms).astype(jnp.bfloat16)
    row_block = teacher_rows
    local_grad = contract_first(
        row_block, lax.all_gather(teacher_grad, "narrow", axis=0, tiled=True)
    )
    grad_teacher_weight = lax.psum(local_grad, "blk")
    return (loss_mean, grad_bytes, grad_teacher_weight)


def solution(mesh):
    return jax.shard_map(
        shards,
        mesh=mesh,
        in_specs=(
            P(("blk", "narrow"), None),
            P(),
            P("blk", "narrow"),
            P("narrow", None),
            P("blk", None),
            P(("blk", "narrow")),
            P(("blk", "narrow")),
        ),
        out_specs=(P(), P(("blk", "narrow"), None), P("narrow", None)),
        check_vma=False,
    )
```

profile of v0, /device:TPU:0, one launch (start us, length us, event | category | flops | bytes accessed | tf_op | source)
XLA Modules:
  0.0 482.1 jit_solution(1676320619805525990)
XLA Ops:
  8.8 5.8 %fusion.18 = f32[512,1024]{1,0:T(8,128)} fusion(bf16[512,2048]{1,0:T(8,128)(2,1)S(1)} %copy-done, bf16[2048,1024]{1,0:T(8,128)(2,1)} %param.10), kind=kOutput, calls=%fused_computation.51 | convolution fusion | flops 2147483648 | bytes 8388608 | tf_op jit(solution)/shard_map/dot_general | solution.py:74
  14.7 46.7 %reduce-scatter.6.cloned.1.call-done = f32[128,1024]{1,0:T(8,128)} async-done(((f32[512,1024]{1,0:T(8,128)}), f32[128,1024]{1,0:T(8,128)}) %reduce-scatter.6.cloned.1.call-update) | async-done | bytes 524304 | tf_op jit(solution)/shard_map/reduce_scatter | solution.py:73
  62.5 1.8 multiply_convert_fusion.2
  66.8 7.1 %fusion = f32[512,1024]{1,0:T(8,128)} fusion(bf16[512,2048]{1,0:T(8,128)(2,1)} %param.7, bf16[2048,1024]{1,0:T(8,128)(2,1)} %param.8, s32[512]{0:T(512)S(1)} %iota_add_fusion, s32[512]{0:T(512)S(1)} %bitcast.31, s32[512]{0:T(512)S(1)} %bitcast.29), kind=kOutput, calls=%fused_computation.6 | convolution fusion | flops 2685665280 | bytes 8394752 | tf_op jit(solution)/shard_map/dot_general | solution.py:64
  73.9 17.9 %all-gather.4.cloned.1.call-done = bf16[512,1024]{1,0:T(8,128)(2,1)} async-done(((bf16[128,1024]{1,0:T(8,128)(2,1)}), bf16[512,1024]{1,0:T(8,128)(2,1)}) %all-gather.4.cloned.1.call-update) | async-done | bytes 1048592 | tf_op jit(solution)/shard_map/all_gather | solution.py:82
  91.8 15.3 %collective-permute-done = bf16[512,1024]{1,0:T(8,128)(2,1)S(1)} collective-permute-done((bf16[512,1024]{1,0:T(8,128)(2,1)}, bf16[512,1024]{1,0:T(8,128)(2,1)S(1)}, u32[]{:S(2)}, u32[]{:S(2)}) %collective-permute-start) | collective-permute-done | bytes 1048608 | tf_op jit(solution)/shard_map/ppermute | solution.py:14
  107.3 15.1 %collective-permute-done.1 = bf16[512,1024]{1,0:T(8,128)(2,1)} collective-permute-done((bf16[512,1024]{1,0:T(8,128)(2,1)S(1)}, bf16[512,1024]{1,0:T(8,128)(2,1)}, u32[]{:S(2)}, u32[]{:S(2)}) %collective-permute-start.1) | collective-permute-done | bytes 1048608 | tf_op jit(solution)/shard_map/ppermute | solution.py:14
  122.3 15.8 %reduce-scatter.4.cloned.1.call-done = f32[128,1024]{1,0:T(8,128)} async-done(((f32[512,1024]{1,0:T(8,128)}), f32[128,1024]{1,0:T(8,128)}) %reduce-scatter.4.cloned.1.call-update) | async-done | bytes 524304 | tf_op jit(solution)/shard_map/reduce_scatter | solution.py:63
  148.3 1.7 collective-permute-start.3
  150.0 23.6 %collective-permute-done.3 = f32[512,1024]{1,0:T(8,128)S(1)} collective-permute-done((f32[512,1024]{1,0:T(8,128)S(1)}, f32[512,1024]{1,0:T(8,128)S(1)}, u32[]{:S(2)}, u32[]{:S(2)}) %collective-permute-start.3) | collective-permute-done | bytes 2097184 | tf_op jit(solution)/shard_map/ppermute | solution.py:14
  174.0 2.9 collective-permute-start.4
  177.3 23.1 %collective-permute-done.4 = f32[512,1024]{1,0:T(8,128)S(1)} collective-permute-done((f32[512,1024]{1,0:T(8,128)S(1)}, f32[512,1024]{1,0:T(8,128)S(1)}, u32[]{:S(2)}, u32[]{:S(2)}) %collective-permute-start.4) | collective-permute-done | bytes 2097184 | tf_op jit(solution)/shard_map/ppermute | solution.py:14
  200.9 2.9 collective-permute-start.5
  204.3 23.1 %collective-permute-done.5 = f32[512,1024]{1,0:T(8,128)S(1)} collective-permute-done((f32[512,1024]{1,0:T(8,128)S(1)}, f32[512,1024]{1,0:T(8,128)S(1)}, u32[]{:S(2)}, u32[]{:S(2)}) %collective-permute-start.5) | collective-permute-done | bytes 2097184 | tf_op jit(solution)/shard_map/ppermute | solution.py:14
  227.4 1.7 add.63
  229.1 44.0 %reduce-scatter.8.cloned.1.call-done = f32[128,1024]{1,0:T(8,128)} async-done(((f32[512,1024]{1,0:T(8,128)}), f32[128,1024]{1,0:T(8,128)}) %reduce-scatter.8.cloned.1.call-update) | async-done | bytes 524304 | tf_op jit(solution)/shard_map/reduce_scatter | solution.py:110
  274.3 1.9 multiply_convert_fusion.1
  276.3 3.2 multiply_reduce_fusion.1
  280.7 23.0 %all-gather.8.cloned.1.call-done = bf16[512,1024]{1,0:T(8,128)(2,1)} async-done(((bf16[128,1024]{1,0:T(8,128)(2,1)}), bf16[512,1024]{1,0:T(8,128)(2,1)}) %all-gather.8.cloned.1.call-update) | async-done | bytes 1048592 | tf_op jit(solution)/shard_map/all_gather | solution.py:120
  303.7 7.0 %convolution_bitcast_fusion = f32[2048,1024]{0,1:T(8,128)} fusion(bf16[512,1024]{1,0:T(8,128)(2,1)} %all-gather.8.cloned.1.call-done, bf16[512,2048]{1,0:T(8,128)(2,1)S(1)} %copy-done), kind=kOutput, calls=%fused_computation | convolution fusion | flops 2147483648 | bytes 11534336 | tf_op jit(solution)/shard_map/dot_general | solution.py:28
  310.7 41.4 %psum.14 = f32[]{:T(128)} all-reduce(f32[]{:T(128)} %get-tuple-element.11), channel_id=1, replica_groups=mesh['blk'=8,'narrow'=4] {'blk','narrow'}, use_global_device_ids=true, to_apply=%region_10.11 | all-reduce | flops 1 | bytes 8 | tf_op jit(solution)/shard_map/psum | solution.py:96
  352.8 7.0 %convolution_convert_fusion = bf16[512,2048]{1,0:T(8,128)(2,1)} fusion(bf16[2048,1024]{1,0:T(8,128)(2,1)} %param.8, bf16[512,1024]{1,0:T(8,128)(2,1)} %all-gather.6.cloned.1.call-done, s32[512]{0:T(512)S(1)} %iota_add_fusion, s32[512]{0:T(512)S(1)} %bitcast.32, s32[512]{0:T(512)S(1)} %bitcast.30), kind=kOutput, calls=%fused_computation.1 | convolution fusion | flops 2686713856 | bytes 7346176 | tf_op jit(solution)/shard_map/dot_general | solution.py:114
  359.8 105.2 %all-reduce.2.cloned.1.call-done = f32[2048,1024]{0,1:T(8,128)} async-done(((f32[2048,1024]{0,1:T(8,128)}), f32[2048,1024]{0,1:T(8,128)}) %all-reduce.2.cloned.1.call-update) | async-done | bytes 8388624 | tf_op jit(solution)/shard_map/psum | solution.py:122
  464.9 9.2 %copy.14 = f32[2048,1024]{1,0:T(8,128)} copy(f32[2048,1024]{0,1:T(8,128)} %all-reduce.2.cloned.1.call-done) | data formatting | bytes 16777216
  (74 shorter events, 19.9 us)
Async XLA Ops:
  7.2 1.6 copy-start
  7.2 57.3 %copy-start.5 = (s32[1,512]{1,0:T(1,128)S(1)}, s32[1,512]{1,0:T(1,128)}, u32[]{:S(2)}) copy-start(s32[1,512]{1,0:T(1,128)} %param.11) | copy-start | bytes 6148
  7.2 54.2 %reduce-scatter.6.cloned.1.call-start = ((), (), s32[]{:S(2)}) async-start(), calls=%async_computation.4 | async-start | bytes 2621440 | tf_op jit(solution)/shard_map/reduce_scatter | solution.py:73
  14.6 77.2 %all-gather.4.cloned.1.call-start = ((), (), s32[]{:S(2)}) async-start(), calls=%async_computation.5 | async-start | bytes 1310720 | tf_op jit(solution)/shard_map/all_gather | solution.py:82
  64.4 73.8 %reduce-scatter.4.cloned.1.call-start = ((), (), s32[]{:S(2)}) async-start(), calls=%async_computation.3 | async-start | bytes 2621440 | tf_op jit(solution)/shard_map/reduce_scatter | solution.py:63
  66.8 40.5 %copy-start.7 = (f32[128]{0:T(128)S(1)}, f32[128]{0:T(128)}, u32[]{:S(2)}) copy-start(f32[128]{0:T(128)} %param.12) | copy-start | bytes 1540
  73.9 199.2 %reduce-scatter.8.cloned.1.call-start = ((), (), s32[]{:S(2)}) async-start(), calls=%async_computation.7 | async-start | bytes 2621440 | tf_op jit(solution)/shard_map/reduce_scatter | solution.py:110
  91.8 15.3 %collective-permute-start = (bf16[512,1024]{1,0:T(8,128)(2,1)}, bf16[512,1024]{1,0:T(8,128)(2,1)S(1)}, u32[]{:S(2)}, u32[]{:S(2)}) collective-permute-start(bf16[512,1024]{1,0:T(8,128)(2,1)} %all-gather.4.cloned.1.call-done), channel_id=1, source_target_pairs={{0,4},{4,8},{8,12},{12,16},{16,20},{20,24},{24,28},{28,0},{1,5},{5... | collective-permute-start | bytes 3145736 | tf_op jit(solution)/shard_map/ppermute | solution.py:14
  107.1 15.2 %collective-permute-start.1 = (bf16[512,1024]{1,0:T(8,128)(2,1)S(1)}, bf16[512,1024]{1,0:T(8,128)(2,1)}, u32[]{:S(2)}, u32[]{:S(2)}) collective-permute-start(bf16[512,1024]{1,0:T(8,128)(2,1)S(1)} %collective-permute-done), channel_id=1, source_target_pairs={{0,4},{4,8},{8,12},{12,16},{16,20},{20,24},{24,28},{28,0},{1,5},{5... | collective-permute-start | bytes 3145736 | tf_op jit(solution)/shard_map/ppermute | solution.py:14
  122.3 20.9 %collective-permute-start.2 = (bf16[512,1024]{1,0:T(8,128)(2,1)}, bf16[512,1024]{1,0:T(8,128)(2,1)}, u32[]{:S(2)}, u32[]{:S(2)}) collective-permute-start(bf16[512,1024]{1,0:T(8,128)(2,1)} %collective-permute-done.1), channel_id=1, source_target_pairs={{0,4},{4,8},{8,12},{12,16},{16,20},{20,24},{24,28},{28,0},{1,5},{5... | collective-permute-start | bytes 3145736 | tf_op jit(solution)/shard_map/ppermute | solution.py:14
  143.3 2.9 copy-start.6
  144.6 3.7 copy-start.2
  147.8 56.0 %copy-start.4 = (bf16[128,2048]{1,0:T(8,128)(2,1)}, bf16[128,2048]{1,0:T(8,128)(2,1)S(1)}, u32[]{:S(2)}) copy-start(bf16[128,2048]{1,0:T(8,128)(2,1)S(1)} %multiply_convert_fusion) | copy-start | bytes 1572868
  148.3 25.3 %collective-permute-start.3 = (f32[512,1024]{1,0:T(8,128)S(1)}, f32[512,1024]{1,0:T(8,128)S(1)}, u32[]{:S(2)}, u32[]{:S(2)}) collective-permute-start(f32[512,1024]{1,0:T(8,128)S(1)} %fusion.15), channel_id=1, source_target_pairs={{0,28},{4,0},{8,4},{12,8},{16,12},{20,16},{24,20},{28,24},{1,29},{... | collective-permute-start | bytes 6291464 | tf_op jit(solution)/shard_map/ppermute | solution.py:14
  174.0 26.4 %collective-permute-start.4 = (f32[512,1024]{1,0:T(8,128)S(1)}, f32[512,1024]{1,0:T(8,128)S(1)}, u32[]{:S(2)}, u32[]{:S(2)}) collective-permute-start(f32[512,1024]{1,0:T(8,128)S(1)} %convolution_add_fusion), channel_id=1, source_target_pairs={{0,28},{4,0},{8,4},{12,8},{16,12},{20,16},{24,20},{28,24},{1,29},{... | collective-permute-start | bytes 6291464 | tf_op jit(solution)/shard_map/ppermute | solution.py:14
  200.9 26.4 %collective-permute-start.5 = (f32[512,1024]{1,0:T(8,128)S(1)}, f32[512,1024]{1,0:T(8,128)S(1)}, u32[]{:S(2)}, u32[]{:S(2)}) collective-permute-start(f32[512,1024]{1,0:T(8,128)S(1)} %add.62), channel_id=1, source_target_pairs={{0,28},{4,0},{8,4},{12,8},{16,12},{20,16},{24,20},{28,24},{1,29},{... | collective-permute-start | bytes 6291464 | tf_op jit(solution)/shard_map/ppermute | solution.py:14
  204.3 68.8 %copy-start.1 = (f32[128,1024]{1,0:T(8,128)S(1)}, f32[128,1024]{1,0:T(8,128)}, u32[]{:S(2)}) copy-start(f32[128,1024]{1,0:T(8,128)} %reduce-scatter.6.cloned.1.call-done) | copy-start | bytes 1572868
  204.3 72.1 %copy-start.3 = (f32[128,1024]{1,0:T(8,128)S(1)}, f32[128,1024]{1,0:T(8,128)}, u32[]{:S(2)}) copy-start(f32[128,1024]{1,0:T(8,128)} %reduce-scatter.4.cloned.1.call-done) | copy-start | bytes 1572868
  229.1 74.6 %all-gather.8.cloned.1.call-start = ((), (), s32[]{:S(2)}) async-start(), calls=%async_computation.8 | async-start | bytes 1310720 | tf_op jit(solution)/shard_map/all_gather | solution.py:120
  276.3 76.5 %all-gather.6.cloned.1.call-start = ((), (), s32[]{:S(2)}) async-start(), calls=%async_computation.6 | async-start | bytes 1310720 | tf_op jit(solution)/shard_map/all_gather | solution.py:112
  280.5 184.5 %all-reduce.2.cloned.1.call-start = ((), (), s32[]{:S(2)}) async-start(), calls=%async_computation.9 | async-start | bytes 16777216 | tf_op jit(solution)/shard_map/psum | solution.py:122
Sparse Core Ops, SparseCore 0:
  14.7 46.5 reduce-scatter.5
  64.5 27.2 all-gather.3
  94.8 43.3 reduce-scatter.3
  229.2 43.8 reduce-scatter.7
  276.4 27.2 all-gather.7
  305.8 27.8 all-gather.5
  338.1 126.7 all-reduce.1
where the time goes:
time: 483 us; the launch traced here: 482 us
  waiting for transfers between devices  353 us (73%)
  blocking collectives  41.4 us (9%)
  matrix products  33.5 us (7%)
  between operations  16.1 us (3%)
  local copies, waits for them, and re-layouts  16 us (3%)
  other arithmetic  14.5 us (3%)
  starting transfers between devices  7.89 us (2%)
    psum x1, waiting for transfers between devices, shards(): grad_teacher_weight = lax.psum(local_grad, 'blk')  105 us
    ppermute x6, waiting for transfers between devices, shifted(): lax.ppermute(x, axis, [(i, (i + by) % devices) for i in range(devices)])  100 us
    reduce_scatter x1, waiting for transfers between devices, shards(): lax.psum_scatter(jnp.dot(row_block, teacher_weight, preferred_element_typ...  46.7 us
    reduce_scatter x1, waiting for transfers between devices, shards(): lax.psum_scatter(carried, 'narrow', scatter_dimension=0, tiled=True)  44 us
    psum x1, blocking collectives, shards(): lax.psum(loss_part, ('blk', 'narrow')) / (span_block * lax.axis_size('blk'))  41.4 us
    all_gather x1, waiting for transfers between devices, shards(): lax.all_gather(teacher_grad, 'narrow', axis=0, tiled=True)  23 us
    all_gather x1, waiting for transfers between devices, shards(): teacher_block = lax.all_gather(teacher, 'narrow', axis=0, tiled=True)  17.9 us
    reduce_scatter x1, waiting for transfers between devices, shards(): lax.psum_scatter(jnp.dot(span_table, projected, preferred_element_type=jn...  15.8 us
  transfers between devices with their start and end apart: 13, of which 11 were waited for; matrix products, arithmetic and copies ran while one was open for 7% of the time, Pallas kernels for 0%

commit v1 on v0

v1 whole, which is shorter than its diff:
```python
import jax
import jax.numpy as jnp
from jax import lax
from jax.sharding import PartitionSpec as P

STOPS = 4
EPS = 1e-06
BF16 = jnp.bfloat16
F32 = jnp.float32


def normalize(values):
    inv_rms = lax.rsqrt(jnp.mean(values * values, axis=-1, keepdims=True) + EPS)
    return (values * inv_rms, inv_rms)


def norm_back(upstream, normed, inv_rms):
    inner_mean = jnp.mean(upstream * normed, axis=-1, keepdims=True)
    return inv_rms * (upstream - normed * inner_mean)


def contract_first(left, right):
    return lax.dot_general(left, right, (((0,), (0,)), ((), ())), preferred_element_type=F32)


def contract_last(left, right):
    return lax.dot_general(left, right, (((1,), (1,)), ((), ())), preferred_element_type=F32)


def permute_blk(x, target):
    count = lax.axis_size("blk")
    return lax.ppermute(x, "blk", [(i, target(i) % count) for i in range(count)])


def sibling(x):
    return permute_blk(x, lambda i: i ^ 1)


def gather_narrow(x):
    count = lax.axis_size("narrow")
    index = lax.axis_index("narrow")
    out = jnp.zeros((count,) + x.shape, x.dtype)
    out = lax.dynamic_update_index_in_dim(out, x, index, 0)
    for by in range(1, count):
        came = lax.ppermute(x, "narrow", [(i, (i + by) % count) for i in range(count)])
        out = lax.dynamic_update_index_in_dim(out, came, lax.rem(index + count - by, count), 0)
    return out


def shards(
    student_bytes, student_weight, teacher_rows, teacher_weight, span_lengths, span_scale, positives
):
    span_dev = span_scale.shape[0]
    embed_width = student_weight.shape[1]
    lanes = lax.axis_size("narrow")
    blocks = lax.axis_size("blk")
    chips = blocks // 2
    lane = lax.axis_index("narrow")
    block = lax.axis_index("blk")
    core = lax.rem(block, 2)
    chip = lax.div(block, 2)
    span_block = span_dev * lanes
    byte_dev = student_bytes.shape[0]
    feats = teacher_rows.shape[1]
    half = feats // 2

    own_half = lax.dynamic_slice_in_dim(teacher_rows, core * half, half, 1)
    sibling_half = sibling(lax.dynamic_slice_in_dim(teacher_rows, (1 - core) * half, half, 1))

    factor_own = span_scale / embed_width
    small = jnp.stack([factor_own, positives.astype(F32)])
    small = gather_narrow(small)
    factor = small[:, 0].reshape(span_block)
    positive = small[:, 1].reshape(span_block)

    byte_lengths = span_lengths[0]
    byte_ends = jnp.cumsum(byte_lengths)
    byte_starts = byte_ends - byte_lengths

    def owner_order(values):
        return values.reshape(span_dev, lanes).T.reshape(span_block)

    lengths = owner_order(byte_lengths)
    ends = owner_order(byte_ends)
    starts = owner_order(byte_starts)
    lengths_f = lengths.astype(F32)[:, None]
    first = lane * byte_dev
    last = first + byte_dev
    byte_pos = first + jnp.arange(byte_dev, dtype=jnp.int32)
    span_table = (
        (byte_pos[None, :] >= starts[:, None]) & (byte_pos[None, :] < ends[:, None])
    ).astype(BF16)
    cut_left = (starts < first) & (ends > first)
    cut_right = (starts < last) & (ends > last)
    left_end = jnp.sum(jnp.where(cut_left, ends, 0))
    right_start = jnp.sum(jnp.where(cut_right, starts - last, 0)) + last
    edge_table = jnp.stack([byte_pos < left_end, byte_pos >= right_start]).astype(BF16)
    projected = jnp.dot(student_bytes, student_weight, preferred_element_type=F32).astype(BF16)
    edges = jnp.dot(edge_table, projected, preferred_element_type=F32)
    from_right = lax.ppermute(edges[0:1], "narrow", [(i + 1, i) for i in range(lanes - 1)])
    from_left = lax.ppermute(edges[1:2], "narrow", [(i, i + 1) for i in range(lanes - 1)])
    partial = jnp.dot(span_table, projected, preferred_element_type=F32)
    pooled = (
        partial
        + jnp.where(cut_right[:, None], from_right, 0.0)
        + jnp.where(cut_left[:, None], from_left, 0.0)
    )
    student_full, student_rms = normalize(pooled / lengths_f)
    begins_here = (starts >= first) & (starts < last)
    student_sparse = jnp.where(begins_here[:, None], student_full, 0.0).astype(BF16)
    student_shard = lax.psum_scatter(student_sparse, "narrow", scatter_dimension=0, tiled=True)
    student = lax.all_gather(student_shard, "narrow", axis=0, tiled=True)

    teacher_rows_late, _ = lax.optimization_barrier((teacher_rows, projected))
    teacher_proj = lax.psum_scatter(
        jnp.dot(teacher_rows_late, teacher_weight, preferred_element_type=F32),
        "narrow",
        scatter_dimension=0,
        tiled=True,
    )
    teacher_full, teacher_rms = normalize(teacher_proj)
    teacher = teacher_full.astype(BF16)

    def following(x):
        ahead = permute_blk(x, lambda i: i - 2)
        mixed = permute_blk(x, lambda i: i - 1 if i % 2 else i - 3)
        return ahead, mixed

    ahead, mixed = following(student)
    other = sibling(ahead)
    student_window = [student, ahead, mixed, other]
    mixed_stop = jnp.where(core == 1, 3, 1)
    window_stops = [0, 2, mixed_stop, 4 - mixed_stop]

    def following_small(x):
        ahead, mixed = following(x)
        other = permute_blk(x, lambda i: i - 3 if i % 2 else i - 1)
        return [x, ahead, mixed, other]

    window_factor = following_small(factor)
    window_positive = following_small(positive)

    keys = [teacher] + [permute_blk(teacher, lambda i, k=k: i + k) for k in range(1, STOPS)]
    near = jnp.arange(span_dev, dtype=F32)[None, :] + (lane * span_dev).astype(F32)
    parts = []
    maxes = []
    for stop in range(STOPS):
        scores = contract_last(student, keys[stop]) * factor[:, None]
        hit = near + stop * span_block == positive[:, None]
        picked = jnp.sum(jnp.where(hit, scores, 0.0), axis=1)
        parts.append((scores, picked))
        maxes.append(jnp.max(scores, axis=1))
    row_max = maxes[0]
    for stop in range(1, STOPS):
        row_max = jnp.maximum(row_max, maxes[stop])
    row_sum = sum(jnp.sum(jnp.exp(s - row_max[:, None]), axis=1) for s, _ in parts)
    picked = sum(p for _, p in parts)
    stats = gather_narrow(jnp.stack([row_max, row_sum, picked]))
    top = jnp.max(stats[:, 0], axis=0)
    log_total = top + jnp.log(jnp.sum(stats[:, 1] * jnp.exp(stats[:, 0] - top), axis=0))
    loss = jnp.sum(log_total - jnp.sum(stats[:, 2], axis=0)).reshape(1)
    window_log_total = following_small(log_total)

    dteacher = jnp.zeros((span_dev, embed_width), F32)
    column = jnp.arange(span_dev, dtype=jnp.int32)[:, None] + lane * span_dev
    for at in range(4):
        scale = window_factor[at][None, :]
        scores = contract_last(teacher, student_window[at]) * scale
        column_here = (column + window_stops[at] * span_block).astype(F32)
        hit = (column_here == window_positive[at][None, :]).astype(F32)
        grads = ((jnp.exp(scores - window_log_total[at][None, :]) - hit) * scale).astype(BF16)
        dteacher = dteacher + jnp.dot(grads, student_window[at], preferred_element_type=F32)
    teacher_grad = norm_back(dteacher, teacher_full, teacher_rms).astype(BF16)
    teacher_grads = lax.all_gather(teacher_grad, "narrow", axis=0, tiled=True)
    sibling_grads = sibling(teacher_grads)

    weight_part = contract_first(own_half, teacher_grads) + contract_first(
        sibling_half, sibling_grads
    )
    slice_rows = half // chips
    narrowed = weight_part.astype(BF16)
    total = lax.dynamic_slice_in_dim(weight_part, chip * slice_rows, slice_rows, 0)
    came = []
    for by in range(1, chips):
        target = lax.rem(chip + by, chips)
        piece = lax.dynamic_slice_in_dim(narrowed, target * slice_rows, slice_rows, 0)
        came.append(permute_blk(piece, lambda i, by=by: i + 2 * by))
    for piece in came:
        total = total + piece.astype(F32)
    total = total.astype(BF16)
    grad_weight = jnp.zeros((feats, embed_width), F32)
    for by in range(chips):
        piece = total if by == 0 else permute_blk(total, lambda i, by=by: i + 2 * by)
        twin = sibling(piece)
        at = lax.rem(chip + chips - by, chips) * slice_rows
        grad_weight = lax.dynamic_update_slice_in_dim(
            grad_weight, piece.astype(F32), core * half + at, 0
        )
        grad_weight = lax.dynamic_update_slice_in_dim(
            grad_weight, twin.astype(F32), (1 - core) * half + at, 0
        )

    teacher_block = lax.all_gather(teacher, "narrow", axis=0, tiled=True)
    back = permute_blk(teacher_block, lambda i: i + 2)
    back_mixed = permute_blk(teacher_block, lambda i: i + 3 if i % 2 else i + 1)
    back_other = sibling(back)
    teacher_window = [teacher_block, back, back_mixed, back_other]
    back_stop = jnp.where(core == 1, 1, 3)
    back_stops = [0, 2, back_stop, 4 - back_stop]
    columns = jnp.arange(span_block, dtype=jnp.int32)[None, :]
    dstudent = jnp.zeros((span_block, embed_width), F32)
    for at in range(4):
        scores = contract_last(student, teacher_window[at]) * factor[:, None]
        column_here = (columns + back_stops[at] * span_block).astype(F32)
        hit = (column_here == positive[:, None]).astype(F32)
        grads = ((jnp.exp(scores - log_total[:, None]) - hit) * factor[:, None]).astype(BF16)
        dstudent = dstudent + jnp.dot(grads, teacher_window[at], preferred_element_type=F32)
    span_grad = (norm_back(dstudent, student_full, student_rms) / lengths_f).astype(BF16)
    byte_grad = contract_first(span_table, span_grad).astype(BF16)
    grad_bytes = contract_last(byte_grad, student_weight).astype(BF16)

    step = 1
    while step < blocks:
        loss = loss + permute_blk(loss, lambda i, step=step: i ^ step)
        step *= 2
    loss_mean = loss[0] / (span_block * blocks)
    return (loss_mean, grad_bytes, grad_weight)


def solution(mesh):
    return jax.shard_map(
        shards,
        mesh=mesh,
        in_specs=(
            P(("blk", "narrow"), None),
            P(),
            P("blk", "narrow"),
            P("narrow", None),
            P("blk", None),
            P(("blk", "narrow")),
            P(("blk", "narrow")),
        ),
        out_specs=(P(), P(("blk", "narrow"), None), P("narrow", None)),
        check_vma=False,
    )
```

time: 483 us -> 329 us (0.68)
  waiting for transfers between devices: 353 us -> 148 us
  starting transfers between devices: 7.89 us -> 64 us
  blocking collectives: 41.4 us -> 0 us
  matrix products: 33.5 us -> 62.9 us
  other arithmetic: 14.5 us -> 24.4 us
  local copies, waits for them, and re-layouts: 16 us -> 10.4 us
    psum x1 -> x0, waiting for transfers between devices: 105 us -> none  [shards(): grad_teacher_weight = lax.psum(local_grad, 'blk')]
    ppermute x6 -> x41, starting transfers between devices: 7.42 us -> 63.8 us  [the longest x33 48.8 us: permute_blk(): lax.ppermute(x, 'blk', [(i, target(i) % count) for i in range(count)])]
    psum x1 -> x0, blocking collectives: 41.4 us -> none  [shards(): lax.psum(loss_part, ('blk', 'narrow')) / (span_block * lax.axis_size('blk'))]
    ppermute x6 -> x41, waiting for transfers between devices: 100 us -> 60.3 us  [the longest x33 53.9 us: permute_blk(): lax.ppermute(x, 'blk', [(i, target(i) % count) for i in range(count)])]
    reduce_scatter x3 -> x2, waiting for transfers between devices: 106 us -> 71.4 us  [the longest x1 43.9 us: shards(): lax.psum_scatter(jnp.dot(teacher_rows_late, teacher_weight, preferred_ele...]
    dot_general x5 -> x17, matrix products: 24.6 us -> 55.6 us  [the longest x4 20.1 us: shards(): jnp.dot(grads, teacher_window[at], preferred_element_type=F32)]
    all_gather x1, waiting for transfers between devices: 17.9 us -> 0.02 us  [shards(): teacher_block = lax.all_gather(teacher, 'narrow', axis=0, tiled=True)]
    dynamic_update_slice x0 -> x9, other arithmetic: none -> 13.8 us  [the longest x4 8.35 us: shards(): lax.dynamic_update_slice_in_dim(grad_weight, piece.astype(F32), core * ha...]
  transfers between devices with their start and end apart: 13 -> 46, of which waited for: 11 -> 18; matrix products, arithmetic and copies ran while one was open for 7% -> 23% of each run, Pallas kernels for 0% -> 0%
where the time goes in v1:
time: 329 us; the launch traced here: 328 us
  waiting for transfers between devices  148 us (45%)
  starting transfers between devices  64 us (19%)
  matrix products  62.9 us (19%)
  other arithmetic  24.4 us (7%)
  between operations  18.6 us (6%)
  local copies, waits for them, and re-layouts  10.4 us (3%)
    ppermute x33, waiting for transfers between devices, permute_blk(): lax.ppermute(x, 'blk', [(i, target(i) % count) for i in range(count)])  53.9 us
    ppermute x33, starting transfers between devices, permute_blk(): lax.ppermute(x, 'blk', [(i, target(i) % count) for i in range(count)])  48.8 us
    reduce_scatter x1, waiting for transfers between devices, shards(): lax.psum_scatter(jnp.dot(teacher_rows_late, teacher_weight, preferred_ele...  43.9 us
    reduce_scatter x1, waiting for transfers between devices, shards(): lax.psum_scatter(student_sparse, 'narrow', scatter_dimension=0, tiled=True)  27.5 us
    dot_general x4, matrix products, shards(): jnp.dot(grads, teacher_window[at], preferred_element_type=F32)  20.1 us
    all_gather x1, waiting for transfers between devices, shards(): student = lax.all_gather(student_shard, 'narrow', axis=0, tiled=True)  15.7 us
    dot_general x4, matrix products, shards(): jnp.dot(grads, student_window[at], preferred_element_type=F32)  11.7 us
    dot_general x5, matrix products, contract_last(): lax.dot_general(left, right, (((1,), (1,)), ((), ())), preferred_element_...  11.4 us
  transfers between devices with their start and end apart: 46, of which 18 were waited for; matrix products, arithmetic and copies ran while one was open for 23% of the time, Pallas kernels for 0%

profile of v1, /device:TPU:0, one launch (start us, length us, event | category | flops | bytes accessed | tf_op | source)
XLA Modules:
  0.0 327.8 jit_solution(13361637550574449503)
XLA Ops:
  12.2 5.2 %convolution_convert_fusion.2 = bf16[512,1024]{1,0:T(8,128)(2,1)S(1)} fusion(bf16[512,2048]{1,0:T(8,128)(2,1)} %param.7, bf16[2048,1024]{1,0:T(8,128)(2,1)} %param.8), kind=kOutput, calls=%fused_computation.9 | convolution fusion | flops 2148007936 | bytes 7340032 | tf_op jit(solution)/shard_map/dot_general | solution.py:98
  18.3 4.9 %collective-permute-start.1 = (f32[1,1024]{1,0:T(1,128)S(1)}, f32[1,1024]{1,0:T(1,128)S(1)}, u32[]{:S(2)}, u32[]{:S(2)}) collective-permute-start(f32[1,1024]{1,0:T(1,128)S(1)} %get-tuple-element.33), channel_id=1, source_target_pairs={{0,1},{1,2},{2,3},{4,5},{5,6},{6,7},{8,9},{9,10},{10,11},{12,13},{... | collective-permute-start | bytes 12296 | tf_op jit(solution)/shard_map/ppermute | solution.py:101
  24.8 3.9 %collective-permute-done = f32[1,1024]{1,0:T(1,128)S(1)} collective-permute-done((f32[1,1024]{1,0:T(1,128)S(1)}, f32[1,1024]{1,0:T(1,128)S(1)}, u32[]{:S(2)}, u32[]{:S(2)}) %collective-permute-start) | collective-permute-done | bytes 4128 | tf_op jit(solution)/shard_map/ppermute | solution.py:100
  32.5 27.5 %reduce-scatter.3.cloned.1.call-done = bf16[128,1024]{1,0:T(8,128)(2,1)} async-done(((bf16[512,1024]{1,0:T(8,128)(2,1)}), bf16[128,1024]{1,0:T(8,128)(2,1)}) %reduce-scatter.3.cloned.1.call-update) | async-done | bytes 262160 | tf_op jit(solution)/shard_map/reduce_scatter | solution.py:111
  60.1 5.8 %fusion.122 = f32[512,1024]{1,0:T(8,128)} fusion(bf16[512,2048]{1,0:T(8,128)(2,1)S(1)} %copy-done, bf16[2048,1024]{1,0:T(8,128)(2,1)} %param.10), kind=kOutput, calls=%fused_computation.215 | convolution fusion | flops 2147483648 | bytes 8388608 | tf_op jit(solution)/shard_map/dot_general | solution.py:116
  72.6 15.7 %all-gather.4.cloned.1.call-done = bf16[512,1024]{1,0:T(8,128)(2,1)} async-done(((bf16[128,1024]{1,0:T(8,128)(2,1)}), bf16[512,1024]{1,0:T(8,128)(2,1)}) %all-gather.4.cloned.1.call-update) | async-done | bytes 1048592 | tf_op jit(solution)/shard_map/all_gather | solution.py:112
  90.7 43.9 %reduce-scatter.5.cloned.1.call-done = f32[128,1024]{1,0:T(8,128)} async-done(((f32[512,1024]{1,0:T(8,128)}), f32[128,1024]{1,0:T(8,128)}) %reduce-scatter.5.cloned.1.call-update) | async-done | bytes 524304 | tf_op jit(solution)/shard_map/reduce_scatter | solution.py:115
  141.6 12.5 %collective-permute-done.7 = bf16[128,1024]{1,0:T(8,128)(2,1)S(1)} collective-permute-done((bf16[128,1024]{1,0:T(8,128)(2,1)S(1)}, bf16[128,1024]{1,0:T(8,128)(2,1)S(1)}, u32[]{:S(2)}, u32[]{:S(2)}) %collective-permute-start.7) | collective-permute-done | bytes 262176 | tf_op jit(solution)/shard_map/ppermute | solution.py:32
  169.2 3.3 %convolution_add_fusion.3 = f32[128,1024]{1,0:T(8,128)} fusion(f32[128,1024]{1,0:T(8,128)} %fusion.40, bf16[512,1024]{1,0:T(8,128)(2,1)} %collective-permute-done.17, bf16[128,1024]{1,0:T(8,128)(2,1)S(1)} %copy-done.3, f32[512]{0:T(512)S(1)} %collective-permute-done.20, f32[512]{0:T(512)S(1)} %collective-permute-done.19, ...), kind=kOutput, calls=%fused_computation.36 | convolution fusion | flops 269025280 | bytes 2365952 | tf_op jit(solution)/shard_map/dot_general | solution.py:172
  172.5 3.9 %collective-permute-done.24 = f32[512]{0:T(512)S(1)} collective-permute-done((f32[512]{0:T(512)S(1)}, f32[512]{0:T(512)S(1)}, u32[]{:S(2)}, u32[]{:S(2)}) %collective-permute-start.24) | collective-permute-done | bytes 2080 | tf_op jit(solution)/shard_map/ppermute | solution.py:32
  183.7 3.6 %multiply_reduce_fusion.2 = (f32[128]{0:T(128)S(1)}, f32[128,1024]{1,0:T(8,128)}) fusion(f32[128,1024]{1,0:T(8,128)} %reduce-scatter.5.cloned.1.call-done, f32[128]{0:T(128)S(1)} %add_rsqrt_fusion.1, f32[128,1024]{1,0:T(8,128)} %convolution_add_fusion.2, bf16[512,1024]{1,0:T(8,128)(2,1)} %collective-permute-done.25, bf16[128,1024]{1,0:T(8,128)(2,1)S(1)} %copy-done.3, ...), kind=kOutput, calls=%fused_computation.89 | convolution fusion | flops 269418368 | bytes 2891264 | tf_op jit(solution)/shard_map/dot_general | solution.py:172
  192.8 3.4 %collective-permute-done.11 = f32[1]{0:T(128)} collective-permute-done((f32[1]{0:T(128)}, f32[1]{0:T(128)}, u32[]{:S(2)}, u32[]{:S(2)}) %collective-permute-start.11) | collective-permute-done | bytes 36 | tf_op jit(solution)/shard_map/ppermute | solution.py:32
  197.5 15.5 %collective-permute-start.12 = (f32[1]{0:T(128)}, f32[1]{0:T(128)}, u32[]{:S(2)}, u32[]{:S(2)}) collective-permute-start(f32[1]{0:T(128)} %add.471), channel_id=1, source_target_pairs={{0,8},{4,12},{8,0},{12,4},{16,24},{20,28},{24,16},{28,20},{1,9},{5... | collective-permute-start | bytes 20 | tf_op jit(solution)/shard_map/ppermute | solution.py:32
  220.0 4.3 %fusion.41 = f32[512,1024]{1,0:T(8,128)} fusion(bf16[512,1024]{1,0:T(8,128)(2,1)} %all-gather.6.cloned.1.call-done, bf16[512,1024]{1,0:T(8,128)(2,1)S(1)} %copy-done.1, f32[512]{0:T(512)S(1)} %iota_convert_fusion, f32[512]{0:T(512)S(1)} %get-tuple-element.26, f32[512]{0:T(512)S(1)} %bitcast.104, f32[512]{0:T(512)S(1)} %bitcast.113), kind=kOutput, calls=%fused_computation.66 | convolution fusion | flops 1075576832 | bytes 4202496 | tf_op jit(solution)/shard_map/dot_general | solution.py:217
  224.3 7.8 %collective-permute-start.16 = (bf16[512,1024]{1,0:T(8,128)(2,1)}, bf16[512,1024]{1,0:T(8,128)(2,1)}, u32[]{:S(2)}, u32[]{:S(2)}) collective-permute-start(bf16[512,1024]{1,0:T(8,128)(2,1)} %collective-permute-done.14), channel_id=1, source_target_pairs={{0,4},{4,0},{8,12},{12,8},{16,20},{20,16},{24,28},{28,24},{1,5},{5... | collective-permute-start | bytes 3145736 | tf_op jit(solution)/shard_map/ppermute | solution.py:32
  232.2 4.5 %fusion.42 = f32[512,1024]{1,0:T(8,128)} fusion(bf16[512,1024]{1,0:T(8,128)(2,1)} %collective-permute-done.14, bf16[512,1024]{1,0:T(8,128)(2,1)S(1)} %copy-done.1, f32[512]{0:T(512)S(1)} %add_convert_fusion.3, f32[512]{0:T(512)S(1)} %get-tuple-element.26, f32[512]{0:T(512)S(1)} %bitcast.105, f32[512]{0:T(512)S(1)} %bitcast.114), kind=kOutput, calls=%fused_computation.67 | convolution fusion | flops 1075576832 | bytes 4202496 | tf_op jit(solution)/shard_map/dot_general | solution.py:217
  236.7 4.3 %fusion.43 = f32[512,1024]{1,0:T(8,128)} fusion(bf16[512,1024]{1,0:T(8,128)(2,1)} %collective-permute-done.15, bf16[512,1024]{1,0:T(8,128)(2,1)S(1)} %copy-done.1, f32[512]{0:T(512)S(1)} %add_convert_fusion.2, f32[512]{0:T(512)S(1)} %get-tuple-element.26, f32[512]{0:T(512)S(1)} %bitcast.106, f32[512]{0:T(512)S(1)} %bitcast.115), kind=kOutput, calls=%fused_computation.68 | convolution fusion | flops 1075576832 | bytes 4202496 | tf_op jit(solution)/shard_map/dot_general | solution.py:217
  243.5 4.8 %fusion.121 = (bf16[1024,1024]{1,0:T(8,128)(2,1)S(1)}, f32[1024,1024]{1,0:T(8,128)}) fusion(f32[1024,1024]{1,0:T(8,128)S(1)} %fusion.44, bf16[512,1024]{1,0:T(8,128)(2,1)} %collective-permute-done.29, bf16[512,1024]{1,0:T(8,128)(2,1)} %collective-permute-done.30), kind=kOutput, calls=%fused_computation.214 | convolution fusion | flops 1075838976 | bytes 12582912 | tf_op jit(solution)/shard_map/dot_general | solution.py:23
  252.1 7.0 %multiply_reduce_fusion = (f32[512]{0:T(512)S(1)}, f32[512,1024]{1,0:T(8,128)}) fusion(f32[512,1024]{1,0:T(8,128)} %copy-done.4, f32[512]{0:T(512)S(1)} %add_rsqrt_fusion, bf16[512,1024]{1,0:T(8,128)(2,1)} %collective-permute-done.16, bf16[512,1024]{1,0:T(8,128)(2,1)S(1)} %copy-done.1, f32[512]{0:T(512)S(1)} %add_convert_fusion.1, ...), kind=kOutput, calls=%fused_computation.3 | convolution fusion | flops 1078722048 | bytes 12595200 | tf_op jit(solution)/shard_map/dot_general | solution.py:217
  259.2 5.4 %collective-permute-done.33 = bf16[256,1024]{1,0:T(8,128)(2,1)} collective-permute-done((bf16[256,1024]{1,0:T(8,128)(2,1)}, bf16[256,1024]{1,0:T(8,128)(2,1)}, u32[]{:S(2)}, u32[]{:S(2)}) %collective-permute-start.33) | collective-permute-done | bytes 524320 | tf_op jit(solution)/shard_map/ppermute | solution.py:32
  264.6 10.8 %collective-permute-done.31 = bf16[256,1024]{1,0:T(8,128)(2,1)} collective-permute-done((bf16[256,1024]{1,0:T(8,128)(2,1)}, bf16[256,1024]{1,0:T(8,128)(2,1)}, u32[]{:S(2)}, u32[]{:S(2)}) %collective-permute-start.31) | collective-permute-done | bytes 524320 | tf_op jit(solution)/shard_map/ppermute | solution.py:32
  275.4 4.5 %broadcast_in_dim.144 = f32[2048,1024]{1,0:T(8,128)} broadcast(f32[]{:T(128)} %constant.98.clone.1), dimensions={} | broadcast | bytes 8388612 | tf_op jit(solution)/shard_map/broadcast_in_dim | solution.py:191
  287.2 8.1 %convolution_convert_fusion = bf16[512,2048]{1,0:T(8,128)(2,1)} fusion(bf16[2048,1024]{1,0:T(8,128)(2,1)} %param.8, f32[512,1024]{1,0:T(8,128)} %get-tuple-element.52, f32[512,1024]{1,0:T(8,128)} %copy-done.4, f32[512]{0:T(512)S(1)} %broadcast_multiply_fusion, f32[512]{0:T(512)S(1)} %add_rsqrt_fusion, f32[512]{0:T(512)S(1)} %bitcast.128, ...), kind=kOutput, calls=%fused_computation | convolution fusion | flops 2689859584 | bytes 10498048 | tf_op jit(solution)/shard_map/dot_general | solution.py:27
  298.6 9.9 %collective-permute-done.37 = bf16[256,1024]{1,0:T(8,128)(2,1)} collective-permute-done((bf16[256,1024]{1,0:T(8,128)(2,1)S(1)}, bf16[256,1024]{1,0:T(8,128)(2,1)}, u32[]{:S(2)}, u32[]{:S(2)}) %collective-permute-start.37) | collective-permute-done | bytes 524320 | tf_op jit(solution)/shard_map/ppermute | solution.py:32
  (180 shorter events, 88.6 us)
Async XLA Ops:
  7.2 52.9 %reduce-scatter.3.cloned.1.call-start = ((), (), s32[]{:S(2)}) async-start(), calls=%async_computation.2 | async-start | bytes 1310720 | tf_op jit(solution)/shard_map/reduce_scatter | solution.py:111
  32.5 55.9 %all-gather.4.cloned.1.call-start = ((), (), s32[]{:S(2)}) async-start(), calls=%async_computation.3 | async-start | bytes 1310720 | tf_op jit(solution)/shard_map/all_gather | solution.py:112
  60.1 74.6 %reduce-scatter.5.cloned.1.call-start = ((), (), s32[]{:S(2)}) async-start(), calls=%async_computation.4 | async-start | bytes 2621440 | tf_op jit(solution)/shard_map/reduce_scatter | solution.py:115
  66.0 123.5 %all-gather.6.cloned.1.call-start = ((), (), s32[]{:S(2)}) async-start(), calls=%async_computation.5 | async-start | bytes 1310720 | tf_op jit(solution)/shard_map/all_gather | solution.py:203
  88.4 76.0 %collective-permute-start.17 = (bf16[512,1024]{1,0:T(8,128)(2,1)}, bf16[512,1024]{1,0:T(8,128)(2,1)}, u32[]{:S(2)}, u32[]{:S(2)}) collective-permute-start(bf16[512,1024]{1,0:T(8,128)(2,1)} %all-gather.4.cloned.1.call-done), channel_id=1, source_target_pairs={{0,24},{4,28},{8,0},{12,4},{16,8},{20,12},{24,16},{28,20},{1,25},{... | collective-permute-start | bytes 3145736 | tf_op jit(solution)/shard_map/ppermute | solution.py:32
  137.0 17.1 %collective-permute-start.7 = (bf16[128,1024]{1,0:T(8,128)(2,1)S(1)}, bf16[128,1024]{1,0:T(8,128)(2,1)S(1)}, u32[]{:S(2)}, u32[]{:S(2)}) collective-permute-start(bf16[128,1024]{1,0:T(8,128)(2,1)S(1)} %multiply_convert_fusion.1), channel_id=1, source_target_pairs={{0,12},{4,16},{8,20},{12,24},{16,28},{20,0},{24,4},{28,8},{1,13},{... | collective-permute-start | bytes 786440 | tf_op jit(solution)/shard_map/ppermute | solution.py:32
  137.8 16.8 %collective-permute-start.6 = (bf16[128,1024]{1,0:T(8,128)(2,1)S(1)}, bf16[128,1024]{1,0:T(8,128)(2,1)S(1)}, u32[]{:S(2)}, u32[]{:S(2)}) collective-permute-start(bf16[128,1024]{1,0:T(8,128)(2,1)S(1)} %multiply_convert_fusion.1), channel_id=1, source_target_pairs={{0,8},{4,12},{8,16},{12,20},{16,24},{20,28},{24,0},{28,4},{1,9},{5... | collective-permute-start | bytes 786440 | tf_op jit(solution)/shard_map/ppermute | solution.py:32
  139.3 15.9 %collective-permute-start.5 = (bf16[128,1024]{1,0:T(8,128)(2,1)S(1)}, bf16[128,1024]{1,0:T(8,128)(2,1)S(1)}, u32[]{:S(2)}, u32[]{:S(2)}) collective-permute-start(bf16[128,1024]{1,0:T(8,128)(2,1)S(1)} %multiply_convert_fusion.1), channel_id=1, source_target_pairs={{0,4},{4,8},{8,12},{12,16},{16,20},{20,24},{24,28},{28,0},{1,5},{5... | collective-permute-start | bytes 786440 | tf_op jit(solution)/shard_map/ppermute | solution.py:32
  160.8 71.3 %all-gather.8.cloned.1.call-start = ((), (), s32[]{:S(2)}) async-start(), calls=%async_computation.6 | async-start | bytes 1310720 | tf_op jit(solution)/shard_map/all_gather | solution.py:174
  164.0 16.5 %collective-permute-start.21 = (bf16[512,1024]{1,0:T(8,128)(2,1)S(1)}, bf16[512,1024]{1,0:T(8,128)(2,1)}, u32[]{:S(2)}, u32[]{:S(2)}) collective-permute-start(bf16[512,1024]{1,0:T(8,128)(2,1)S(1)} %copy-done.1), channel_id=1, source_target_pairs={{0,20},{4,0},{8,28},{12,8},{16,4},{20,16},{24,12},{28,24},{1,21},{... | collective-permute-start | bytes 3145736 | tf_op jit(solution)/shard_map/ppermute | solution.py:32
  164.4 19.3 %collective-permute-start.25 = (bf16[512,1024]{1,0:T(8,128)(2,1)}, bf16[512,1024]{1,0:T(8,128)(2,1)}, u32[]{:S(2)}, u32[]{:S(2)}) collective-permute-start(bf16[512,1024]{1,0:T(8,128)(2,1)} %collective-permute-done.17), channel_id=1, source_target_pairs={{0,4},{4,0},{8,12},{12,8},{16,20},{20,16},{24,28},{28,24},{1,5},{5... | collective-permute-start | bytes 3145736 | tf_op jit(solution)/shard_map/ppermute | solution.py:32
  189.5 34.8 %collective-permute-start.14 = (bf16[512,1024]{1,0:T(8,128)(2,1)}, bf16[512,1024]{1,0:T(8,128)(2,1)}, u32[]{:S(2)}, u32[]{:S(2)}) collective-permute-start(bf16[512,1024]{1,0:T(8,128)(2,1)} %all-gather.6.cloned.1.call-done), channel_id=1, source_target_pairs={{0,8},{4,12},{8,16},{12,20},{16,24},{20,28},{24,0},{28,4},{1,9},{5... | collective-permute-start | bytes 3145736 | tf_op jit(solution)/shard_map/ppermute | solution.py:32
  192.0 51.4 %collective-permute-start.29 = (bf16[512,1024]{1,0:T(8,128)(2,1)}, bf16[512,1024]{1,0:T(8,128)(2,1)}, u32[]{:S(2)}, u32[]{:S(2)}) collective-permute-start(bf16[512,1024]{1,0:T(8,128)(2,1)} %constant_dynamic-slice_fusion.3), channel_id=1, source_target_pairs={{0,4},{4,0},{8,12},{12,8},{16,20},{20,16},{24,28},{28,24},{1,5},{5... | collective-permute-start | bytes 3145736 | tf_op jit(solution)/shard_map/ppermute | solution.py:32
  192.0 44.6 %collective-permute-start.15 = (bf16[512,1024]{1,0:T(8,128)(2,1)}, bf16[512,1024]{1,0:T(8,128)(2,1)}, u32[]{:S(2)}, u32[]{:S(2)}) collective-permute-start(bf16[512,1024]{1,0:T(8,128)(2,1)} %all-gather.6.cloned.1.call-done), channel_id=1, source_target_pairs={{0,4},{4,16},{8,12},{12,24},{16,20},{20,0},{24,28},{28,8},{1,5},{5... | collective-permute-start | bytes 3145736 | tf_op jit(solution)/shard_map/ppermute | solution.py:32
  197.5 17.5 %collective-permute-start.12 = (f32[1]{0:T(128)}, f32[1]{0:T(128)}, u32[]{:S(2)}, u32[]{:S(2)}) collective-permute-start(f32[1]{0:T(128)} %add.471), channel_id=1, source_target_pairs={{0,8},{4,12},{8,0},{12,4},{16,24},{20,28},{24,16},{28,20},{1,9},{5... | collective-permute-start | bytes 20 | tf_op jit(solution)/shard_map/ppermute | solution.py:32
  224.3 27.9 %collective-permute-start.16 = (bf16[512,1024]{1,0:T(8,128)(2,1)}, bf16[512,1024]{1,0:T(8,128)(2,1)}, u32[]{:S(2)}, u32[]{:S(2)}) collective-permute-start(bf16[512,1024]{1,0:T(8,128)(2,1)} %collective-permute-done.14), channel_id=1, source_target_pairs={{0,4},{4,0},{8,12},{12,8},{16,20},{20,16},{24,28},{28,24},{1,5},{5... | collective-permute-start | bytes 3145736 | tf_op jit(solution)/shard_map/ppermute | solution.py:32
  249.6 15.0 %collective-permute-start.33 = (bf16[256,1024]{1,0:T(8,128)(2,1)}, bf16[256,1024]{1,0:T(8,128)(2,1)}, u32[]{:S(2)}, u32[]{:S(2)}) collective-permute-start(bf16[256,1024]{1,0:T(8,128)(2,1)} %get-tuple-element.30), channel_id=1, source_target_pairs={{0,24},{4,28},{8,0},{12,4},{16,8},{20,12},{24,16},{28,20},{1,25},{... | collective-permute-start | bytes 1572872 | tf_op jit(solution)/shard_map/ppermute | solution.py:32
  249.6 15.1 %collective-permute-start.32 = (bf16[256,1024]{1,0:T(8,128)(2,1)}, bf16[256,1024]{1,0:T(8,128)(2,1)}, u32[]{:S(2)}, u32[]{:S(2)}) collective-permute-start(bf16[256,1024]{1,0:T(8,128)(2,1)} %get-tuple-element.31), channel_id=1, source_target_pairs={{0,16},{4,20},{8,24},{12,28},{16,0},{20,4},{24,8},{28,12},{1,17},{... | collective-permute-start | bytes 1572872 | tf_op jit(solution)/shard_map/ppermute | solution.py:32
  250.1 25.3 %collective-permute-start.31 = (bf16[256,1024]{1,0:T(8,128)(2,1)}, bf16[256,1024]{1,0:T(8,128)(2,1)}, u32[]{:S(2)}, u32[]{:S(2)}) collective-permute-start(bf16[256,1024]{1,0:T(8,128)(2,1)} %get-tuple-element.29), channel_id=1, source_target_pairs={{0,8},{4,12},{8,16},{12,20},{16,24},{20,28},{24,0},{28,4},{1,9},{5... | collective-permute-start | bytes 1572872 | tf_op jit(solution)/shard_map/ppermute | solution.py:32
  282.9 26.5 %collective-permute-start.34 = (bf16[256,1024]{1,0:T(8,128)(2,1)S(1)}, bf16[256,1024]{1,0:T(8,128)(2,1)}, u32[]{:S(2)}, u32[]{:S(2)}) collective-permute-start(bf16[256,1024]{1,0:T(8,128)(2,1)S(1)} %get-tuple-element.24), channel_id=1, source_target_pairs={{0,4},{4,0},{8,12},{12,8},{16,20},{20,16},{24,28},{28,24},{1,5},{5... | collective-permute-start | bytes 1572872 | tf_op jit(solution)/shard_map/ppermute | solution.py:32
  282.9 15.8 %collective-permute-start.35 = (bf16[256,1024]{1,0:T(8,128)(2,1)S(1)}, bf16[256,1024]{1,0:T(8,128)(2,1)}, u32[]{:S(2)}, u32[]{:S(2)}) collective-permute-start(bf16[256,1024]{1,0:T(8,128)(2,1)S(1)} %get-tuple-element.24), channel_id=1, source_target_pairs={{0,8},{4,12},{8,16},{12,20},{16,24},{20,28},{24,0},{28,4},{1,9},{5... | collective-permute-start | bytes 1572872 | tf_op jit(solution)/shard_map/ppermute | solution.py:32
  283.2 25.4 %collective-permute-start.37 = (bf16[256,1024]{1,0:T(8,128)(2,1)S(1)}, bf16[256,1024]{1,0:T(8,128)(2,1)}, u32[]{:S(2)}, u32[]{:S(2)}) collective-permute-start(bf16[256,1024]{1,0:T(8,128)(2,1)S(1)} %get-tuple-element.24), channel_id=1, source_target_pairs={{0,16},{4,20},{8,24},{12,28},{16,0},{20,4},{24,8},{28,12},{1,17},{... | collective-permute-start | bytes 1572872 | tf_op jit(solution)/shard_map/ppermute | solution.py:32
  284.6 24.7 %collective-permute-start.39 = (bf16[256,1024]{1,0:T(8,128)(2,1)S(1)}, bf16[256,1024]{1,0:T(8,128)(2,1)S(1)}, u32[]{:S(2)}, u32[]{:S(2)}) collective-permute-start(bf16[256,1024]{1,0:T(8,128)(2,1)S(1)} %get-tuple-element.24), channel_id=1, source_target_pairs={{0,24},{4,28},{8,0},{12,4},{16,8},{20,12},{24,16},{28,20},{1,25},{... | collective-permute-start | bytes 1572872 | tf_op jit(solution)/shard_map/ppermute | solution.py:32
  298.6 15.0 %collective-permute-start.36 = (bf16[256,1024]{1,0:T(8,128)(2,1)}, bf16[256,1024]{1,0:T(8,128)(2,1)S(1)}, u32[]{:S(2)}, u32[]{:S(2)}) collective-permute-start(bf16[256,1024]{1,0:T(8,128)(2,1)} %collective-permute-done.35), channel_id=1, source_target_pairs={{0,4},{4,0},{8,12},{12,8},{16,20},{20,16},{24,28},{28,24},{1,5},{5... | collective-permute-start | bytes 1572872 | tf_op jit(solution)/shard_map/ppermute | solution.py:32
  (29 other events, 297.1 us)
Sparse Core Ops, SparseCore 0:
  32.6 27.3 reduce-scatter.2
  61.7 26.6 all-gather.3
  91.3 43.3 reduce-scatter.4
  160.9 27.2 all-gather.5
  189.6 27.4 all-gather.7

commit v2 on v1

v2 whole, which is shorter than its diff:
```python
import functools

import jax
import jax.numpy as jnp
from jax import lax
from jax.experimental import pallas as pl
from jax.experimental.pallas import tpu as pltpu
from jax.sharding import PartitionSpec as P

STOPS = 4
EPS = 1e-06
BF16 = jnp.bfloat16
F32 = jnp.float32


def normalize(values):
    inv_rms = lax.rsqrt(jnp.mean(values * values, axis=-1, keepdims=True) + EPS)
    return (values * inv_rms, inv_rms)


def norm_back(upstream, normed, inv_rms):
    inner_mean = jnp.mean(upstream * normed, axis=-1, keepdims=True)
    return inv_rms * (upstream - normed * inner_mean)


def contract_first(left, right):
    return lax.dot_general(left, right, (((0,), (0,)), ((), ())), preferred_element_type=F32)


def contract_last(left, right):
    return lax.dot_general(left, right, (((1,), (1,)), ((), ())), preferred_element_type=F32)


def permute_blk(x, target):
    count = lax.axis_size("blk")
    return lax.ppermute(x, "blk", [(i, target(i) % count) for i in range(count)])


def sibling(x):
    return permute_blk(x, lambda i: i ^ 1)


def gather_narrow(x):
    count = lax.axis_size("narrow")
    index = lax.axis_index("narrow")
    out = jnp.zeros((count,) + x.shape, x.dtype)
    out = lax.dynamic_update_index_in_dim(out, x, index, 0)
    for by in range(1, count):
        came = lax.ppermute(x, "narrow", [(i, (i + by) % count) for i in range(count)])
        out = lax.dynamic_update_index_in_dim(out, came, lax.rem(index + count - by, count), 0)
    return out


def following(x):
    ahead = permute_blk(x, lambda i: i - 2)
    mixed = permute_blk(x, lambda i: i - 1 if i % 2 else i - 3)
    return ahead, mixed


def following_other(x):
    return permute_blk(x, lambda i: i - 3 if i % 2 else i - 1)


def scatter_narrow(x, rows):
    count = lax.axis_size("narrow")
    index = lax.axis_index("narrow")
    total = lax.dynamic_slice_in_dim(x, index * rows, rows, 0)
    for by in range(1, count):
        target = lax.rem(index + by, count)
        piece = lax.dynamic_slice_in_dim(x, target * rows, rows, 0)
        total += lax.ppermute(piece, "narrow", [(i, (i + by) % count) for i in range(count)])
    return total


def teacher_side(rows, teacher_ref, rms_ref, s0_ref, s1_ref, s2_ref, s3_ref, small_ref, out_ref):
    teacher = teacher_ref[...]
    dteacher = None
    for at, ref in enumerate((s0_ref, s1_ref, s2_ref, s3_ref)):
        scale = small_ref[at : at + 1, :]
        log_total = small_ref[4 + at : 5 + at, :]
        column = small_ref[8 + at : 9 + at, :].astype(jnp.int32)
        scores = contract_last(teacher, ref[...]) * scale
        here = lax.broadcasted_iota(jnp.int32, scores.shape, 0) + pl.program_id(0) * rows
        hit = jnp.where(here == column, 1.0, 0.0)
        grads = ((jnp.exp(scores - log_total) - hit) * scale).astype(BF16)
        term = jnp.dot(grads, ref[...], preferred_element_type=F32)
        dteacher = term if dteacher is None else dteacher + term
    full = teacher.astype(F32)
    inner_mean = jnp.mean(dteacher * full, axis=-1, keepdims=True)
    out_ref[...] = (rms_ref[...] * (dteacher - full * inner_mean)).astype(BF16)


def teacher_grads_of(teacher, rms, window, small):
    span_block, width = teacher.shape
    rows = 256
    whole = pl.BlockSpec((span_block, width), lambda i: (0, 0))
    part = pl.BlockSpec((rows, width), lambda i: (i, 0))
    return pl.pallas_call(
        functools.partial(teacher_side, rows),
        grid=(span_block // rows,),
        in_specs=[part, pl.BlockSpec((rows, 1), lambda i: (i, 0))] + [whole] * 4 + [pl.BlockSpec(small.shape, lambda i: (0, 0))],
        out_specs=part,
        out_shape=jax.ShapeDtypeStruct((span_block, width), BF16),
        compiler_params=pltpu.CompilerParams(vmem_limit_bytes=48 * 1024 * 1024),
        cost_estimate=pl.CostEstimate(
            flops=16 * span_block * span_block * width,
            bytes_accessed=14 * span_block * width,
            transcendentals=4 * span_block * span_block,
        ),
        name="teacher_side",
    )(teacher, rms, *window, small)


def student_side(student_ref, full_ref, scalar_ref, own_ref, others_ref, out_ref):
    student = student_ref[...]
    scale = scalar_ref[:, 0:1]
    log_total = scalar_ref[:, 1:2]

    def term(keys, at):
        column = scalar_ref[:, 4 + at : 5 + at].astype(jnp.int32)
        scores = contract_last(student, keys) * scale
        here = lax.broadcasted_iota(jnp.int32, scores.shape, 1)
        hit = jnp.where(here == column, 1.0, 0.0)
        grads = ((jnp.exp(scores - log_total) - hit) * scale).astype(BF16)
        return jnp.dot(grads, keys, preferred_element_type=F32)

    dstudent = term(own_ref[...], 0)
    for at in range(others_ref.shape[0]):
        dstudent = dstudent + term(others_ref[at], 1 + at)
    full = full_ref[...]
    inner_mean = jnp.mean(dstudent * full, axis=-1, keepdims=True)
    grad = scalar_ref[:, 2:3] * (dstudent - full * inner_mean) / scalar_ref[:, 3:4]
    out_ref[...] = grad.astype(BF16)


def span_grads_of(student, full, scalars, own, others):
    span_block, width = student.shape
    rows = 256
    part = pl.BlockSpec((rows, width), lambda i: (i, 0))
    return pl.pallas_call(
        student_side,
        grid=(span_block // rows,),
        in_specs=[
            part,
            part,
            pl.BlockSpec((rows, scalars.shape[1]), lambda i: (i, 0)),
            pl.BlockSpec(own.shape, lambda i: (0, 0)),
            pl.BlockSpec(others.shape, lambda i: (0, 0, 0)),
        ],
        out_specs=part,
        out_shape=jax.ShapeDtypeStruct((span_block, width), BF16),
        compiler_params=pltpu.CompilerParams(vmem_limit_bytes=48 * 1024 * 1024),
        cost_estimate=pl.CostEstimate(
            flops=16 * span_block * span_block * width,
            bytes_accessed=16 * span_block * width,
            transcendentals=4 * span_block * span_block,
        ),
        name="student_side",
    )(student, full, scalars, own, others)


def shards(
    student_bytes, student_weight, teacher_rows, teacher_weight, span_lengths, span_scale, positives
):
    span_dev = span_scale.shape[0]
    embed_width = student_weight.shape[1]
    lanes = lax.axis_size("narrow")
    blocks = lax.axis_size("blk")
    chips = blocks // 2
    lane = lax.axis_index("narrow")
    block = lax.axis_index("blk")
    core = lax.rem(block, 2)
    chip = lax.div(block, 2)
    span_block = span_dev * lanes
    byte_dev = student_bytes.shape[0]
    feats = teacher_rows.shape[1]
    half = feats // 2

    own_half = lax.dynamic_slice_in_dim(teacher_rows, core * half, half, 1)
    sibling_half = sibling(lax.dynamic_slice_in_dim(teacher_rows, (1 - core) * half, half, 1))

    teacher_part = jnp.dot(teacher_rows, teacher_weight, preferred_element_type=F32)
    student_bytes, teacher_part = lax.optimization_barrier((student_bytes, teacher_part))
    teacher_proj = lax.psum_scatter(teacher_part, "narrow", scatter_dimension=0, tiled=True)

    small = gather_narrow(jnp.stack([span_scale / embed_width, positives.astype(F32)]))
    small = small.transpose(1, 0, 2).reshape(2, span_block)
    ahead_small, mixed_small = following(small)
    other_small = following_other(small)

    byte_lengths = span_lengths[0]
    byte_ends = jnp.cumsum(byte_lengths)
    byte_starts = byte_ends - byte_lengths

    def owner_order(values):
        return values.reshape(span_dev, lanes).T.reshape(span_block)

    lengths = owner_order(byte_lengths)
    ends = owner_order(byte_ends)
    starts = owner_order(byte_starts)
    lengths_f = lengths.astype(F32)[:, None]
    first = lane * byte_dev
    last = first + byte_dev
    byte_pos = first + jnp.arange(byte_dev, dtype=jnp.int32)
    span_table = (
        (byte_pos[None, :] >= starts[:, None]) & (byte_pos[None, :] < ends[:, None])
    ).astype(BF16)
    cut_left = (starts < first) & (ends > first)
    cut_right = (starts < last) & (ends > last)
    left_end = jnp.sum(jnp.where(cut_left, ends, 0))
    right_start = jnp.sum(jnp.where(cut_right, starts - last, 0)) + last
    edge_table = jnp.stack([byte_pos < left_end, byte_pos >= right_start]).astype(BF16)
    projected = jnp.dot(student_bytes, student_weight, preferred_element_type=F32).astype(BF16)
    edges = jnp.dot(edge_table, projected, preferred_element_type=F32)
    from_right = lax.ppermute(edges[0:1], "narrow", [(i + 1, i) for i in range(lanes - 1)])
    from_left = lax.ppermute(edges[1:2], "narrow", [(i, i + 1) for i in range(lanes - 1)])
    partial = jnp.dot(span_table, projected, preferred_element_type=F32)
    pooled = (
        partial
        + jnp.where(cut_right[:, None], from_right, 0.0)
        + jnp.where(cut_left[:, None], from_left, 0.0)
    )
    student_full, student_rms = normalize(pooled / lengths_f)
    begins_here = (starts >= first) & (starts < last)
    student_sparse = jnp.where(begins_here[:, None], student_full, 0.0).astype(BF16)
    student_shard = scatter_narrow(student_sparse, span_dev)
    student_shard, teacher_proj, small, ahead_small, mixed_small, other_small = (
        lax.optimization_barrier(
            (student_shard, teacher_proj, small, ahead_small, mixed_small, other_small)
        )
    )
    factor, positive = small[0], small[1]
    window_small = [small, ahead_small, mixed_small, other_small]
    student = lax.all_gather(student_shard, "narrow", axis=0, tiled=True)

    teacher_full, teacher_rms = normalize(teacher_proj)
    teacher = teacher_full.astype(BF16)
    keys = jnp.concatenate(
        [teacher] + [permute_blk(teacher, lambda i, k=k: i + k) for k in range(1, STOPS)], axis=0
    )
    teacher, student, keys = lax.optimization_barrier((teacher, student, keys))
    teacher_block = lax.all_gather(teacher, "narrow", axis=0, tiled=True)

    ahead, mixed = following(student)
    other = sibling(ahead)
    student_window = [student, ahead, mixed, other]
    mixed_stop = jnp.where(core == 1, 3, 1)
    window_stops = [jnp.int32(0), jnp.int32(2), mixed_stop, 4 - mixed_stop]

    near = jnp.arange(STOPS * span_dev, dtype=jnp.int32)
    near = (near // span_dev) * span_block + lane * span_dev + near % span_dev
    hit = near.astype(F32)[None, :] == positive[:, None]
    scores = contract_last(student, keys) * factor[:, None]
    picked = jnp.sum(jnp.where(hit, scores, 0.0), axis=1)
    row_max = jnp.max(scores, axis=1)
    row_sum = jnp.sum(jnp.exp(scores - row_max[:, None]), axis=1)
    rms_row = jnp.pad(teacher_rms[:, 0], (0, span_block - span_dev))
    stats = gather_narrow(jnp.stack([row_max, row_sum, picked, rms_row]))
    block_rms = stats[:, 3, :span_dev].reshape(span_block, 1)
    top = jnp.max(stats[:, 0], axis=0)
    log_total = top + jnp.log(jnp.sum(stats[:, 1] * jnp.exp(stats[:, 0] - top), axis=0))
    loss = jnp.sum(log_total - jnp.sum(stats[:, 2], axis=0))
    note = jnp.concatenate([log_total, jnp.broadcast_to(loss, (128,))])
    notes = [note, *following(note), following_other(note)]
    window_log_total = [x[:span_block] for x in notes]

    ahead_loss, mixed_loss, other_loss = [x[span_block] for x in notes[1:]]
    four = jnp.stack(
        [
            loss,
            jnp.where(core == 1, other_loss, mixed_loss),
            ahead_loss,
            jnp.where(core == 1, mixed_loss, other_loss),
        ]
    )
    turned = [four] + [permute_blk(four, lambda i, by=by: i - by) for by in range(4, blocks, 4)]
    turned = jnp.concatenate(turned * 2)
    in_order = lax.dynamic_slice_in_dim(turned, lax.rem(blocks - block, blocks), blocks)
    loss_mean = jnp.sum(in_order) / (span_block * blocks)

    others, teacher_block = lax.optimization_barrier((keys[span_dev:], teacher_block))
    others = lax.all_gather(others, "narrow", axis=0)

    small = jnp.stack(
        [x[0] for x in window_small]
        + window_log_total
        + [x[1] - (stop * span_block).astype(F32) for x, stop in zip(window_small, window_stops)]
    )
    teacher_grads = teacher_grads_of(teacher_block, block_rms, student_window, small)
    sibling_grads = sibling(teacher_grads)

    weight_part = contract_first(own_half, teacher_grads) + contract_first(
        sibling_half, sibling_grads
    )
    slice_rows = half // chips
    narrowed = weight_part.astype(BF16)
    total = lax.dynamic_slice_in_dim(weight_part, chip * slice_rows, slice_rows, 0)
    came = []
    for by in range(1, chips):
        target = lax.rem(chip + by, chips)
        piece = lax.dynamic_slice_in_dim(narrowed, target * slice_rows, slice_rows, 0)
        came.append(permute_blk(piece, lambda i, by=by: i + 2 * by))
    for piece in came:
        total = total + piece.astype(F32)
    total = (total + 0.0 * loss_mean).astype(BF16)
    place = positive.astype(jnp.int32)
    stop, place = place // span_block, place % span_block
    at_lane, at_row = place // span_dev, place % span_dev
    columns = [jnp.where(stop == 0, place, -1)] + [
        jnp.where((stop > 0) & (at_lane == i), (stop - 1) * span_dev + at_row, -1)
        for i in range(lanes)
    ]
    scalars = jnp.stack(
        [factor, log_total + 0.0 * weight_part[0, 0], student_rms[:, 0], lengths_f[:, 0]]
        + [x.astype(F32) for x in columns],
        axis=1,
    )
    span_grad = span_grads_of(student, student_full, scalars, teacher_block, others)
    byte_grad = contract_first(span_table, span_grad).astype(BF16)
    grad_bytes = contract_last(byte_grad, student_weight).astype(BF16)

    zero = 0.0 * grad_bytes[0, 0].astype(F32)
    grad_weight = jnp.tile(total.astype(F32), (2 * chips, 1))
    for by in range(chips):
        piece = total if by == 0 else permute_blk(total, lambda i, by=by: i + 2 * by)
        twin = sibling(piece)
        at = lax.rem(chip + chips - by, chips) * slice_rows
        grad_weight = lax.dynamic_update_slice_in_dim(
            grad_weight, piece.astype(F32), core * half + at, 0
        )
        grad_weight = lax.dynamic_update_slice_in_dim(
            grad_weight, twin.astype(F32) + (zero if by == chips - 1 else 0.0), (1 - core) * half + at, 0
        )

    return (loss_mean, grad_bytes, grad_weight)


def solution(mesh):
    return jax.shard_map(
        shards,
        mesh=mesh,
        in_specs=(
            P(("blk", "narrow"), None),
            P(),
            P("blk", "narrow"),
            P("narrow", None),
            P("blk", None),
            P(("blk", "narrow")),
            P(("blk", "narrow")),
        ),
        out_specs=(P(), P(("blk", "narrow"), None), P("narrow", None)),
        check_vma=False,
    )
```

time: 329 us -> 281 us (0.85)
  matrix products: 62.9 us -> 27.8 us
  waiting for transfers between devices: 148 us -> 119 us
  starting transfers between devices: 64 us -> 39.5 us
  local copies, waits for them, and re-layouts: 10.4 us -> 28.1 us
  Pallas kernels: 0 us -> 16.6 us
    reduce_scatter x2 -> x1, waiting for transfers between devices: 71.4 us -> 0.01 us  [shards(): lax.psum_scatter(teacher_part, 'narrow', scatter_dimension=0, tiled=True)]
    ppermute x6, waiting for transfers between devices: 2.45 us -> 37.9 us  [gather_narrow(): lax.ppermute(x, 'narrow', [(i, (i + by) % count) for i in range(count)])]
    dot_general x9 -> x1, matrix products: 37.6 us -> 5.84 us  [shards(): jnp.dot(teacher_rows, teacher_weight, preferred_element_type=F32)]
    ppermute x33 -> x25, starting transfers between devices: 48.8 us -> 20.5 us  [permute_blk(): lax.ppermute(x, 'blk', [(i, target(i) % count) for i in range(count)])]
    pallas_call x0 -> x2, Pallas kernels: none -> 16.6 us  [the longest x1 9.1 us: span_grads_of(): pl.pallas_call(student_side, grid=(span_block // rows,), in_specs=[part,...]
    ppermute x33 -> x25, waiting for transfers between devices: 53.9 us -> 68.7 us  [permute_blk(): lax.ppermute(x, 'blk', [(i, target(i) % count) for i in range(count)])]
    all_gather x1, waiting for transfers between devices: 15.7 us -> 8.41 us  [shards(): student = lax.all_gather(student_shard, 'narrow', axis=0, tiled=True)]
    unnamed x15 -> x28, local copies, waits for them, and re-layouts: 2.45 us -> 9.54 us
  transfers between devices with their start and end apart: 46 -> 40, of which waited for: 18 -> 17; matrix products, arithmetic and copies ran while one was open for 23% -> 24% of each run, Pallas kernels for 0% -> 6%
where the time goes in v2:
time: 281 us; the launch traced here: 280 us
  waiting for transfers between devices  119 us (42%)
  starting transfers between devices  39.5 us (14%)
  local copies, waits for them, and re-layouts  28.1 us (10%)
  matrix products  27.8 us (10%)
  other arithmetic  27.5 us (10%)
  between operations  21.4 us (8%)
  Pallas kernels  16.6 us (6%)
    ppermute x25, waiting for transfers between devices, permute_blk(): lax.ppermute(x, 'blk', [(i, target(i) % count) for i in range(count)])  68.7 us
    ppermute x6, waiting for transfers between devices, gather_narrow(): lax.ppermute(x, 'narrow', [(i, (i + by) % count) for i in range(count)])  37.9 us
    ppermute x25, starting transfers between devices, permute_blk(): lax.ppermute(x, 'blk', [(i, target(i) % count) for i in range(count)])  20.5 us
    unnamed x28, local copies, waits for them, and re-layouts  9.54 us
    dot_general x2, matrix products, contract_last(): lax.dot_general(left, right, (((1,), (1,)), ((), ())), preferred_element_...  9.16 us
    pallas_call x1, Pallas kernels, span_grads_of(): pl.pallas_call(student_side, grid=(span_block // rows,), in_specs=[part,...  9.1 us
    all_gather x1, waiting for transfers between devices, shards(): student = lax.all_gather(student_shard, 'narrow', axis=0, tiled=True)  8.41 us
    ppermute x6, starting transfers between devices, gather_narrow(): lax.ppermute(x, 'narrow', [(i, (i + by) % count) for i in range(count)])  7.99 us
  transfers between devices with their start and end apart: 40, of which 17 were waited for; matrix products, arithmetic and copies ran while one was open for 24% of the time, Pallas kernels for 6%

profile of v2, /device:TPU:0, one launch (start us, length us, event | category | flops | bytes accessed | tf_op | source)
XLA Modules:
  0.0 279.9 jit_solution(9338142097393502296)
XLA Ops:
  8.8 5.8 %fusion.44 = f32[512,1024]{1,0:T(8,128)} fusion(bf16[512,2048]{1,0:T(8,128)(2,1)S(1)} %copy-done, bf16[2048,1024]{1,0:T(8,128)(2,1)} %param.10), kind=kOutput, calls=%fused_computation.125 | convolution fusion | flops 2147483648 | bytes 8388608 | tf_op jit(solution)/shard_map/dot_general | solution.py:182
  18.8 5.2 %convolution_convert_fusion.2 = bf16[512,1024]{1,0:T(8,128)(2,1)S(1)} fusion(bf16[512,2048]{1,0:T(8,128)(2,1)} %param.7, bf16[2048,1024]{1,0:T(8,128)(2,1)} %param.8), kind=kOutput, calls=%fused_computation.6 | convolution fusion | flops 2148007936 | bytes 7340032 | tf_op jit(solution)/shard_map/dot_general | solution.py:213
  24.3 4.9 %collective-permute-start.1 = (f32[1,1024]{1,0:T(1,128)S(1)}, f32[1,1024]{1,0:T(1,128)S(1)}, u32[]{:S(2)}, u32[]{:S(2)}) collective-permute-start(f32[1,1024]{1,0:T(1,128)S(1)} %get-tuple-element.55), channel_id=1, source_target_pairs={{0,1},{1,2},{2,3},{4,5},{5,6},{6,7},{8,9},{9,10},{10,11},{12,13},{... | collective-permute-start | bytes 12296 | tf_op jit(solution)/shard_map/ppermute | solution.py:216
  30.8 4.0 %collective-permute-done = f32[1,1024]{1,0:T(1,128)S(1)} collective-permute-done((f32[1,1024]{1,0:T(1,128)S(1)}, f32[1,1024]{1,0:T(1,128)S(1)}, u32[]{:S(2)}, u32[]{:S(2)}) %collective-permute-start) | collective-permute-done | bytes 4128 | tf_op jit(solution)/shard_map/ppermute | solution.py:215
  43.7 2.3 collective-permute-start.6
  46.0 31.5 %collective-permute-done.5 = f32[2,128]{1,0:T(2,128)S(1)} collective-permute-done((f32[2,128]{1,0:T(2,128)S(1)}, f32[2,128]{1,0:T(2,128)S(1)}, u32[]{:S(2)}, u32[]{:S(2)}) %collective-permute-start.5) | collective-permute-done | bytes 1056 | tf_op jit(solution)/shard_map/ppermute | solution.py:49
  77.6 5.2 %collective-permute-done.6 = f32[2,128]{1,0:T(2,128)S(1)} collective-permute-done((f32[2,128]{1,0:T(2,128)S(1)}, f32[2,128]{1,0:T(2,128)S(1)}, u32[]{:S(2)}, u32[]{:S(2)}) %collective-permute-start.6) | collective-permute-done | bytes 1056 | tf_op jit(solution)/shard_map/ppermute | solution.py:49
  82.9 2.4 collective-permute-start.8
  93.2 14.7 %collective-permute-done.13 = bf16[128,1024]{1,0:T(8,128)(2,1)S(1)} collective-permute-done((bf16[128,1024]{1,0:T(8,128)(2,1)S(1)}, bf16[128,1024]{1,0:T(8,128)(2,1)S(1)}, u32[]{:S(2)}, u32[]{:S(2)}) %collective-permute-start.13) | collective-permute-done | bytes 262176 | tf_op jit(solution)/shard_map/ppermute | solution.py:36
  108.9 8.4 %all-gather.5.cloned.1.call-done.s0_ref.student_ref = bf16[512,1024]{1,0:T(8,128)(2,1)} async-done(((bf16[128,1024]{1,0:T(8,128)(2,1)}), bf16[512,1024]{1,0:T(8,128)(2,1)}) %all-gather.5.cloned.1.call-update) | async-done | bytes 1048592 | tf_op jit(solution)/shard_map/all_gather | solution.py:234
  117.3 2.4 collective-permute-start.21
  121.0 2.3 fusion.42
  123.3 19.1 %collective-permute-done.21.s1_ref = bf16[512,1024]{1,0:T(8,128)(2,1)S(1)} collective-permute-done((bf16[512,1024]{1,0:T(8,128)(2,1)}, bf16[512,1024]{1,0:T(8,128)(2,1)S(1)}, u32[]{:S(2)}, u32[]{:S(2)}) %collective-permute-start.21) | collective-permute-done | bytes 1048608 | tf_op jit(solution)/shard_map/ppermute | solution.py:36
  161.6 7.5 %teacher_side.1 = bf16[512,1024]{1,0:T(8,128)(2,1)S(1)} custom-call(bf16[512,1024]{1,0:T(8,128)(2,1)S(1)} %copy-done.4, f32[512,1]{1,0:T(8,128)S(1)} %copy.67.rms_ref, bf16[512,1024]{1,0:T(8,128)(2,1)S(1)} %copy-done.2, bf16[512,1024]{1,0:T(8,128)(2,1)S(1)} %copy-done.7, bf16[512,1024]{1,0:T(8,128)(2,1)} %collective-permute-done.22.s2_ref, ...), custom_call_target="tpu_custom_call" | custom-call | flops 4294967296 | bytes 7340032 | tf_op jit(solution)/shard_map/teacher_side/pallas_call | solution.py:98
  169.8 2.3 collective-permute-done.25
  172.1 2.8 %fusion.45 = f32[1024,1024]{1,0:T(8,128)S(1)} fusion(bf16[512,1024]{1,0:T(8,128)(2,1)} %collective-permute-done.24, bf16[512,1024]{1,0:T(8,128)(2,1)} %collective-permute-done.25), kind=kOutput, calls=%fused_computation.126 | convolution fusion | flops 1073741824 | bytes 6291456 | tf_op jit(solution)/shard_map/dot_general | solution.py:27
  174.9 3.4 %fusion.43 = (bf16[1024,1024]{1,0:T(8,128)(2,1)S(1)}, f32[1024,1024]{1,0:T(8,128)}) fusion(f32[1024,1024]{1,0:T(8,128)S(1)} %fusion.45, bf16[512,1024]{1,0:T(8,128)(2,1)S(1)} %teacher_side.1, bf16[512,2048]{1,0:T(8,128)(2,1)S(1)} %copy-done, s32[]{:T(128)S(6)} %select_n.297), kind=kOutput, calls=%fused_computation.124 | convolution fusion | flops 1075838976 | bytes 12582916 | tf_op jit(solution)/shard_map/dot_general | solution.py:27
  189.1 17.0 %collective-permute-done.20 = f32[4]{0:T(128)S(1)} collective-permute-done((f32[4]{0:T(128)S(1)}, f32[4]{0:T(128)S(1)}, u32[]{:S(2)}, u32[]{:S(2)}) %collective-permute-start.20) | collective-permute-done | bytes 48 | tf_op jit(solution)/shard_map/ppermute | solution.py:36
  206.1 2.7 concatenate.12
  218.8 4.5 %tile.4 = f32[8,256,1024]{2,1,0:T(8,128)} broadcast(bf16[256,1024]{1,0:T(8,128)(2,1)S(1)} %add_convert_fusion), dimensions={1,2} | broadcast | bytes 8912896 | tf_op jit(solution)/shard_map/tile | solution.py:323
  224.4 3.8 %collective-permute-done.30 = bf16[256,1024]{1,0:T(8,128)(2,1)} collective-permute-done((bf16[256,1024]{1,0:T(8,128)(2,1)S(1)}, bf16[256,1024]{1,0:T(8,128)(2,1)}, u32[]{:S(2)}, u32[]{:S(2)}) %collective-permute-start.30) | collective-permute-done | bytes 524320 | tf_op jit(solution)/shard_map/ppermute | solution.py:36
  228.2 10.0 %collective-permute-done.32 = bf16[256,1024]{1,0:T(8,128)(2,1)} collective-permute-done((bf16[256,1024]{1,0:T(8,128)(2,1)S(1)}, bf16[256,1024]{1,0:T(8,128)(2,1)}, u32[]{:S(2)}, u32[]{:S(2)}) %collective-permute-start.32) | collective-permute-done | bytes 524320 | tf_op jit(solution)/shard_map/ppermute | solution.py:36
  251.1 9.1 %student_side.1 = bf16[512,1024]{1,0:T(8,128)(2,1)S(1)} custom-call(bf16[512,1024]{1,0:T(8,128)(2,1)S(1)} %copy-done.3, f32[512,1024]{1,0:T(8,128)S(1)} %copy-done.1, f32[512,9]{1,0:T(8,128)S(1)} %copy.69.scalar_ref, bf16[512,1024]{1,0:T(8,128)(2,1)S(1)} %copy-done.5, bf16[4,384,1024]{2,1,0:T(8,128)(2,1)} %bitcast.138), custom_call_target="tpu_custom_call" | custom-call | flops 4294967296 | bytes 8388608 | tf_op jit(solution)/shard_map/student_side/pallas_call | solution.py:140
  261.2 6.9 %convolution_convert_fusion = bf16[512,2048]{1,0:T(8,128)(2,1)} fusion(bf16[2048,1024]{1,0:T(8,128)(2,1)} %param.8, bf16[512,1024]{1,0:T(8,128)(2,1)} %copy-done.8, s32[512]{0:T(512)S(1)} %iota_add_fusion.1, s32[512]{0:T(512)S(1)} %bitcast.123, s32[512]{0:T(512)S(1)} %bitcast.125), kind=kOutput, calls=%fused_computation | convolution fusion | flops 2686713856 | bytes 7346176 | tf_op jit(solution)/shard_map/dot_general | solution.py:31
  (185 shorter events, 80.4 us)
Async XLA Ops:
  7.2 81.2 %reduce-scatter.2.cloned.1.call-start = ((), (), s32[]{:S(2)}) async-start(), calls=%async_computation.1 | async-start | bytes 2621440 | tf_op jit(solution)/shard_map/reduce_scatter | solution.py:184
  14.6 102.7 %all-gather.5.cloned.1.call-start = ((), (), s32[]{:S(2)}) async-start(), calls=%async_computation.2 | async-start | bytes 1310720 | tf_op jit(solution)/shard_map/all_gather | solution.py:234
  38.4 46.9 %collective-permute-start.4 = (bf16[128,1024]{1,0:T(8,128)(2,1)}, bf16[128,1024]{1,0:T(8,128)(2,1)}, u32[]{:S(2)}, u32[]{:S(2)}) collective-permute-start(bf16[128,1024]{1,0:T(8,128)(2,1)} %get-tuple-element.50), channel_id=1, source_target_pairs={{0,3},{1,0},{2,1},{3,2},{4,7},{5,4},{6,5},{7,6},{8,11},{9,8},{10,9... | collective-permute-start | bytes 786440 | tf_op jit(solution)/shard_map/ppermute | solution.py:71
  40.2 45.9 %collective-permute-start.3 = (bf16[128,1024]{1,0:T(8,128)(2,1)}, bf16[128,1024]{1,0:T(8,128)(2,1)}, u32[]{:S(2)}, u32[]{:S(2)}) collective-permute-start(bf16[128,1024]{1,0:T(8,128)(2,1)} %get-tuple-element.51), channel_id=1, source_target_pairs={{0,2},{1,3},{2,0},{3,1},{4,6},{5,7},{6,4},{7,5},{8,10},{9,11},{10,... | collective-permute-start | bytes 786440 | tf_op jit(solution)/shard_map/ppermute | solution.py:71
  41.6 44.5 %collective-permute-start.2 = (bf16[128,1024]{1,0:T(8,128)(2,1)S(1)}, bf16[128,1024]{1,0:T(8,128)(2,1)}, u32[]{:S(2)}, u32[]{:S(2)}) collective-permute-start(bf16[128,1024]{1,0:T(8,128)(2,1)S(1)} %get-tuple-element.49), channel_id=1, source_target_pairs={{0,1},{1,2},{2,3},{3,0},{4,5},{5,6},{6,7},{7,4},{8,9},{9,10},{10,1... | collective-permute-start | bytes 786440 | tf_op jit(solution)/shard_map/ppermute | solution.py:71
  43.1 34.5 %collective-permute-start.5 = (f32[2,128]{1,0:T(2,128)S(1)}, f32[2,128]{1,0:T(2,128)S(1)}, u32[]{:S(2)}, u32[]{:S(2)}) collective-permute-start(f32[2,128]{1,0:T(2,128)S(1)} %pad_maximum_fusion.2), channel_id=1, source_target_pairs={{0,1},{1,2},{2,3},{3,0},{4,5},{5,6},{6,7},{7,4},{8,9},{9,10},{10,1... | collective-permute-start | bytes 3080 | tf_op jit(solution)/shard_map/ppermute | solution.py:49
  43.7 39.1 %collective-permute-start.6 = (f32[2,128]{1,0:T(2,128)S(1)}, f32[2,128]{1,0:T(2,128)S(1)}, u32[]{:S(2)}, u32[]{:S(2)}) collective-permute-start(f32[2,128]{1,0:T(2,128)S(1)} %pad_maximum_fusion.2), channel_id=1, source_target_pairs={{0,2},{1,3},{2,0},{3,1},{4,6},{5,7},{6,4},{7,5},{8,10},{9,11},{10,... | collective-permute-start | bytes 3080 | tf_op jit(solution)/shard_map/ppermute | solution.py:49
  88.4 69.5 %all-gather.7.cloned.1.call-start = ((), (), s32[]{:S(2)}) async-start(), calls=%async_computation.3 | async-start | bytes 1310720 | tf_op jit(solution)/shard_map/all_gather | solution.py:242
  90.8 17.1 %collective-permute-start.13 = (bf16[128,1024]{1,0:T(8,128)(2,1)S(1)}, bf16[128,1024]{1,0:T(8,128)(2,1)S(1)}, u32[]{:S(2)}, u32[]{:S(2)}) collective-permute-start(bf16[128,1024]{1,0:T(8,128)(2,1)S(1)} %multiply_convert_fusion), channel_id=1, source_target_pairs={{0,12},{4,16},{8,20},{12,24},{16,28},{20,0},{24,4},{28,8},{1,13},{... | collective-permute-start | bytes 786440 | tf_op jit(solution)/shard_map/ppermute | solution.py:36
  91.8 16.1 %collective-permute-start.12 = (bf16[128,1024]{1,0:T(8,128)(2,1)S(1)}, bf16[128,1024]{1,0:T(8,128)(2,1)S(1)}, u32[]{:S(2)}, u32[]{:S(2)}) collective-permute-start(bf16[128,1024]{1,0:T(8,128)(2,1)S(1)} %multiply_convert_fusion), channel_id=1, source_target_pairs={{0,8},{4,12},{8,16},{12,20},{16,24},{20,28},{24,0},{28,4},{1,9},{5... | collective-permute-start | bytes 786440 | tf_op jit(solution)/shard_map/ppermute | solution.py:36
  93.2 14.7 %collective-permute-start.11 = (bf16[128,1024]{1,0:T(8,128)(2,1)S(1)}, bf16[128,1024]{1,0:T(8,128)(2,1)S(1)}, u32[]{:S(2)}, u32[]{:S(2)}) collective-permute-start(bf16[128,1024]{1,0:T(8,128)(2,1)S(1)} %multiply_convert_fusion), channel_id=1, source_target_pairs={{0,4},{4,8},{8,12},{12,16},{16,20},{20,24},{24,28},{28,0},{1,5},{5... | collective-permute-start | bytes 786440 | tf_op jit(solution)/shard_map/ppermute | solution.py:36
  117.3 25.0 %collective-permute-start.21 = (bf16[512,1024]{1,0:T(8,128)(2,1)}, bf16[512,1024]{1,0:T(8,128)(2,1)S(1)}, u32[]{:S(2)}, u32[]{:S(2)}) collective-permute-start(bf16[512,1024]{1,0:T(8,128)(2,1)} %all-gather.5.cloned.1.call-done.s0_ref.student_ref), channel_id=1, source_target_pairs={{0,24},{4,28},{8,0},{12,4},{16,8},{20,12},{24,16},{28,20},{1,25},{... | collective-permute-start | bytes 3145736 | tf_op jit(solution)/shard_map/ppermute | solution.py:36
  120.8 127.5 %all-gather.9.cloned.1.call-start = ((), (), s32[]{:S(2)}) async-start(), calls=%async_computation.4 | async-start | bytes 3932160 | tf_op jit(solution)/shard_map/all_gather | solution.py:282
  120.9 37.0 %collective-permute-start.22 = (bf16[512,1024]{1,0:T(8,128)(2,1)}, bf16[512,1024]{1,0:T(8,128)(2,1)}, u32[]{:S(2)}, u32[]{:S(2)}) collective-permute-start(bf16[512,1024]{1,0:T(8,128)(2,1)} %all-gather.5.cloned.1.call-done.s0_ref.student_ref), channel_id=1, source_target_pairs={{0,20},{4,0},{8,28},{12,8},{16,4},{20,16},{24,12},{28,24},{1,21},{... | collective-permute-start | bytes 3145736 | tf_op jit(solution)/shard_map/ppermute | solution.py:36
  142.4 15.6 %collective-permute-start.23 = (bf16[512,1024]{1,0:T(8,128)(2,1)S(1)}, bf16[512,1024]{1,0:T(8,128)(2,1)}, u32[]{:S(2)}, u32[]{:S(2)}) collective-permute-start(bf16[512,1024]{1,0:T(8,128)(2,1)S(1)} %collective-permute-done.21.s1_ref), channel_id=1, source_target_pairs={{0,4},{4,0},{8,12},{12,8},{16,20},{20,16},{24,28},{28,24},{1,5},{5... | collective-permute-start | bytes 3145736 | tf_op jit(solution)/shard_map/ppermute | solution.py:36
  179.2 31.0 %collective-permute-start.28 = (bf16[256,1024]{1,0:T(8,128)(2,1)}, bf16[256,1024]{1,0:T(8,128)(2,1)}, u32[]{:S(2)}, u32[]{:S(2)}) collective-permute-start(bf16[256,1024]{1,0:T(8,128)(2,1)} %get-tuple-element.47), channel_id=1, source_target_pairs={{0,24},{4,28},{8,0},{12,4},{16,8},{20,12},{24,16},{28,20},{1,25},{... | collective-permute-start | bytes 1572872 | tf_op jit(solution)/shard_map/ppermute | solution.py:36
  180.9 29.3 %collective-permute-start.27 = (bf16[256,1024]{1,0:T(8,128)(2,1)S(1)}, bf16[256,1024]{1,0:T(8,128)(2,1)}, u32[]{:S(2)}, u32[]{:S(2)}) collective-permute-start(bf16[256,1024]{1,0:T(8,128)(2,1)S(1)} %get-tuple-element.48), channel_id=1, source_target_pairs={{0,16},{4,20},{8,24},{12,28},{16,0},{20,4},{24,8},{28,12},{1,17},{... | collective-permute-start | bytes 1572872 | tf_op jit(solution)/shard_map/ppermute | solution.py:36
  181.6 28.6 %collective-permute-start.26 = (bf16[256,1024]{1,0:T(8,128)(2,1)S(1)}, bf16[256,1024]{1,0:T(8,128)(2,1)}, u32[]{:S(2)}, u32[]{:S(2)}) collective-permute-start(bf16[256,1024]{1,0:T(8,128)(2,1)S(1)} %get-tuple-element.46), channel_id=1, source_target_pairs={{0,8},{4,12},{8,16},{12,20},{16,24},{20,28},{24,0},{28,4},{1,9},{5... | collective-permute-start | bytes 1572872 | tf_op jit(solution)/shard_map/ppermute | solution.py:36
  188.6 17.5 %collective-permute-start.20 = (f32[4]{0:T(128)S(1)}, f32[4]{0:T(128)S(1)}, u32[]{:S(2)}, u32[]{:S(2)}) collective-permute-start(f32[4]{0:T(128)S(1)} %pad_maximum_fusion.3), channel_id=1, source_target_pairs={{0,16},{4,20},{8,24},{12,28},{16,0},{20,4},{24,8},{28,12},{1,17},{... | collective-permute-start | bytes 56 | tf_op jit(solution)/shard_map/ppermute | solution.py:36
  212.3 26.4 %collective-permute-start.29 = (bf16[256,1024]{1,0:T(8,128)(2,1)S(1)}, bf16[256,1024]{1,0:T(8,128)(2,1)S(1)}, u32[]{:S(2)}, u32[]{:S(2)}) collective-permute-start(bf16[256,1024]{1,0:T(8,128)(2,1)S(1)} %add_convert_fusion), channel_id=1, source_target_pairs={{0,4},{4,0},{8,12},{12,8},{16,20},{20,16},{24,28},{28,24},{1,5},{5... | collective-permute-start | bytes 1572872 | tf_op jit(solution)/shard_map/ppermute | solution.py:36
  212.4 15.8 %collective-permute-start.30 = (bf16[256,1024]{1,0:T(8,128)(2,1)S(1)}, bf16[256,1024]{1,0:T(8,128)(2,1)}, u32[]{:S(2)}, u32[]{:S(2)}) collective-permute-start(bf16[256,1024]{1,0:T(8,128)(2,1)S(1)} %add_convert_fusion), channel_id=1, source_target_pairs={{0,8},{4,12},{8,16},{12,20},{16,24},{20,28},{24,0},{28,4},{1,9},{5... | collective-permute-start | bytes 1572872 | tf_op jit(solution)/shard_map/ppermute | solution.py:36
  212.8 25.3 %collective-permute-start.32 = (bf16[256,1024]{1,0:T(8,128)(2,1)S(1)}, bf16[256,1024]{1,0:T(8,128)(2,1)}, u32[]{:S(2)}, u32[]{:S(2)}) collective-permute-start(bf16[256,1024]{1,0:T(8,128)(2,1)S(1)} %add_convert_fusion), channel_id=1, source_target_pairs={{0,16},{4,20},{8,24},{12,28},{16,0},{20,4},{24,8},{28,12},{1,17},{... | collective-permute-start | bytes 1572872 | tf_op jit(solution)/shard_map/ppermute | solution.py:36
  214.3 24.0 %collective-permute-start.34 = (bf16[256,1024]{1,0:T(8,128)(2,1)S(1)}, bf16[256,1024]{1,0:T(8,128)(2,1)}, u32[]{:S(2)}, u32[]{:S(2)}) collective-permute-start(bf16[256,1024]{1,0:T(8,128)(2,1)S(1)} %add_convert_fusion), channel_id=1, source_target_pairs={{0,24},{4,28},{8,0},{12,4},{16,8},{20,12},{24,16},{28,20},{1,25},{... | collective-permute-start | bytes 1572872 | tf_op jit(solution)/shard_map/ppermute | solution.py:36
  238.3 31.8 %collective-permute-start.35 = (bf16[256,1024]{1,0:T(8,128)(2,1)}, bf16[256,1024]{1,0:T(8,128)(2,1)}, u32[]{:S(2)}, u32[]{:S(2)}) collective-permute-start(bf16[256,1024]{1,0:T(8,128)(2,1)} %collective-permute-done.34), channel_id=1, source_target_pairs={{0,4},{4,0},{8,12},{12,8},{16,20},{20,16},{24,28},{28,24},{1,5},{5... | collective-permute-start | bytes 1572872 | tf_op jit(solution)/shard_map/ppermute | solution.py:36
  (29 other events, 181.2 us)
Sparse Core Ops, SparseCore 0:
  14.7 62.9 reduce-scatter.1
  88.6 28.7 all-gather.4
  121.0 25.5 all-gather.6
  169.8 64.3 all-gather.8

commit v3 on v2

--- a/solution.py
+++ b/solution.py
@@ -8,6 +8,7 @@
 from jax.sharding import PartitionSpec as P
 
 STOPS = 4
+MOST_BYTES = 16
 EPS = 1e-06
 BF16 = jnp.bfloat16
 F32 = jnp.float32
@@ -159,6 +160,34 @@
     )(student, full, scalars, own, others)
 
 
+def assemble(order_ref, *refs):
+    for at, ref in enumerate(refs[:-1]):
+
+        @pl.when(pl.program_id(0) == at)
+        def _(ref=ref):
+            refs[-1][...] = ref[...].astype(F32)
+
+
+def assembled(order, pieces):
+    rows, width = pieces[0].shape
+    count = len(pieces)
+    return pl.pallas_call(
+        assemble,
+        grid_spec=pltpu.PrefetchScalarGridSpec(
+            num_scalar_prefetch=1,
+            grid=(count,),
+            in_specs=[pl.BlockSpec((rows, width), lambda i, order: (0, 0))] * count,
+            out_specs=pl.BlockSpec((rows, width), lambda i, order: (order[i], 0)),
+        ),
+        out_shape=jax.ShapeDtypeStruct((count * rows, width), F32),
+        compiler_params=pltpu.CompilerParams(vmem_limit_bytes=32 * 1024 * 1024),
+        cost_estimate=pl.CostEstimate(
+            flops=count * rows * width, bytes_accessed=6 * count * rows * width, transcendentals=0
+        ),
+        name="assemble",
+    )(order, *pieces)
+
+
 def shards(
     student_bytes, student_weight, teacher_rows, teacher_weight, span_lengths, span_scale, positives
 ):
@@ -179,6 +208,15 @@
     own_half = lax.dynamic_slice_in_dim(teacher_rows, core * half, half, 1)
     sibling_half = sibling(lax.dynamic_slice_in_dim(teacher_rows, (1 - core) * half, half, 1))
 
+    spread = jnp.arange(MOST_BYTES, dtype=jnp.int32)
+    edge_bytes = jnp.concatenate(
+        [
+            lax.ppermute(student_bytes[-MOST_BYTES:], "narrow", [(i, i + 1) for i in range(lanes - 1)]),
+            lax.ppermute(student_bytes[:MOST_BYTES], "narrow", [(i + 1, i) for i in range(lanes - 1)]),
+        ],
+        axis=0,
+    )
+
     teacher_part = jnp.dot(teacher_rows, teacher_weight, preferred_element_type=F32)
     student_bytes, teacher_part = lax.optimization_barrier((student_bytes, teacher_part))
     teacher_proj = lax.psum_scatter(teacher_part, "narrow", scatter_dimension=0, tiled=True)
@@ -205,45 +243,39 @@
     span_table = (
         (byte_pos[None, :] >= starts[:, None]) & (byte_pos[None, :] < ends[:, None])
     ).astype(BF16)
-    cut_left = (starts < first) & (ends > first)
-    cut_right = (starts < last) & (ends > last)
-    left_end = jnp.sum(jnp.where(cut_left, ends, 0))
-    right_start = jnp.sum(jnp.where(cut_right, starts - last, 0)) + last
-    edge_table = jnp.stack([byte_pos < left_end, byte_pos >= right_start]).astype(BF16)
+    edge_pos = jnp.concatenate([first - MOST_BYTES + spread, last + spread])
+    edge_table = (
+        (edge_pos[None, :] >= starts[:, None]) & (edge_pos[None, :] < ends[:, None])
+    ).astype(BF16)
     projected = jnp.dot(student_bytes, student_weight, preferred_element_type=F32).astype(BF16)
-    edges = jnp.dot(edge_table, projected, preferred_element_type=F32)
-    from_right = lax.ppermute(edges[0:1], "narrow", [(i + 1, i) for i in range(lanes - 1)])
-    from_left = lax.ppermute(edges[1:2], "narrow", [(i, i + 1) for i in range(lanes - 1)])
-    partial = jnp.dot(span_table, projected, preferred_element_type=F32)
-    pooled = (
-        partial
-        + jnp.where(cut_right[:, None], from_right, 0.0)
-        + jnp.where(cut_left[:, None], from_left, 0.0)
+    projected_edge = jnp.dot(edge_bytes, student_weight, preferred_element_type=F32).astype(BF16)
+    pooled = jnp.dot(span_table, projected, preferred_element_type=F32) + jnp.dot(
+        edge_table, projected_edge, preferred_element_type=F32
     )
     student_full, student_rms = normalize(pooled / lengths_f)
     begins_here = (starts >= first) & (starts < last)
     student_sparse = jnp.where(begins_here[:, None], student_full, 0.0).astype(BF16)
+    student_sparse, small, ahead_small, mixed_small, other_small, own_half = (
+        lax.optimization_barrier(
+            (student_sparse, small, ahead_small, mixed_small, other_small, own_half)
+        )
+    )
     student_shard = scatter_narrow(student_sparse, span_dev)
-    student_shard, teacher_proj, small, ahead_small, mixed_small, other_small = (
-        lax.optimization_barrier(
-            (student_shard, teacher_proj, small, ahead_small, mixed_small, other_small)
-        )
-    )
     factor, positive = small[0], small[1]
     window_small = [small, ahead_small, mixed_small, other_small]
+    student_shard, teacher_proj = lax.optimization_barrier((student_shard, teacher_proj))
     student = lax.all_gather(student_shard, "narrow", axis=0, tiled=True)
 
     teacher_full, teacher_rms = normalize(teacher_proj)
     teacher = teacher_full.astype(BF16)
-    keys = jnp.concatenate(
-        [teacher] + [permute_blk(teacher, lambda i, k=k: i + k) for k in range(1, STOPS)], axis=0
-    )
-    teacher, student, keys = lax.optimization_barrier((teacher, student, keys))
+    others = jnp.concatenate(
+        [permute_blk(teacher, lambda i, k=k: i + k) for k in range(1, STOPS)], axis=0
+    )
+    keys = jnp.concatenate([teacher, others], axis=0)
+    teacher, student, keys, others = lax.optimization_barrier((teacher, student, keys, others))
     teacher_block = lax.all_gather(teacher, "narrow", axis=0, tiled=True)
 
     ahead, mixed = following(student)
-    other = sibling(ahead)
-    student_window = [student, ahead, mixed, other]
     mixed_stop = jnp.where(core == 1, 3, 1)
     window_stops = [jnp.int32(0), jnp.int32(2), mixed_stop, 4 - mixed_stop]
 
@@ -260,25 +292,22 @@
     top = jnp.max(stats[:, 0], axis=0)
     log_total = top + jnp.log(jnp.sum(stats[:, 1] * jnp.exp(stats[:, 0] - top), axis=0))
     loss = jnp.sum(log_total - jnp.sum(stats[:, 2], axis=0))
+    ahead, log_total = lax.optimization_barrier((ahead, log_total))
+    student_window = [student, ahead, mixed, sibling(ahead)]
     note = jnp.concatenate([log_total, jnp.broadcast_to(loss, (128,))])
     notes = [note, *following(note), following_other(note)]
     window_log_total = [x[:span_block] for x in notes]
 
-    ahead_loss, mixed_loss, other_loss = [x[span_block] for x in notes[1:]]
-    four = jnp.stack(
-        [
-            loss,
-            jnp.where(core == 1, other_loss, mixed_loss),
-            ahead_loss,
-            jnp.where(core == 1, mixed_loss, other_loss),
-        ]
-    )
-    turned = [four] + [permute_blk(four, lambda i, by=by: i - by) for by in range(4, blocks, 4)]
-    turned = jnp.concatenate(turned * 2)
-    in_order = lax.dynamic_slice_in_dim(turned, lax.rem(blocks - block, blocks), blocks)
-    loss_mean = jnp.sum(in_order) / (span_block * blocks)
-
-    others, teacher_block = lax.optimization_barrier((keys[span_dev:], teacher_block))
+    spots = jnp.arange(128, dtype=jnp.int32)
+    terms = jnp.zeros((128,), F32)
+    for x, stop in zip(notes, window_stops):
+        terms = jnp.where(spots == lax.rem(block + stop, blocks), x[span_block:], terms)
+    own_terms = terms
+    for by in range(4, blocks, 4):
+        terms = terms + permute_blk(own_terms, lambda i, by=by: i - by)
+    loss_mean = jnp.sum(terms) / (span_block * blocks)
+
+    others, log_total = lax.optimization_barrier((others, log_total))
     others = lax.all_gather(others, "narrow", axis=0)
 
     small = jnp.stack(
@@ -319,19 +348,17 @@
     byte_grad = contract_first(span_table, span_grad).astype(BF16)
     grad_bytes = contract_last(byte_grad, student_weight).astype(BF16)
 
-    zero = 0.0 * grad_bytes[0, 0].astype(F32)
-    grad_weight = jnp.tile(total.astype(F32), (2 * chips, 1))
+    pieces = []
+    order = []
     for by in range(chips):
         piece = total if by == 0 else permute_blk(total, lambda i, by=by: i + 2 * by)
-        twin = sibling(piece)
-        at = lax.rem(chip + chips - by, chips) * slice_rows
-        grad_weight = lax.dynamic_update_slice_in_dim(
-            grad_weight, piece.astype(F32), core * half + at, 0
-        )
-        grad_weight = lax.dynamic_update_slice_in_dim(
-            grad_weight, twin.astype(F32) + (zero if by == chips - 1 else 0.0), (1 - core) * half + at, 0
-        )
-
+        if by > 0:
+            made = span_grad if by == chips - 1 else grad_bytes
+            piece, _ = lax.optimization_barrier((piece, made))
+        pieces += [piece, sibling(piece)]
+        at = lax.rem(chip + chips - by, chips)
+        order += [core * chips + at, (1 - core) * chips + at]
+    grad_weight = assembled(jnp.stack(order), pieces)
     return (loss_mean, grad_bytes, grad_weight)
 
 

time: 281 us -> 247 us (0.88)
  waiting for transfers between devices: 119 us -> 99.7 us
  other arithmetic: 27.5 us -> 13.7 us
  local copies, waits for them, and re-layouts: 28.1 us -> 15 us
  Pallas kernels: 16.6 us -> 23.4 us
  starting transfers between devices: 39.5 us -> 44.6 us
  matrix products: 27.8 us -> 32.3 us
  between operations: 21.4 us -> 17.4 us
    ppermute x6, waiting for transfers between devices: 37.9 us -> 1.1 us  [gather_narrow(): lax.ppermute(x, 'narrow', [(i, (i + by) % count) for i in range(count)])]
    ppermute x3, waiting for transfers between devices: 0.01 us -> 32 us  [scatter_narrow(): lax.ppermute(piece, 'narrow', [(i, (i + by) % count) for i in range(count)])]
    dynamic_update_slice x8 -> x0, other arithmetic: 12.9 us -> none  [the longest x4 7.46 us: shards(): lax.dynamic_update_slice_in_dim(grad_weight, piece.astype(F32), core * ha...]
    ppermute x25, waiting for transfers between devices: 68.7 us -> 61.7 us  [permute_blk(): lax.ppermute(x, 'blk', [(i, target(i) % count) for i in range(count)])]
    pallas_call x0 -> x1, Pallas kernels: none -> 6.49 us  [assembled(): pl.pallas_call(assemble, grid_spec=pltpu.PrefetchScalarGridSpec(num_scala...]
    another operation x5, local copies, waits for them, and re-layouts: 4.84 us -> 0.47 us  [the longest x1 4.46 us: shards(): grad_weight = jnp.tile(total.astype(F32), (2 * chips, 1))]
    slice x7 -> x2, local copies, waits for them, and re-layouts: 5.16 us -> 0.96 us  [the longest x1 0.89 us: shards(): student_bytes[-MOST_BYTES:]]
    ppermute x2, waiting for transfers between devices: 3.97 us -> 0.01 us  [the longest x1 0.01 us: shards(): lax.ppermute(student_bytes[-MOST_BYTES:], 'narrow', [(i, i + 1) for i in...]
  transfers between devices with their start and end apart: 40 -> 40, of which waited for: 17 -> 16; matrix products, arithmetic and copies ran while one was open for 24% -> 19% of each run, Pallas kernels for 6% -> 7%
where the time goes in v3:
time: 247 us; the launch traced here: 246 us
  waiting for transfers between devices  99.7 us (40%)
  starting transfers between devices  44.6 us (18%)
  matrix products  32.3 us (13%)
  Pallas kernels  23.4 us (9%)
  between operations  17.4 us (7%)
  local copies, waits for them, and re-layouts  15 us (6%)
  other arithmetic  13.7 us (6%)
    ppermute x25, waiting for transfers between devices, permute_blk(): lax.ppermute(x, 'blk', [(i, target(i) % count) for i in range(count)])  61.7 us
    ppermute x3, waiting for transfers between devices, scatter_narrow(): lax.ppermute(piece, 'narrow', [(i, (i + by) % count) for i in range(count)])  32 us
    ppermute x25, starting transfers between devices, permute_blk(): lax.ppermute(x, 'blk', [(i, target(i) % count) for i in range(count)])  24.3 us
    ppermute x6, starting transfers between devices, gather_narrow(): lax.ppermute(x, 'narrow', [(i, (i + by) % count) for i in range(count)])  11.9 us
    dot_general x2, matrix products, contract_last(): lax.dot_general(left, right, (((1,), (1,)), ((), ())), preferred_element_...  9.24 us
    pallas_call x1, Pallas kernels, span_grads_of(): pl.pallas_call(student_side, grid=(span_block // rows,), in_specs=[part,...  9.1 us
    pallas_call x1, Pallas kernels, teacher_grads_of(): pl.pallas_call(functools.partial(teacher_side, rows), grid=(span_block //...  7.79 us
    unnamed x26, local copies, waits for them, and re-layouts  7.13 us
  transfers between devices with their start and end apart: 40, of which 16 were waited for; matrix products, arithmetic and copies ran while one was open for 19% of the time, Pallas kernels for 7%

profile of v3, /device:TPU:0, one launch (start us, length us, event | category | flops | bytes accessed | tf_op | source)
XLA Modules:
  0.0 246.0 jit_solution(1629408574805919098)
XLA Ops:
  7.2 6.5 %fusion.51 = f32[512,1024]{1,0:T(8,128)} fusion(bf16[512,2048]{1,0:T(8,128)(2,1)} %param.9, bf16[2048,1024]{1,0:T(8,128)(2,1)} %param.10), kind=kOutput, calls=%fused_computation.121 | convolution fusion | flops 2147483648 | bytes 8388608 | tf_op jit(solution)/shard_map/dot_general | solution.py:220
  14.4 3.1 %collective-permute-start.2 = (f32[2,128]{1,0:T(2,128)S(1)}, f32[2,128]{1,0:T(2,128)S(1)}, u32[]{:S(2)}, u32[]{:S(2)}) collective-permute-start(f32[2,128]{1,0:T(2,128)S(1)} %pad_maximum_fusion.3), channel_id=1, source_target_pairs={{0,1},{1,2},{2,3},{3,0},{4,5},{5,6},{6,7},{7,4},{8,9},{9,10},{10,1... | collective-permute-start | bytes 3080 | tf_op jit(solution)/shard_map/ppermute | solution.py:50
  17.4 2.6 %collective-permute-start.3 = (f32[2,128]{1,0:T(2,128)S(1)}, f32[2,128]{1,0:T(2,128)S(1)}, u32[]{:S(2)}, u32[]{:S(2)}) collective-permute-start(f32[2,128]{1,0:T(2,128)S(1)} %pad_maximum_fusion.3), channel_id=1, source_target_pairs={{0,2},{1,3},{2,0},{3,1},{4,6},{5,7},{6,4},{7,5},{8,10},{9,11},{10,... | collective-permute-start | bytes 3080 | tf_op jit(solution)/shard_map/ppermute | solution.py:50
  22.3 2.6 %collective-permute-start = (bf16[16,2048]{1,0:T(8,128)(2,1)S(1)}, bf16[16,2048]{1,0:T(8,128)(2,1)S(1)}, u32[]{:S(2)}, u32[]{:S(2)}) collective-permute-start(bf16[16,2048]{1,0:T(8,128)(2,1)S(1)} %get-tuple-element.63), channel_id=1, source_target_pairs={{0,1},{1,2},{2,3},{4,5},{5,6},{6,7},{8,9},{9,10},{10,11},{12,13},{... | collective-permute-start | bytes 196616 | tf_op jit(solution)/shard_map/ppermute | solution.py:214
  30.1 5.7 %fusion = f32[512,1024]{1,0:T(8,128)S(1)} fusion(bf16[512,2048]{1,0:T(8,128)(2,1)} %param.7, bf16[2048,1024]{1,0:T(8,128)(2,1)} %param.8, s32[512]{0:T(512)S(1)} %iota_add_fusion, s32[512]{0:T(512)S(1)} %bitcast.127, s32[512]{0:T(512)S(1)} %bitcast.112), kind=kOutput, calls=%fused_computation.9 | convolution fusion | flops 2685665280 | bytes 8394752 | tf_op jit(solution)/shard_map/dot_general | solution.py:252
  36.2 2.5 %collective-permute-start.5 = (f32[2,512]{1,0:T(2,128)S(1)}, f32[2,512]{1,0:T(2,128)S(1)}, u32[]{:S(2)}, u32[]{:S(2)}) collective-permute-start(f32[2,512]{1,0:T(2,128)S(1)} %bitcast.100), channel_id=1, source_target_pairs={{0,24},{4,28},{8,0},{12,4},{16,8},{20,12},{24,16},{28,20},{1,25},{... | collective-permute-start | bytes 12296 | tf_op jit(solution)/shard_map/ppermute | solution.py:37
  39.3 4.7 %multiply_reduce_fusion = (f32[512]{0:T(512)S(1)}, f32[512,1024]{1,0:T(8,128)}) fusion(f32[512]{0:T(512)S(1)} %bitcast.115, f32[512,1024]{1,0:T(8,128)S(1)} %fusion, bf16[2048,1024]{1,0:T(8,128)(2,1)} %param.8, bf16[16,2048]{1,0:T(8,128)(2,1)S(1)} %collective-permute-done.1, bf16[16,2048]{1,0:T(8,128)(2,1)S(1)} %collective-permute-done, ...), kind=kOutput, calls=%fused_computation.3 | convolution fusion | flops 170212864 | bytes 8528000 | tf_op jit(solution)/shard_map/dot_general | solution.py:252
  51.1 13.7 %collective-permute-done.10 = bf16[128,1024]{1,0:T(8,128)(2,1)} collective-permute-done((bf16[128,1024]{1,0:T(8,128)(2,1)}, bf16[128,1024]{1,0:T(8,128)(2,1)}, u32[]{:S(2)}, u32[]{:S(2)}) %collective-permute-start.10) | collective-permute-done | bytes 262176 | tf_op jit(solution)/shard_map/ppermute | solution.py:72
  64.9 8.5 %collective-permute-done.8 = bf16[128,1024]{1,0:T(8,128)(2,1)} collective-permute-done((bf16[128,1024]{1,0:T(8,128)(2,1)}, bf16[128,1024]{1,0:T(8,128)(2,1)}, u32[]{:S(2)}, u32[]{:S(2)}) %collective-permute-start.8) | collective-permute-done | bytes 262176 | tf_op jit(solution)/shard_map/ppermute | solution.py:72
  73.4 9.8 %collective-permute-done.9 = bf16[128,1024]{1,0:T(8,128)(2,1)} collective-permute-done((bf16[128,1024]{1,0:T(8,128)(2,1)S(1)}, bf16[128,1024]{1,0:T(8,128)(2,1)}, u32[]{:S(2)}, u32[]{:S(2)}) %collective-permute-start.9) | collective-permute-done | bytes 262176 | tf_op jit(solution)/shard_map/ppermute | solution.py:72
  91.4 5.2 %collective-permute-done.11 = bf16[128,1024]{1,0:T(8,128)(2,1)S(1)} collective-permute-done((bf16[128,1024]{1,0:T(8,128)(2,1)S(1)}, bf16[128,1024]{1,0:T(8,128)(2,1)S(1)}, u32[]{:S(2)}, u32[]{:S(2)}) %collective-permute-start.11) | collective-permute-done | bytes 262176 | tf_op jit(solution)/shard_map/ppermute | solution.py:37
  97.8 7.7 %collective-permute-done.13 = bf16[128,1024]{1,0:T(8,128)(2,1)S(1)} collective-permute-done((bf16[128,1024]{1,0:T(8,128)(2,1)S(1)}, bf16[128,1024]{1,0:T(8,128)(2,1)S(1)}, u32[]{:S(2)}, u32[]{:S(2)}) %collective-permute-start.13) | collective-permute-done | bytes 262176 | tf_op jit(solution)/shard_map/ppermute | solution.py:37
  107.5 4.8 %all-gather.5.cloned.1.call-done.s0_ref.student_ref = bf16[512,1024]{1,0:T(8,128)(2,1)} async-done(((bf16[128,1024]{1,0:T(8,128)(2,1)}), bf16[512,1024]{1,0:T(8,128)(2,1)}) %all-gather.5.cloned.1.call-update) | async-done | bytes 1048592 | tf_op jit(solution)/shard_map/all_gather | solution.py:267
  124.5 13.0 %collective-permute-done.14.s1_ref = bf16[512,1024]{1,0:T(8,128)(2,1)} collective-permute-done((bf16[512,1024]{1,0:T(8,128)(2,1)}, bf16[512,1024]{1,0:T(8,128)(2,1)}, u32[]{:S(2)}, u32[]{:S(2)}) %collective-permute-start.14) | collective-permute-done | bytes 1048608 | tf_op jit(solution)/shard_map/ppermute | solution.py:37
  138.8 3.3 %collective-permute-start.20 = (f32[640]{0:T(1024)S(1)}, f32[640]{0:T(1024)S(1)}, u32[]{:S(2)}, u32[]{:S(2)}) collective-permute-start(f32[640]{0:T(1024)S(1)} %concatenate.20), channel_id=1, source_target_pairs={{0,24},{4,28},{8,0},{12,4},{16,8},{20,12},{24,16},{28,20},{1,25},{... | collective-permute-start | bytes 7688 | tf_op jit(solution)/shard_map/ppermute | solution.py:37
  143.5 6.5 %collective-permute-done.19 = f32[640]{0:T(1024)S(1)} collective-permute-done((f32[640]{0:T(1024)S(1)}, f32[640]{0:T(1024)S(1)}, u32[]{:S(2)}, u32[]{:S(2)}) %collective-permute-start.19) | collective-permute-done | bytes 2592 | tf_op jit(solution)/shard_map/ppermute | solution.py:37
  152.7 7.8 %teacher_side.1 = bf16[512,1024]{1,0:T(8,128)(2,1)S(1)} custom-call(bf16[512,1024]{1,0:T(8,128)(2,1)S(1)} %copy-done.3, f32[512,1]{1,0:T(8,128)S(1)} %copy.67.rms_ref, bf16[512,1024]{1,0:T(8,128)(2,1)S(1)} %copy-done.1, bf16[512,1024]{1,0:T(8,128)(2,1)} %collective-permute-done.14.s1_ref, bf16[512,1024]{1,0:T(8,128)(2,1)} %collective-permute-done.22.s2_ref, ...), custom_call_target="tpu_custom_call" | custom-call | flops 4294967296 | bytes 7340032 | tf_op jit(solution)/shard_map/teacher_side/pallas_call | solution.py:99
  164.7 2.8 %fusion.52 = f32[1024,1024]{1,0:T(8,128)S(1)} fusion(bf16[512,1024]{1,0:T(8,128)(2,1)} %collective-permute-done.24, bf16[512,1024]{1,0:T(8,128)(2,1)} %collective-permute-done.25), kind=kOutput, calls=%fused_computation.122 | convolution fusion | flops 1073741824 | bytes 6291456 | tf_op jit(solution)/shard_map/dot_general | solution.py:28
  167.6 3.4 %fusion.50 = (bf16[1024,1024]{1,0:T(8,128)(2,1)S(1)}, f32[1024,1024]{1,0:T(8,128)}) fusion(f32[1024,1024]{1,0:T(8,128)S(1)} %fusion.52, bf16[512,1024]{1,0:T(8,128)(2,1)S(1)} %copy-done.6, bf16[512,1024]{1,0:T(8,128)(2,1)S(1)} %teacher_side.1), kind=kOutput, calls=%fused_computation.120 | convolution fusion | flops 1075838976 | bytes 12582912 | tf_op jit(solution)/shard_map/dot_general | solution.py:28
  171.8 2.5 %collective-permute-start.26 = (bf16[256,1024]{1,0:T(8,128)(2,1)}, bf16[256,1024]{1,0:T(8,128)(2,1)}, u32[]{:S(2)}, u32[]{:S(2)}) collective-permute-start(bf16[256,1024]{1,0:T(8,128)(2,1)} %get-tuple-element.58), channel_id=1, source_target_pairs={{0,8},{4,12},{8,16},{12,20},{16,24},{20,28},{24,0},{28,4},{1,9},{5... | collective-permute-start | bytes 1572872 | tf_op jit(solution)/shard_map/ppermute | solution.py:37
  177.6 20.9 %collective-permute-done.21 = f32[128]{0:T(128)S(1)} collective-permute-done((f32[128]{0:T(128)S(1)}, f32[128]{0:T(128)S(1)}, u32[]{:S(2)}, u32[]{:S(2)}) %collective-permute-start.21) | collective-permute-done | bytes 544 | tf_op jit(solution)/shard_map/ppermute | solution.py:37
  209.8 9.1 %student_side.1 = bf16[512,1024]{1,0:T(8,128)(2,1)S(1)} custom-call(bf16[512,1024]{1,0:T(8,128)(2,1)S(1)} %copy-done.2, f32[512,1024]{1,0:T(8,128)S(1)} %get-tuple-element.57.full_ref, f32[512,9]{1,0:T(8,128)S(1)} %copy.69.scalar_ref, bf16[512,1024]{1,0:T(8,128)(2,1)S(1)} %copy-done.4, bf16[4,384,1024]{2,1,0:T(8,128)(2,1)} %bitcast.133), custom_call_target="tpu_custom_call" | custom-call | flops 4294967296 | bytes 8388608 | tf_op jit(solution)/shard_map/student_side/pallas_call | solution.py:141
  220.4 6.9 %convolution_convert_fusion = bf16[512,2048]{1,0:T(8,128)(2,1)} fusion(bf16[2048,1024]{1,0:T(8,128)(2,1)} %param.8, bf16[512,1024]{1,0:T(8,128)(2,1)} %copy-done.5, s32[512]{0:T(512)S(1)} %iota_add_fusion, s32[512]{0:T(512)S(1)} %bitcast.129, s32[512]{0:T(512)S(1)} %bitcast.114), kind=kOutput, calls=%fused_computation | convolution fusion | flops 2686713856 | bytes 7346176 | tf_op jit(solution)/shard_map/dot_general | solution.py:32
  231.8 6.5 %assemble.1 = f32[2048,1024]{1,0:T(8,128)} custom-call(s32[8]{0:T(128)S(1)} %stack.103.order_ref, bf16[256,1024]{1,0:T(8,128)(2,1)S(1)} %add_convert_fusion.refs_0_, bf16[256,1024]{1,0:T(8,128)(2,1)} %collective-permute-done.29.refs_1_, bf16[256,1024]{1,0:T(8,128)(2,1)} %collective-permute-done.30.refs_2_, ...), custom_call_target="tpu_custom_call" | custom-call | flops 2097152 | bytes 12582912 | tf_op jit(solution)/shard_map/assemble/pallas_call | solution.py:174
  (170 shorter events, 68.5 us)
Async XLA Ops:
  7.2 78.0 %reduce-scatter.2.cloned.1.call-start = ((), (), s32[]{:S(2)}) async-start(), calls=%async_computation.1 | async-start | bytes 2621440 | tf_op jit(solution)/shard_map/reduce_scatter | solution.py:222
  13.7 98.5 %all-gather.5.cloned.1.call-start = ((), (), s32[]{:S(2)}) async-start(), calls=%async_computation.2 | async-start | bytes 1310720 | tf_op jit(solution)/shard_map/all_gather | solution.py:267
  14.4 21.6 %collective-permute-start.2 = (f32[2,128]{1,0:T(2,128)S(1)}, f32[2,128]{1,0:T(2,128)S(1)}, u32[]{:S(2)}, u32[]{:S(2)}) collective-permute-start(f32[2,128]{1,0:T(2,128)S(1)} %pad_maximum_fusion.3), channel_id=1, source_target_pairs={{0,1},{1,2},{2,3},{3,0},{4,5},{5,6},{6,7},{7,4},{8,9},{9,10},{10,1... | collective-permute-start | bytes 3080 | tf_op jit(solution)/shard_map/ppermute | solution.py:50
  17.4 18.6 %collective-permute-start.3 = (f32[2,128]{1,0:T(2,128)S(1)}, f32[2,128]{1,0:T(2,128)S(1)}, u32[]{:S(2)}, u32[]{:S(2)}) collective-permute-start(f32[2,128]{1,0:T(2,128)S(1)} %pad_maximum_fusion.3), channel_id=1, source_target_pairs={{0,2},{1,3},{2,0},{3,1},{4,6},{5,7},{6,4},{7,5},{8,10},{9,11},{10,... | collective-permute-start | bytes 3080 | tf_op jit(solution)/shard_map/ppermute | solution.py:50
  20.0 16.1 %collective-permute-start.4 = (f32[2,128]{1,0:T(2,128)S(1)}, f32[2,128]{1,0:T(2,128)S(1)}, u32[]{:S(2)}, u32[]{:S(2)}) collective-permute-start(f32[2,128]{1,0:T(2,128)S(1)} %pad_maximum_fusion.3), channel_id=1, source_target_pairs={{0,3},{1,0},{2,1},{3,2},{4,7},{5,4},{6,5},{7,6},{8,11},{9,8},{10,9... | collective-permute-start | bytes 3080 | tf_op jit(solution)/shard_map/ppermute | solution.py:50
  22.3 17.0 %collective-permute-start = (bf16[16,2048]{1,0:T(8,128)(2,1)S(1)}, bf16[16,2048]{1,0:T(8,128)(2,1)S(1)}, u32[]{:S(2)}, u32[]{:S(2)}) collective-permute-start(bf16[16,2048]{1,0:T(8,128)(2,1)S(1)} %get-tuple-element.63), channel_id=1, source_target_pairs={{0,1},{1,2},{2,3},{4,5},{5,6},{6,7},{8,9},{9,10},{10,11},{12,13},{... | collective-permute-start | bytes 196616 | tf_op jit(solution)/shard_map/ppermute | solution.py:214
  24.9 14.4 %collective-permute-start.1 = (bf16[16,2048]{1,0:T(8,128)(2,1)S(1)}, bf16[16,2048]{1,0:T(8,128)(2,1)S(1)}, u32[]{:S(2)}, u32[]{:S(2)}) collective-permute-start(bf16[16,2048]{1,0:T(8,128)(2,1)S(1)} %get-tuple-element.64), channel_id=1, source_target_pairs={{1,0},{2,1},{3,2},{5,4},{6,5},{7,6},{9,8},{10,9},{11,10},{13,12},{... | collective-permute-start | bytes 196616 | tf_op jit(solution)/shard_map/ppermute | solution.py:215
  46.8 18.1 %collective-permute-start.10 = (bf16[128,1024]{1,0:T(8,128)(2,1)}, bf16[128,1024]{1,0:T(8,128)(2,1)}, u32[]{:S(2)}, u32[]{:S(2)}) collective-permute-start(bf16[128,1024]{1,0:T(8,128)(2,1)} %get-tuple-element.66), channel_id=1, source_target_pairs={{0,3},{1,0},{2,1},{3,2},{4,7},{5,4},{6,5},{7,6},{8,11},{9,8},{10,9... | collective-permute-start | bytes 786440 | tf_op jit(solution)/shard_map/ppermute | solution.py:72
  49.2 24.2 %collective-permute-start.8 = (bf16[128,1024]{1,0:T(8,128)(2,1)}, bf16[128,1024]{1,0:T(8,128)(2,1)}, u32[]{:S(2)}, u32[]{:S(2)}) collective-permute-start(bf16[128,1024]{1,0:T(8,128)(2,1)} %get-tuple-element.65), channel_id=1, source_target_pairs={{0,1},{1,2},{2,3},{3,0},{4,5},{5,6},{6,7},{7,4},{8,9},{9,10},{10,1... | collective-permute-start | bytes 786440 | tf_op jit(solution)/shard_map/ppermute | solution.py:72
  49.5 33.7 %collective-permute-start.9 = (bf16[128,1024]{1,0:T(8,128)(2,1)S(1)}, bf16[128,1024]{1,0:T(8,128)(2,1)}, u32[]{:S(2)}, u32[]{:S(2)}) collective-permute-start(bf16[128,1024]{1,0:T(8,128)(2,1)S(1)} %get-tuple-element.67), channel_id=1, source_target_pairs={{0,2},{1,3},{2,0},{3,1},{4,6},{5,7},{6,4},{7,5},{8,10},{9,11},{10,... | collective-permute-start | bytes 786440 | tf_op jit(solution)/shard_map/ppermute | solution.py:72
  85.2 64.9 %all-gather.7.cloned.1.call-start = ((), (), s32[]{:S(2)}) async-start(), calls=%async_computation.3 | async-start | bytes 1310720 | tf_op jit(solution)/shard_map/all_gather | solution.py:276
  89.1 16.4 %collective-permute-start.13 = (bf16[128,1024]{1,0:T(8,128)(2,1)S(1)}, bf16[128,1024]{1,0:T(8,128)(2,1)S(1)}, u32[]{:S(2)}, u32[]{:S(2)}) collective-permute-start(bf16[128,1024]{1,0:T(8,128)(2,1)S(1)} %multiply_convert_fusion), channel_id=1, source_target_pairs={{0,12},{4,16},{8,20},{12,24},{16,28},{20,0},{24,4},{28,8},{1,13},{... | collective-permute-start | bytes 786440 | tf_op jit(solution)/shard_map/ppermute | solution.py:37
  112.3 95.1 %all-gather.9.cloned.1.call-start = ((), (), s32[]{:S(2)}) async-start(), calls=%async_computation.4 | async-start | bytes 3932160 | tf_op jit(solution)/shard_map/all_gather | solution.py:311
  112.4 25.1 %collective-permute-start.14 = (bf16[512,1024]{1,0:T(8,128)(2,1)}, bf16[512,1024]{1,0:T(8,128)(2,1)}, u32[]{:S(2)}, u32[]{:S(2)}) collective-permute-start(bf16[512,1024]{1,0:T(8,128)(2,1)} %all-gather.5.cloned.1.call-done.s0_ref.student_ref), channel_id=1, source_target_pairs={{0,24},{4,28},{8,0},{12,4},{16,8},{20,12},{24,16},{28,20},{1,25},{... | collective-permute-start | bytes 3145736 | tf_op jit(solution)/shard_map/ppermute | solution.py:37
  137.6 12.5 %collective-permute-start.22 = (bf16[512,1024]{1,0:T(8,128)(2,1)S(1)}, bf16[512,1024]{1,0:T(8,128)(2,1)}, u32[]{:S(2)}, u32[]{:S(2)}) collective-permute-start(bf16[512,1024]{1,0:T(8,128)(2,1)S(1)} %copy-done), channel_id=1, source_target_pairs={{0,20},{4,0},{8,28},{12,8},{16,4},{20,16},{24,12},{28,24},{1,21},{... | collective-permute-start | bytes 3145736 | tf_op jit(solution)/shard_map/ppermute | solution.py:37
  143.4 18.9 %collective-permute-start.24 = (bf16[512,1024]{1,0:T(8,128)(2,1)}, bf16[512,1024]{1,0:T(8,128)(2,1)}, u32[]{:S(2)}, u32[]{:S(2)}) collective-permute-start(bf16[512,1024]{1,0:T(8,128)(2,1)} %get-tuple-element.61), channel_id=1, source_target_pairs={{0,4},{4,0},{8,12},{12,8},{16,20},{20,16},{24,28},{28,24},{1,5},{5... | collective-permute-start | bytes 3145736 | tf_op jit(solution)/shard_map/ppermute | solution.py:37
  171.8 29.8 %collective-permute-start.26 = (bf16[256,1024]{1,0:T(8,128)(2,1)}, bf16[256,1024]{1,0:T(8,128)(2,1)}, u32[]{:S(2)}, u32[]{:S(2)}) collective-permute-start(bf16[256,1024]{1,0:T(8,128)(2,1)} %get-tuple-element.58), channel_id=1, source_target_pairs={{0,8},{4,12},{8,16},{12,20},{16,24},{20,28},{24,0},{28,4},{1,9},{5... | collective-permute-start | bytes 1572872 | tf_op jit(solution)/shard_map/ppermute | solution.py:37
  174.3 27.3 %collective-permute-start.27 = (bf16[256,1024]{1,0:T(8,128)(2,1)S(1)}, bf16[256,1024]{1,0:T(8,128)(2,1)}, u32[]{:S(2)}, u32[]{:S(2)}) collective-permute-start(bf16[256,1024]{1,0:T(8,128)(2,1)S(1)} %get-tuple-element.60), channel_id=1, source_target_pairs={{0,16},{4,20},{8,24},{12,28},{16,0},{20,4},{24,8},{28,12},{1,17},{... | collective-permute-start | bytes 1572872 | tf_op jit(solution)/shard_map/ppermute | solution.py:37
  175.0 26.7 %collective-permute-start.28 = (bf16[256,1024]{1,0:T(8,128)(2,1)S(1)}, bf16[256,1024]{1,0:T(8,128)(2,1)}, u32[]{:S(2)}, u32[]{:S(2)}) collective-permute-start(bf16[256,1024]{1,0:T(8,128)(2,1)S(1)} %get-tuple-element.59), channel_id=1, source_target_pairs={{0,24},{4,28},{8,0},{12,4},{16,8},{20,12},{24,16},{28,20},{1,25},{... | collective-permute-start | bytes 1572872 | tf_op jit(solution)/shard_map/ppermute | solution.py:37
  176.5 22.0 %collective-permute-start.21 = (f32[128]{0:T(128)S(1)}, f32[128]{0:T(128)S(1)}, u32[]{:S(2)}, u32[]{:S(2)}) collective-permute-start(f32[128]{0:T(128)S(1)} %compare_select_fusion.10), channel_id=1, source_target_pairs={{0,16},{4,20},{8,24},{12,28},{16,0},{20,4},{24,8},{28,12},{1,17},{... | collective-permute-start | bytes 1544 | tf_op jit(solution)/shard_map/ppermute | solution.py:37
  203.7 16.2 %collective-permute-start.34 = (bf16[256,1024]{1,0:T(8,128)(2,1)S(1)}, bf16[256,1024]{1,0:T(8,128)(2,1)S(1)}, u32[]{:S(2)}, u32[]{:S(2)}) collective-permute-start(bf16[256,1024]{1,0:T(8,128)(2,1)S(1)} %add_convert_fusion.refs_0_), channel_id=1, source_target_pairs={{0,24},{4,28},{8,0},{12,4},{16,8},{20,12},{24,16},{28,20},{1,25},{... | collective-permute-start | bytes 1572872 | tf_op jit(solution)/shard_map/ppermute | solution.py:37
  204.0 23.3 %collective-permute-start.32 = (bf16[256,1024]{1,0:T(8,128)(2,1)S(1)}, bf16[256,1024]{1,0:T(8,128)(2,1)}, u32[]{:S(2)}, u32[]{:S(2)}) collective-permute-start(bf16[256,1024]{1,0:T(8,128)(2,1)S(1)} %add_convert_fusion.refs_0_), channel_id=1, source_target_pairs={{0,16},{4,20},{8,24},{12,28},{16,0},{20,4},{24,8},{28,12},{1,17},{... | collective-permute-start | bytes 1572872 | tf_op jit(solution)/shard_map/ppermute | solution.py:37
  205.4 24.3 %collective-permute-start.30 = (bf16[256,1024]{1,0:T(8,128)(2,1)S(1)}, bf16[256,1024]{1,0:T(8,128)(2,1)}, u32[]{:S(2)}, u32[]{:S(2)}) collective-permute-start(bf16[256,1024]{1,0:T(8,128)(2,1)S(1)} %add_convert_fusion.refs_0_), channel_id=1, source_target_pairs={{0,8},{4,12},{8,16},{12,20},{16,24},{20,28},{24,0},{28,4},{1,9},{5... | collective-permute-start | bytes 1572872 | tf_op jit(solution)/shard_map/ppermute | solution.py:37
  207.4 23.1 %collective-permute-start.29 = (bf16[256,1024]{1,0:T(8,128)(2,1)S(1)}, bf16[256,1024]{1,0:T(8,128)(2,1)}, u32[]{:S(2)}, u32[]{:S(2)}) collective-permute-start(bf16[256,1024]{1,0:T(8,128)(2,1)S(1)} %add_convert_fusion.refs_0_), channel_id=1, source_target_pairs={{0,4},{4,0},{8,12},{12,8},{16,20},{20,16},{24,28},{28,24},{1,5},{5... | collective-permute-start | bytes 1572872 | tf_op jit(solution)/shard_map/ppermute | solution.py:37
  (28 other events, 197.6 us)
Sparse Core Ops, SparseCore 0:
  13.8 56.6 reduce-scatter.1
  85.3 26.9 all-gather.4
  113.9 27.8 all-gather.6
  143.3 62.5 all-gather.8

commit v4 on v3

--- a/solution.py
+++ b/solution.py
@@ -255,14 +255,7 @@
     student_full, student_rms = normalize(pooled / lengths_f)
     begins_here = (starts >= first) & (starts < last)
     student_sparse = jnp.where(begins_here[:, None], student_full, 0.0).astype(BF16)
-    student_sparse, small, ahead_small, mixed_small, other_small, own_half = (
-        lax.optimization_barrier(
-            (student_sparse, small, ahead_small, mixed_small, other_small, own_half)
-        )
-    )
     student_shard = scatter_narrow(student_sparse, span_dev)
-    factor, positive = small[0], small[1]
-    window_small = [small, ahead_small, mixed_small, other_small]
     student_shard, teacher_proj = lax.optimization_barrier((student_shard, teacher_proj))
     student = lax.all_gather(student_shard, "narrow", axis=0, tiled=True)
 
@@ -272,7 +265,11 @@
         [permute_blk(teacher, lambda i, k=k: i + k) for k in range(1, STOPS)], axis=0
     )
     keys = jnp.concatenate([teacher, others], axis=0)
-    teacher, student, keys, others = lax.optimization_barrier((teacher, student, keys, others))
+    window_small = [small, ahead_small, mixed_small, other_small]
+    teacher, student, keys, others, own_half, *window_small = lax.optimization_barrier(
+        (teacher, student, keys, others, own_half, *window_small)
+    )
+    factor, positive = window_small[0][0], window_small[0][1]
     teacher_block = lax.all_gather(teacher, "narrow", axis=0, tiled=True)
 
     ahead, mixed = following(student)
@@ -292,38 +289,38 @@
     top = jnp.max(stats[:, 0], axis=0)
     log_total = top + jnp.log(jnp.sum(stats[:, 1] * jnp.exp(stats[:, 0] - top), axis=0))
     loss = jnp.sum(log_total - jnp.sum(stats[:, 2], axis=0))
-    ahead, log_total = lax.optimization_barrier((ahead, log_total))
-    student_window = [student, ahead, mixed, sibling(ahead)]
     note = jnp.concatenate([log_total, jnp.broadcast_to(loss, (128,))])
     notes = [note, *following(note), following_other(note)]
+    ahead, *notes = lax.optimization_barrier((ahead, *notes))
+    student_window = [student, ahead, mixed, sibling(ahead)]
     window_log_total = [x[:span_block] for x in notes]
 
+    others, log_total = lax.optimization_barrier((others, log_total))
+    others = lax.all_gather(others, "narrow", axis=0)
+
+    small = jnp.stack(
+        [x[0] for x in window_small]
+        + window_log_total
+        + [x[1] - (stop * span_block).astype(F32) for x, stop in zip(window_small, window_stops)]
+    )
+    teacher_grads = teacher_grads_of(teacher_block, block_rms, student_window, small)
+    sibling_grads = sibling(teacher_grads)
+
+    weight_part = contract_first(own_half, teacher_grads)
+    weight_part, sibling_grads = lax.optimization_barrier((weight_part, sibling_grads))
+    weight_part = weight_part + contract_first(sibling_half, sibling_grads)
+    slice_rows = half // chips
+    narrowed = weight_part.astype(BF16)
+    total = lax.dynamic_slice_in_dim(weight_part, chip * slice_rows, slice_rows, 0)
     spots = jnp.arange(128, dtype=jnp.int32)
     terms = jnp.zeros((128,), F32)
     for x, stop in zip(notes, window_stops):
         terms = jnp.where(spots == lax.rem(block + stop, blocks), x[span_block:], terms)
-    own_terms = terms
+    own_terms, total = lax.optimization_barrier((terms, total))
     for by in range(4, blocks, 4):
         terms = terms + permute_blk(own_terms, lambda i, by=by: i - by)
     loss_mean = jnp.sum(terms) / (span_block * blocks)
 
-    others, log_total = lax.optimization_barrier((others, log_total))
-    others = lax.all_gather(others, "narrow", axis=0)
-
-    small = jnp.stack(
-        [x[0] for x in window_small]
-        + window_log_total
-        + [x[1] - (stop * span_block).astype(F32) for x, stop in zip(window_small, window_stops)]
-    )
-    teacher_grads = teacher_grads_of(teacher_block, block_rms, student_window, small)
-    sibling_grads = sibling(teacher_grads)
-
-    weight_part = contract_first(own_half, teacher_grads) + contract_first(
-        sibling_half, sibling_grads
-    )
-    slice_rows = half // chips
-    narrowed = weight_part.astype(BF16)
-    total = lax.dynamic_slice_in_dim(weight_part, chip * slice_rows, slice_rows, 0)
     came = []
     for by in range(1, chips):
         target = lax.rem(chip + by, chips)

time: 247 us -> 243 us (0.984)
  waiting for transfers between devices: 99.7 us -> 89.7 us
  starting transfers between devices: 44.6 us -> 47.1 us
    ppermute x25, waiting for transfers between devices: 61.7 us -> 41.2 us  [permute_blk(): lax.ppermute(x, 'blk', [(i, target(i) % count) for i in range(count)])]
    ppermute x3, waiting for transfers between devices: 32 us -> 37.5 us  [scatter_narrow(): lax.ppermute(piece, 'narrow', [(i, (i + by) % count) for i in range(count)])]
    ppermute x6, starting transfers between devices: 11.9 us -> 8.05 us  [gather_narrow(): lax.ppermute(x, 'narrow', [(i, (i + by) % count) for i in range(count)])]
    ppermute x1, starting transfers between devices: 2.58 us -> 5.56 us  [shards(): lax.ppermute(student_bytes[-MOST_BYTES:], 'narrow', [(i, i + 1) for i in...]
    ppermute x25, starting transfers between devices: 24.3 us -> 27.1 us  [permute_blk(): lax.ppermute(x, 'blk', [(i, target(i) % count) for i in range(count)])]
    ppermute x6, waiting for transfers between devices: 1.1 us -> 3.68 us  [gather_narrow(): lax.ppermute(x, 'narrow', [(i, (i + by) % count) for i in range(count)])]
    unnamed x26 -> x22, local copies, waits for them, and re-layouts: 7.13 us -> 6.41 us
  transfers between devices with their start and end apart: 40 -> 40, of which waited for: 16 -> 20; matrix products, arithmetic and copies ran while one was open for 19% -> 21% of each run, Pallas kernels for 7% -> 7%
where the time goes in v4:
time: 243 us; the launch traced here: 242 us
  waiting for transfers between devices  89.7 us (37%)
  starting transfers between devices  47.1 us (19%)
  matrix products  33.5 us (14%)
  Pallas kernels  23.4 us (10%)
  between operations  17.3 us (7%)
  local copies, waits for them, and re-layouts  16.2 us (7%)
  other arithmetic  14.5 us (6%)
    ppermute x25, waiting for transfers between devices, permute_blk(): lax.ppermute(x, 'blk', [(i, target(i) % count) for i in range(count)])  41.2 us
    ppermute x3, waiting for transfers between devices, scatter_narrow(): lax.ppermute(piece, 'narrow', [(i, (i + by) % count) for i in range(count)])  37.5 us
    ppermute x25, starting transfers between devices, permute_blk(): lax.ppermute(x, 'blk', [(i, target(i) % count) for i in range(count)])  27.1 us
    dot_general x2, matrix products, contract_last(): lax.dot_general(left, right, (((1,), (1,)), ((), ())), preferred_element_...  9.24 us
    pallas_call x1, Pallas kernels, span_grads_of(): pl.pallas_call(student_side, grid=(span_block // rows,), in_specs=[part,...  9.1 us
    ppermute x6, starting transfers between devices, gather_narrow(): lax.ppermute(x, 'narrow', [(i, (i + by) % count) for i in range(count)])  8.05 us
    pallas_call x1, Pallas kernels, teacher_grads_of(): pl.pallas_call(functools.partial(teacher_side, rows), grid=(span_block //...  7.79 us
    dot_general x1, matrix products, shards(): jnp.dot(span_table, projected, preferred_element_type=F32)  7.03 us
  transfers between devices with their start and end apart: 40, of which 20 were waited for; matrix products, arithmetic and copies ran while one was open for 21% of the time, Pallas kernels for 7%

profile of v4, /device:TPU:0, one launch (start us, length us, event | category | flops | bytes accessed | tf_op | source)
XLA Modules:
  0.0 241.7 jit_solution(7158297747602512927)
XLA Ops:
  7.2 6.5 %fusion.51 = f32[512,1024]{1,0:T(8,128)} fusion(bf16[512,2048]{1,0:T(8,128)(2,1)} %param.9, bf16[2048,1024]{1,0:T(8,128)(2,1)} %param.10), kind=kOutput, calls=%fused_computation.121 | convolution fusion | flops 2147483648 | bytes 8388608 | tf_op jit(solution)/shard_map/dot_general | solution.py:220
  15.9 5.6 %collective-permute-start = (bf16[16,2048]{1,0:T(8,128)(2,1)S(1)}, bf16[16,2048]{1,0:T(8,128)(2,1)S(1)}, u32[]{:S(2)}, u32[]{:S(2)}) collective-permute-start(bf16[16,2048]{1,0:T(8,128)(2,1)S(1)} %get-tuple-element.77), channel_id=1, source_target_pairs={{0,1},{1,2},{2,3},{4,5},{5,6},{6,7},{8,9},{9,10},{10,11},{12,13},{... | collective-permute-start | bytes 196616 | tf_op jit(solution)/shard_map/ppermute | solution.py:214
  24.0 7.0 %fusion = f32[512,1024]{1,0:T(8,128)} fusion(bf16[512,2048]{1,0:T(8,128)(2,1)} %param.7, bf16[2048,1024]{1,0:T(8,128)(2,1)} %param.8, s32[512]{0:T(512)S(1)} %iota_add_fusion, s32[512]{0:T(512)S(1)} %bitcast.127, s32[512]{0:T(512)S(1)} %bitcast.111), kind=kOutput, calls=%fused_computation.8 | convolution fusion | flops 2685665280 | bytes 8394752 | tf_op jit(solution)/shard_map/dot_general | solution.py:252
  31.1 5.4 %multiply_reduce_fusion = (f32[512]{0:T(512)S(1)}, f32[512,1024]{1,0:T(8,128)}) fusion(f32[512]{0:T(512)S(1)} %bitcast.114, f32[512,1024]{1,0:T(8,128)} %fusion, bf16[2048,1024]{1,0:T(8,128)(2,1)} %param.8, bf16[16,2048]{1,0:T(8,128)(2,1)S(1)} %collective-permute-done.1, bf16[16,2048]{1,0:T(8,128)(2,1)S(1)} %collective-permute-done, s32[32]{0:T(128)S(1)} %pad_add_fusion, ...), kind=kOutput, calls=%fused_computation.2 | convolution fusion | flops 170212864 | bytes 8528000 | tf_op jit(solution)/shard_map/dot_general | solution.py:252
  39.3 2.0 collective-permute-start.4
  44.3 14.1 %collective-permute-done.4 = bf16[128,1024]{1,0:T(8,128)(2,1)} collective-permute-done((bf16[128,1024]{1,0:T(8,128)(2,1)}, bf16[128,1024]{1,0:T(8,128)(2,1)}, u32[]{:S(2)}, u32[]{:S(2)}) %collective-permute-start.4) | collective-permute-done | bytes 262176 | tf_op jit(solution)/shard_map/ppermute | solution.py:72
  58.4 23.4 %collective-permute-done.3 = bf16[128,1024]{1,0:T(8,128)(2,1)} collective-permute-done((bf16[128,1024]{1,0:T(8,128)(2,1)}, bf16[128,1024]{1,0:T(8,128)(2,1)}, u32[]{:S(2)}, u32[]{:S(2)}) %collective-permute-start.3) | collective-permute-done | bytes 262176 | tf_op jit(solution)/shard_map/ppermute | solution.py:72
  90.3 3.1 %constant_dynamic-slice_fusion.4 = (bf16[512,1024]{1,0:T(8,128)(2,1)}, bf16[512,1024]{1,0:T(8,128)(2,1)}) fusion(bf16[512,2048]{1,0:T(8,128)(2,1)} %param.9, s32[]{:T(128)S(6)} %select_n.260, s32[]{:T(128)S(6)} %select_n.248), kind=kLoop, calls=%fused_computation.73 | loop fusion | bytes 4194312 | tf_op jit(solution)/shard_map/dynamic_slice | solution.py:209
  99.7 3.6 %collective-permute-done.7 = bf16[128,1024]{1,0:T(8,128)(2,1)S(1)} collective-permute-done((bf16[128,1024]{1,0:T(8,128)(2,1)S(1)}, bf16[128,1024]{1,0:T(8,128)(2,1)S(1)}, u32[]{:S(2)}, u32[]{:S(2)}) %collective-permute-start.7) | collective-permute-done | bytes 262176 | tf_op jit(solution)/shard_map/ppermute | solution.py:37
  106.3 4.4 %all-gather.5.cloned.1.call-done.s0_ref.student_ref = bf16[512,1024]{1,0:T(8,128)(2,1)} async-done(((bf16[128,1024]{1,0:T(8,128)(2,1)}), bf16[512,1024]{1,0:T(8,128)(2,1)}) %all-gather.5.cloned.1.call-update) | async-done | bytes 1048592 | tf_op jit(solution)/shard_map/all_gather | solution.py:260
  110.8 2.4 collective-permute-start.14
  113.2 2.4 fusion.50
  118.4 2.4 collective-permute-start.17
  126.8 9.2 %collective-permute-done.18 = f32[640]{0:T(1024)S(1)} collective-permute-done((f32[640]{0:T(1024)S(1)}, f32[640]{0:T(1024)S(1)}, u32[]{:S(2)}, u32[]{:S(2)}) %collective-permute-start.18) | collective-permute-done | bytes 2592 | tf_op jit(solution)/shard_map/ppermute | solution.py:37
  136.6 2.6 %collective-permute-done.21.s2_ref = bf16[512,1024]{1,0:T(8,128)(2,1)} collective-permute-done((bf16[512,1024]{1,0:T(8,128)(2,1)S(1)}, bf16[512,1024]{1,0:T(8,128)(2,1)}, u32[]{:S(2)}, u32[]{:S(2)}) %collective-permute-start.21) | collective-permute-done | bytes 1048608 | tf_op jit(solution)/shard_map/ppermute | solution.py:37
  142.7 7.8 %teacher_side.1 = bf16[512,1024]{1,0:T(8,128)(2,1)S(1)} custom-call(bf16[512,1024]{1,0:T(8,128)(2,1)S(1)} %copy-done.3, f32[512,1]{1,0:T(8,128)S(1)} %copy.67.rms_ref, bf16[512,1024]{1,0:T(8,128)(2,1)S(1)} %copy-done.1, bf16[512,1024]{1,0:T(8,128)(2,1)} %collective-permute-done.14.s1_ref, bf16[512,1024]{1,0:T(8,128)(2,1)} %collective-permute-done.21.s2_ref, ...), custom_call_target="tpu_custom_call" | custom-call | flops 4294967296 | bytes 7340032 | tf_op jit(solution)/shard_map/teacher_side/pallas_call | solution.py:99
  151.1 2.5 %fusion.52 = f32[1024,1024]{1,0:T(8,128)S(1)} fusion(bf16[512,1024]{1,0:T(8,128)(2,1)} %get-tuple-element.41, bf16[512,1024]{1,0:T(8,128)(2,1)S(1)} %teacher_side.1), kind=kOutput, calls=%fused_computation.122 | convolution fusion | flops 1073741824 | bytes 6291456 | tf_op jit(solution)/shard_map/dot_general | solution.py:28
  155.1 2.8 %fusion.53 = f32[1024,1024]{1,0:T(8,128)S(1)} fusion(bf16[512,1024]{1,0:T(8,128)(2,1)} %collective-permute-done.24, bf16[512,1024]{1,0:T(8,128)(2,1)} %collective-permute-done.23), kind=kOutput, calls=%fused_computation.123 | convolution fusion | flops 1073741824 | bytes 6291456 | tf_op jit(solution)/shard_map/dot_general | solution.py:28
  160.3 10.0 %collective-permute-start.28 = (bf16[256,1024]{1,0:T(8,128)(2,1)}, bf16[256,1024]{1,0:T(8,128)(2,1)}, u32[]{:S(2)}, u32[]{:S(2)}) collective-permute-start(bf16[256,1024]{1,0:T(8,128)(2,1)} %get-tuple-element.73), channel_id=1, source_target_pairs={{0,24},{4,28},{8,0},{12,4},{16,8},{20,12},{24,16},{28,20},{1,25},{... | collective-permute-start | bytes 1572872 | tf_op jit(solution)/shard_map/ppermute | solution.py:37
  174.9 20.8 %collective-permute-done.25 = f32[128]{0:T(128)S(1)} collective-permute-done((f32[128]{0:T(128)S(1)}, f32[128]{0:T(128)S(1)}, u32[]{:S(2)}, u32[]{:S(2)}) %collective-permute-start.25) | collective-permute-done | bytes 544 | tf_op jit(solution)/shard_map/ppermute | solution.py:37
  199.9 2.7 %collective-permute-start.34 = (bf16[256,1024]{1,0:T(8,128)(2,1)S(1)}, bf16[256,1024]{1,0:T(8,128)(2,1)}, u32[]{:S(2)}, u32[]{:S(2)}) collective-permute-start(bf16[256,1024]{1,0:T(8,128)(2,1)S(1)} %add_convert_fusion.refs_0_), channel_id=1, source_target_pairs={{0,24},{4,28},{8,0},{12,4},{16,8},{20,12},{24,16},{28,20},{1,25},{... | collective-permute-start | bytes 1572872 | tf_op jit(solution)/shard_map/ppermute | solution.py:37
  206.8 9.1 %student_side.1 = bf16[512,1024]{1,0:T(8,128)(2,1)S(1)} custom-call(bf16[512,1024]{1,0:T(8,128)(2,1)S(1)} %copy-done.2, f32[512,1024]{1,0:T(8,128)S(1)} %get-tuple-element.71.full_ref, f32[512,9]{1,0:T(8,128)S(1)} %copy.69.scalar_ref, bf16[512,1024]{1,0:T(8,128)(2,1)S(1)} %copy-done.4, bf16[4,384,1024]{2,1,0:T(8,128)(2,1)} %bitcast.133), custom_call_target="tpu_custom_call" | custom-call | flops 4294967296 | bytes 8388608 | tf_op jit(solution)/shard_map/student_side/pallas_call | solution.py:141
  216.9 6.9 %convolution_convert_fusion = bf16[512,2048]{1,0:T(8,128)(2,1)} fusion(bf16[2048,1024]{1,0:T(8,128)(2,1)} %param.8, bf16[512,1024]{1,0:T(8,128)(2,1)} %copy-done.5, s32[512]{0:T(512)S(1)} %iota_add_fusion, s32[512]{0:T(512)S(1)} %bitcast.129, s32[512]{0:T(512)S(1)} %bitcast.113), kind=kOutput, calls=%fused_computation | convolution fusion | flops 2686713856 | bytes 7346176 | tf_op jit(solution)/shard_map/dot_general | solution.py:32
  227.6 6.5 %assemble.1 = f32[2048,1024]{1,0:T(8,128)} custom-call(s32[8]{0:T(128)S(1)} %stack.103.order_ref, bf16[256,1024]{1,0:T(8,128)(2,1)S(1)} %add_convert_fusion.refs_0_, bf16[256,1024]{1,0:T(8,128)(2,1)S(1)} %collective-permute-done.29.refs_1_, bf16[256,1024]{1,0:T(8,128)(2,1)} %collective-permute-done.30.refs_2_, ...), custom_call_target="tpu_custom_call" | custom-call | flops 2097152 | bytes 12582912 | tf_op jit(solution)/shard_map/assemble/pallas_call | solution.py:174
  (169 shorter events, 61.3 us)
Async XLA Ops:
  7.2 76.6 %reduce-scatter.2.cloned.1.call-start = ((), (), s32[]{:S(2)}) async-start(), calls=%async_computation.1 | async-start | bytes 2621440 | tf_op jit(solution)/shard_map/reduce_scatter | solution.py:222
  13.7 97.0 %all-gather.5.cloned.1.call-start = ((), (), s32[]{:S(2)}) async-start(), calls=%async_computation.2 | async-start | bytes 1310720 | tf_op jit(solution)/shard_map/all_gather | solution.py:260
  14.6 16.4 %collective-permute-start.1 = (bf16[16,2048]{1,0:T(8,128)(2,1)S(1)}, bf16[16,2048]{1,0:T(8,128)(2,1)S(1)}, u32[]{:S(2)}, u32[]{:S(2)}) collective-permute-start(bf16[16,2048]{1,0:T(8,128)(2,1)S(1)} %get-tuple-element.78), channel_id=1, source_target_pairs={{1,0},{2,1},{3,2},{5,4},{6,5},{7,6},{9,8},{10,9},{11,10},{13,12},{... | collective-permute-start | bytes 196616 | tf_op jit(solution)/shard_map/ppermute | solution.py:215
  15.9 15.1 %collective-permute-start = (bf16[16,2048]{1,0:T(8,128)(2,1)S(1)}, bf16[16,2048]{1,0:T(8,128)(2,1)S(1)}, u32[]{:S(2)}, u32[]{:S(2)}) collective-permute-start(bf16[16,2048]{1,0:T(8,128)(2,1)S(1)} %get-tuple-element.77), channel_id=1, source_target_pairs={{0,1},{1,2},{2,3},{4,5},{5,6},{6,7},{8,9},{9,10},{10,11},{12,13},{... | collective-permute-start | bytes 196616 | tf_op jit(solution)/shard_map/ppermute | solution.py:214
  39.3 19.1 %collective-permute-start.4 = (bf16[128,1024]{1,0:T(8,128)(2,1)}, bf16[128,1024]{1,0:T(8,128)(2,1)}, u32[]{:S(2)}, u32[]{:S(2)}) collective-permute-start(bf16[128,1024]{1,0:T(8,128)(2,1)} %get-tuple-element.80), channel_id=1, source_target_pairs={{0,3},{1,0},{2,1},{3,2},{4,7},{5,4},{6,5},{7,6},{8,11},{9,8},{10,9... | collective-permute-start | bytes 786440 | tf_op jit(solution)/shard_map/ppermute | solution.py:72
  41.3 40.5 %collective-permute-start.3 = (bf16[128,1024]{1,0:T(8,128)(2,1)}, bf16[128,1024]{1,0:T(8,128)(2,1)}, u32[]{:S(2)}, u32[]{:S(2)}) collective-permute-start(bf16[128,1024]{1,0:T(8,128)(2,1)} %get-tuple-element.81), channel_id=1, source_target_pairs={{0,2},{1,3},{2,0},{3,1},{4,6},{5,7},{6,4},{7,5},{8,10},{9,11},{10,... | collective-permute-start | bytes 786440 | tf_op jit(solution)/shard_map/ppermute | solution.py:72
  42.7 39.1 %collective-permute-start.2 = (bf16[128,1024]{1,0:T(8,128)(2,1)S(1)}, bf16[128,1024]{1,0:T(8,128)(2,1)}, u32[]{:S(2)}, u32[]{:S(2)}) collective-permute-start(bf16[128,1024]{1,0:T(8,128)(2,1)S(1)} %get-tuple-element.79), channel_id=1, source_target_pairs={{0,1},{1,2},{2,3},{3,0},{4,5},{5,6},{6,7},{7,4},{8,9},{9,10},{10,1... | collective-permute-start | bytes 786440 | tf_op jit(solution)/shard_map/ppermute | solution.py:72
  83.8 56.5 %all-gather.7.cloned.1.call-start = ((), (), s32[]{:S(2)}) async-start(), calls=%async_computation.3 | async-start | bytes 1310720 | tf_op jit(solution)/shard_map/all_gather | solution.py:273
  86.2 17.1 %collective-permute-start.7 = (bf16[128,1024]{1,0:T(8,128)(2,1)S(1)}, bf16[128,1024]{1,0:T(8,128)(2,1)S(1)}, u32[]{:S(2)}, u32[]{:S(2)}) collective-permute-start(bf16[128,1024]{1,0:T(8,128)(2,1)S(1)} %multiply_convert_fusion), channel_id=1, source_target_pairs={{0,12},{4,16},{8,20},{12,24},{16,28},{20,0},{24,4},{28,8},{1,13},{... | collective-permute-start | bytes 786440 | tf_op jit(solution)/shard_map/ppermute | solution.py:37
  87.2 16.1 %collective-permute-start.6 = (bf16[128,1024]{1,0:T(8,128)(2,1)S(1)}, bf16[128,1024]{1,0:T(8,128)(2,1)S(1)}, u32[]{:S(2)}, u32[]{:S(2)}) collective-permute-start(bf16[128,1024]{1,0:T(8,128)(2,1)S(1)} %multiply_convert_fusion), channel_id=1, source_target_pairs={{0,8},{4,12},{8,16},{12,20},{16,24},{20,28},{24,0},{28,4},{1,9},{5... | collective-permute-start | bytes 786440 | tf_op jit(solution)/shard_map/ppermute | solution.py:37
  88.7 14.6 %collective-permute-start.5 = (bf16[128,1024]{1,0:T(8,128)(2,1)S(1)}, bf16[128,1024]{1,0:T(8,128)(2,1)S(1)}, u32[]{:S(2)}, u32[]{:S(2)}) collective-permute-start(bf16[128,1024]{1,0:T(8,128)(2,1)S(1)} %multiply_convert_fusion), channel_id=1, source_target_pairs={{0,4},{4,8},{8,12},{12,16},{16,20},{20,24},{24,28},{28,0},{1,5},{5... | collective-permute-start | bytes 786440 | tf_op jit(solution)/shard_map/ppermute | solution.py:37
  110.8 93.6 %all-gather.9.cloned.1.call-start = ((), (), s32[]{:S(2)}) async-start(), calls=%async_computation.4 | async-start | bytes 3932160 | tf_op jit(solution)/shard_map/all_gather | solution.py:299
  110.8 25.2 %collective-permute-start.14 = (bf16[512,1024]{1,0:T(8,128)(2,1)}, bf16[512,1024]{1,0:T(8,128)(2,1)}, u32[]{:S(2)}, u32[]{:S(2)}) collective-permute-start(bf16[512,1024]{1,0:T(8,128)(2,1)} %all-gather.5.cloned.1.call-done.s0_ref.student_ref), channel_id=1, source_target_pairs={{0,24},{4,28},{8,0},{12,4},{16,8},{20,12},{24,16},{28,20},{1,25},{... | collective-permute-start | bytes 3145736 | tf_op jit(solution)/shard_map/ppermute | solution.py:37
  123.6 12.5 %collective-permute-start.18 = (f32[640]{0:T(1024)S(1)}, f32[640]{0:T(1024)S(1)}, u32[]{:S(2)}, u32[]{:S(2)}) collective-permute-start(f32[640]{0:T(1024)S(1)} %concatenate.20), channel_id=1, source_target_pairs={{0,24},{4,28},{8,0},{12,4},{16,8},{20,12},{24,16},{28,20},{1,25},{... | collective-permute-start | bytes 7688 | tf_op jit(solution)/shard_map/ppermute | solution.py:37
  124.2 11.9 %collective-permute-start.19 = (f32[640]{0:T(1024)S(1)}, f32[640]{0:T(1024)S(1)}, u32[]{:S(2)}, u32[]{:S(2)}) collective-permute-start(f32[640]{0:T(1024)S(1)} %concatenate.20), channel_id=1, source_target_pairs={{0,20},{4,0},{8,28},{12,8},{16,4},{20,16},{24,12},{28,24},{1,21},{... | collective-permute-start | bytes 7688 | tf_op jit(solution)/shard_map/ppermute | solution.py:37
  125.7 13.4 %collective-permute-start.21 = (bf16[512,1024]{1,0:T(8,128)(2,1)S(1)}, bf16[512,1024]{1,0:T(8,128)(2,1)}, u32[]{:S(2)}, u32[]{:S(2)}) collective-permute-start(bf16[512,1024]{1,0:T(8,128)(2,1)S(1)} %copy-done), channel_id=1, source_target_pairs={{0,20},{4,0},{8,28},{12,8},{16,4},{20,16},{24,12},{28,24},{1,21},{... | collective-permute-start | bytes 3145736 | tf_op jit(solution)/shard_map/ppermute | solution.py:37
  160.3 36.5 %collective-permute-start.28 = (bf16[256,1024]{1,0:T(8,128)(2,1)}, bf16[256,1024]{1,0:T(8,128)(2,1)}, u32[]{:S(2)}, u32[]{:S(2)}) collective-permute-start(bf16[256,1024]{1,0:T(8,128)(2,1)} %get-tuple-element.73), channel_id=1, source_target_pairs={{0,24},{4,28},{8,0},{12,4},{16,8},{20,12},{24,16},{28,20},{1,25},{... | collective-permute-start | bytes 1572872 | tf_op jit(solution)/shard_map/ppermute | solution.py:37
  170.4 26.5 %collective-permute-start.27 = (bf16[256,1024]{1,0:T(8,128)(2,1)S(1)}, bf16[256,1024]{1,0:T(8,128)(2,1)}, u32[]{:S(2)}, u32[]{:S(2)}) collective-permute-start(bf16[256,1024]{1,0:T(8,128)(2,1)S(1)} %get-tuple-element.74), channel_id=1, source_target_pairs={{0,16},{4,20},{8,24},{12,28},{16,0},{20,4},{24,8},{28,12},{1,17},{... | collective-permute-start | bytes 1572872 | tf_op jit(solution)/shard_map/ppermute | solution.py:37
  171.0 25.9 %collective-permute-start.26 = (bf16[256,1024]{1,0:T(8,128)(2,1)S(1)}, bf16[256,1024]{1,0:T(8,128)(2,1)}, u32[]{:S(2)}, u32[]{:S(2)}) collective-permute-start(bf16[256,1024]{1,0:T(8,128)(2,1)S(1)} %get-tuple-element.72), channel_id=1, source_target_pairs={{0,8},{4,12},{8,16},{12,20},{16,24},{20,28},{24,0},{28,4},{1,9},{5... | collective-permute-start | bytes 1572872 | tf_op jit(solution)/shard_map/ppermute | solution.py:37
  172.6 23.1 %collective-permute-start.25 = (f32[128]{0:T(128)S(1)}, f32[128]{0:T(128)S(1)}, u32[]{:S(2)}, u32[]{:S(2)}) collective-permute-start(f32[128]{0:T(128)S(1)} %compare_select_fusion.10), channel_id=1, source_target_pairs={{0,16},{4,20},{8,24},{12,28},{16,0},{20,4},{24,8},{28,12},{1,17},{... | collective-permute-start | bytes 1544 | tf_op jit(solution)/shard_map/ppermute | solution.py:37
  198.9 27.0 %collective-permute-start.29 = (bf16[256,1024]{1,0:T(8,128)(2,1)S(1)}, bf16[256,1024]{1,0:T(8,128)(2,1)S(1)}, u32[]{:S(2)}, u32[]{:S(2)}) collective-permute-start(bf16[256,1024]{1,0:T(8,128)(2,1)S(1)} %add_convert_fusion.refs_0_), channel_id=1, source_target_pairs={{0,4},{4,0},{8,12},{12,8},{16,20},{20,16},{24,28},{28,24},{1,5},{5... | collective-permute-start | bytes 1572872 | tf_op jit(solution)/shard_map/ppermute | solution.py:37
  199.0 24.7 %collective-permute-start.30 = (bf16[256,1024]{1,0:T(8,128)(2,1)S(1)}, bf16[256,1024]{1,0:T(8,128)(2,1)}, u32[]{:S(2)}, u32[]{:S(2)}) collective-permute-start(bf16[256,1024]{1,0:T(8,128)(2,1)S(1)} %add_convert_fusion.refs_0_), channel_id=1, source_target_pairs={{0,8},{4,12},{8,16},{12,20},{16,24},{20,28},{24,0},{28,4},{1,9},{5... | collective-permute-start | bytes 1572872 | tf_op jit(solution)/shard_map/ppermute | solution.py:37
  199.1 25.6 %collective-permute-start.32 = (bf16[256,1024]{1,0:T(8,128)(2,1)S(1)}, bf16[256,1024]{1,0:T(8,128)(2,1)}, u32[]{:S(2)}, u32[]{:S(2)}) collective-permute-start(bf16[256,1024]{1,0:T(8,128)(2,1)S(1)} %add_convert_fusion.refs_0_), channel_id=1, source_target_pairs={{0,16},{4,20},{8,24},{12,28},{16,0},{20,4},{24,8},{28,12},{1,17},{... | collective-permute-start | bytes 1572872 | tf_op jit(solution)/shard_map/ppermute | solution.py:37
  199.9 24.8 %collective-permute-start.34 = (bf16[256,1024]{1,0:T(8,128)(2,1)S(1)}, bf16[256,1024]{1,0:T(8,128)(2,1)}, u32[]{:S(2)}, u32[]{:S(2)}) collective-permute-start(bf16[256,1024]{1,0:T(8,128)(2,1)S(1)} %add_convert_fusion.refs_0_), channel_id=1, source_target_pairs={{0,24},{4,28},{8,0},{12,4},{16,8},{20,12},{24,16},{28,20},{1,25},{... | collective-permute-start | bytes 1572872 | tf_op jit(solution)/shard_map/ppermute | solution.py:37
  (26 other events, 211.5 us)
Sparse Core Ops, SparseCore 0:
  13.8 60.9 reduce-scatter.1
  83.9 26.8 all-gather.4
  112.4 27.7 all-gather.6
  141.7 62.5 all-gather.8

commit v5 on v4

--- a/solution.py
+++ b/solution.py
@@ -8,6 +8,7 @@
 from jax.sharding import PartitionSpec as P
 
 STOPS = 4
+VMEM_LIMIT = 40 * 1024 * 1024
 MOST_BYTES = 16
 EPS = 1e-06
 BF16 = jnp.bfloat16
@@ -73,10 +74,9 @@
     return total
 
 
-def teacher_side(rows, teacher_ref, rms_ref, s0_ref, s1_ref, s2_ref, s3_ref, small_ref, out_ref):
-    teacher = teacher_ref[...]
+def teacher_terms(rows, stops, teacher, small_ref, windows):
     dteacher = None
-    for at, ref in enumerate((s0_ref, s1_ref, s2_ref, s3_ref)):
+    for at, ref in zip(stops, windows):
         scale = small_ref[at : at + 1, :]
         log_total = small_ref[4 + at : 5 + at, :]
         column = small_ref[8 + at : 9 + at, :].astype(jnp.int32)
@@ -86,9 +86,19 @@
         grads = ((jnp.exp(scores - log_total) - hit) * scale).astype(BF16)
         term = jnp.dot(grads, ref[...], preferred_element_type=F32)
         dteacher = term if dteacher is None else dteacher + term
+    return dteacher
+
+
+def teacher_first(rows, stops, teacher_ref, small_ref, *refs):
+    refs[-1][...] = teacher_terms(rows, stops, teacher_ref[...], small_ref, refs[:-1])
+
+
+def teacher_last(rows, stops, teacher_ref, small_ref, sum_ref, rms_ref, *refs):
+    teacher = teacher_ref[...]
+    dteacher = sum_ref[...] + teacher_terms(rows, stops, teacher, small_ref, refs[:-1])
     full = teacher.astype(F32)
     inner_mean = jnp.mean(dteacher * full, axis=-1, keepdims=True)
-    out_ref[...] = (rms_ref[...] * (dteacher - full * inner_mean)).astype(BF16)
+    refs[-1][...] = (rms_ref[...] * (dteacher - full * inner_mean)).astype(BF16)
 
 
 def teacher_grads_of(teacher, rms, window, small):
@@ -96,20 +106,27 @@
     rows = 256
     whole = pl.BlockSpec((span_block, width), lambda i: (0, 0))
     part = pl.BlockSpec((rows, width), lambda i: (i, 0))
-    return pl.pallas_call(
-        functools.partial(teacher_side, rows),
-        grid=(span_block // rows,),
-        in_specs=[part, pl.BlockSpec((rows, 1), lambda i: (i, 0))] + [whole] * 4 + [pl.BlockSpec(small.shape, lambda i: (0, 0))],
-        out_specs=part,
-        out_shape=jax.ShapeDtypeStruct((span_block, width), BF16),
-        compiler_params=pltpu.CompilerParams(vmem_limit_bytes=48 * 1024 * 1024),
-        cost_estimate=pl.CostEstimate(
-            flops=16 * span_block * span_block * width,
-            bytes_accessed=14 * span_block * width,
-            transcendentals=4 * span_block * span_block,
-        ),
-        name="teacher_side",
-    )(teacher, rms, *window, small)
+    scalars = pl.BlockSpec(small.shape, lambda i: (0, 0))
+
+    def call(body, stops, extra_specs, extra, out_type, name):
+        return pl.pallas_call(
+            functools.partial(body, rows, stops),
+            grid=(span_block // rows,),
+            in_specs=[part, scalars] + extra_specs + [whole] * len(stops),
+            out_specs=part,
+            out_shape=jax.ShapeDtypeStruct((span_block, width), out_type),
+            compiler_params=pltpu.CompilerParams(vmem_limit_bytes=VMEM_LIMIT),
+            cost_estimate=pl.CostEstimate(
+                flops=4 * len(stops) * span_block * span_block * width,
+                bytes_accessed=(8 + 2 * len(stops)) * span_block * width,
+                transcendentals=len(stops) * span_block * span_block,
+            ),
+            name=name,
+        )(teacher, small, *extra, *[window[at] for at in stops])
+
+    dteacher = call(teacher_first, (0, 1, 3), [], (), F32, "teacher_first")
+    rms_spec = pl.BlockSpec((rows, 1), lambda i: (i, 0))
+    return call(teacher_last, (2,), [part, rms_spec], (dteacher, rms), BF16, "teacher_last")
 
 
 def student_side(student_ref, full_ref, scalar_ref, own_ref, others_ref, out_ref):
@@ -319,16 +336,17 @@
     own_terms, total = lax.optimization_barrier((terms, total))
     for by in range(4, blocks, 4):
         terms = terms + permute_blk(own_terms, lambda i, by=by: i - by)
-    loss_mean = jnp.sum(terms) / (span_block * blocks)
 
     came = []
     for by in range(1, chips):
         target = lax.rem(chip + by, chips)
         piece = lax.dynamic_slice_in_dim(narrowed, target * slice_rows, slice_rows, 0)
         came.append(permute_blk(piece, lambda i, by=by: i + 2 * by))
+    *came, terms = lax.optimization_barrier((*came, terms))
+    loss_mean = jnp.sum(terms) / (span_block * blocks)
     for piece in came:
         total = total + piece.astype(F32)
-    total = (total + 0.0 * loss_mean).astype(BF16)
+    total = total.astype(BF16)
     place = positive.astype(jnp.int32)
     stop, place = place // span_block, place % span_block
     at_lane, at_row = place // span_dev, place % span_dev

time: 243 us -> 242 us (level)
  waiting for transfers between devices: 89.7 us -> 85.4 us
  starting transfers between devices: 47.1 us -> 51.2 us
    ppermute x3, waiting for transfers between devices: 37.5 us -> 30.2 us  [scatter_narrow(): lax.ppermute(piece, 'narrow', [(i, (i + by) % count) for i in range(count)])]
    ppermute x6, starting transfers between devices: 8.05 us -> 15.1 us  [gather_narrow(): lax.ppermute(x, 'narrow', [(i, (i + by) % count) for i in range(count)])]
    all_gather x1, waiting for transfers between devices: 1.75 us -> 8.66 us  [shards(): others = lax.all_gather(others, 'narrow', axis=0)]
    ppermute x25, waiting for transfers between devices: 41.2 us -> 36.1 us  [permute_blk(): lax.ppermute(x, 'blk', [(i, target(i) % count) for i in range(count)])]
    ppermute x25, starting transfers between devices: 27.1 us -> 23.2 us  [permute_blk(): lax.ppermute(x, 'blk', [(i, target(i) % count) for i in range(count)])]
    unnamed x22 -> x32, local copies, waits for them, and re-layouts: 6.41 us -> 9.37 us
    pallas_call x1 -> x2, Pallas kernels: 7.79 us -> 7.93 us  [call(): pl.pallas_call(functools.partial(body, rows, stops), grid=(span_block //...]
  transfers between devices with their start and end apart: 40 -> 40, of which waited for: 20 -> 16; matrix products, arithmetic and copies ran while one was open for 21% -> 20% of each run, Pallas kernels for 7% -> 7%
where the time goes in v5:
time: 242 us; the launch traced here: 241 us
  waiting for transfers between devices  85.4 us (35%)
  starting transfers between devices  51.2 us (21%)
  matrix products  33.1 us (14%)
  Pallas kernels  23.5 us (10%)
  local copies, waits for them, and re-layouts  17.3 us (7%)
  between operations  16.7 us (7%)
  other arithmetic  14 us (6%)
    ppermute x25, waiting for transfers between devices, permute_blk(): lax.ppermute(x, 'blk', [(i, target(i) % count) for i in range(count)])  36.1 us
    ppermute x3, waiting for transfers between devices, scatter_narrow(): lax.ppermute(piece, 'narrow', [(i, (i + by) % count) for i in range(count)])  30.2 us
    ppermute x25, starting transfers between devices, permute_blk(): lax.ppermute(x, 'blk', [(i, target(i) % count) for i in range(count)])  23.2 us
    ppermute x6, starting transfers between devices, gather_narrow(): lax.ppermute(x, 'narrow', [(i, (i + by) % count) for i in range(count)])  15.1 us
    unnamed x32, local copies, waits for them, and re-layouts  9.37 us
    pallas_call x1, Pallas kernels, span_grads_of(): pl.pallas_call(student_side, grid=(span_block // rows,), in_specs=[part,...  9.1 us
    dot_general x2, matrix products, contract_last(): lax.dot_general(left, right, (((1,), (1,)), ((), ())), preferred_element_...  8.86 us
    all_gather x1, waiting for transfers between devices, shards(): others = lax.all_gather(others, 'narrow', axis=0)  8.66 us
  transfers between devices with their start and end apart: 40, of which 16 were waited for; matrix products, arithmetic and copies ran while one was open for 20% of the time, Pallas kernels for 7%

profile of v5, /device:TPU:0, one launch (start us, length us, event | category | flops | bytes accessed | tf_op | source)
XLA Modules:
  0.0 241.2 jit_solution(12987382835253637689)
XLA Ops:
  7.2 6.5 %fusion.51 = f32[512,1024]{1,0:T(8,128)} fusion(bf16[512,2048]{1,0:T(8,128)(2,1)} %param.9, bf16[2048,1024]{1,0:T(8,128)(2,1)} %param.10), kind=kOutput, calls=%fused_computation.120 | convolution fusion | flops 2147483648 | bytes 8388608 | tf_op jit(solution)/shard_map/dot_general | solution.py:237
  14.6 4.9 %collective-permute-start = (bf16[16,2048]{1,0:T(8,128)(2,1)S(1)}, bf16[16,2048]{1,0:T(8,128)(2,1)S(1)}, u32[]{:S(2)}, u32[]{:S(2)}) collective-permute-start(bf16[16,2048]{1,0:T(8,128)(2,1)S(1)} %get-tuple-element.85), channel_id=1, source_target_pairs={{0,1},{1,2},{2,3},{4,5},{5,6},{6,7},{8,9},{9,10},{10,11},{12,13},{... | collective-permute-start | bytes 196616 | tf_op jit(solution)/shard_map/ppermute | solution.py:231
  23.4 7.0 %fusion = f32[512,1024]{1,0:T(8,128)} fusion(bf16[512,2048]{1,0:T(8,128)(2,1)} %param.7, bf16[2048,1024]{1,0:T(8,128)(2,1)} %param.8, s32[512]{0:T(512)S(1)} %iota_add_fusion, s32[512]{0:T(512)S(1)} %bitcast.127, s32[512]{0:T(512)S(1)} %bitcast.111), kind=kOutput, calls=%fused_computation.8 | convolution fusion | flops 2685665280 | bytes 8394752 | tf_op jit(solution)/shard_map/dot_general | solution.py:269
  30.5 5.4 %multiply_reduce_fusion = (f32[512]{0:T(512)S(1)}, f32[512,1024]{1,0:T(8,128)}) fusion(f32[512]{0:T(512)S(1)} %bitcast.114, f32[512,1024]{1,0:T(8,128)} %fusion, bf16[2048,1024]{1,0:T(8,128)(2,1)} %param.8, bf16[16,2048]{1,0:T(8,128)(2,1)S(1)} %collective-permute-done.1, bf16[16,2048]{1,0:T(8,128)(2,1)S(1)} %collective-permute-done, s32[32]{0:T(128)S(1)} %pad_add_fusion, ...), kind=kOutput, calls=%fused_computation.2 | convolution fusion | flops 170212864 | bytes 8528000 | tf_op jit(solution)/shard_map/dot_general | solution.py:269
  38.6 2.7 %collective-permute-start.2 = (bf16[128,1024]{1,0:T(8,128)(2,1)}, bf16[128,1024]{1,0:T(8,128)(2,1)}, u32[]{:S(2)}, u32[]{:S(2)}) collective-permute-start(bf16[128,1024]{1,0:T(8,128)(2,1)} %get-tuple-element.87), channel_id=1, source_target_pairs={{0,1},{1,2},{2,3},{3,0},{4,5},{5,6},{6,7},{7,4},{8,9},{9,10},{10,1... | collective-permute-start | bytes 786440 | tf_op jit(solution)/shard_map/ppermute | solution.py:73
  41.3 2.6 %collective-permute-start.3 = (bf16[128,1024]{1,0:T(8,128)(2,1)}, bf16[128,1024]{1,0:T(8,128)(2,1)}, u32[]{:S(2)}, u32[]{:S(2)}) collective-permute-start(bf16[128,1024]{1,0:T(8,128)(2,1)} %get-tuple-element.89), channel_id=1, source_target_pairs={{0,2},{1,3},{2,0},{3,1},{4,6},{5,7},{6,4},{7,5},{8,10},{9,11},{10,... | collective-permute-start | bytes 786440 | tf_op jit(solution)/shard_map/ppermute | solution.py:73
  45.2 11.3 %collective-permute-done.2 = bf16[128,1024]{1,0:T(8,128)(2,1)} collective-permute-done((bf16[128,1024]{1,0:T(8,128)(2,1)}, bf16[128,1024]{1,0:T(8,128)(2,1)}, u32[]{:S(2)}, u32[]{:S(2)}) %collective-permute-start.2) | collective-permute-done | bytes 262176 | tf_op jit(solution)/shard_map/ppermute | solution.py:73
  56.6 18.6 %collective-permute-done.3 = bf16[128,1024]{1,0:T(8,128)(2,1)} collective-permute-done((bf16[128,1024]{1,0:T(8,128)(2,1)}, bf16[128,1024]{1,0:T(8,128)(2,1)}, u32[]{:S(2)}, u32[]{:S(2)}) %collective-permute-start.3) | collective-permute-done | bytes 262176 | tf_op jit(solution)/shard_map/ppermute | solution.py:73
  83.7 7.7 %collective-permute-start.8 = (f32[2,128]{1,0:T(2,128)S(1)}, f32[2,128]{1,0:T(2,128)S(1)}, u32[]{:S(2)}, u32[]{:S(2)}) collective-permute-start(f32[2,128]{1,0:T(2,128)S(1)} %pad_maximum_fusion.3), channel_id=1, source_target_pairs={{0,1},{1,2},{2,3},{3,0},{4,5},{5,6},{6,7},{7,4},{8,9},{9,10},{10,1... | collective-permute-start | bytes 3080 | tf_op jit(solution)/shard_map/ppermute | solution.py:51
  92.2 3.0 %constant_dynamic-slice_fusion.4 = (bf16[512,1024]{1,0:T(8,128)(2,1)}, bf16[512,1024]{1,0:T(8,128)(2,1)}) fusion(bf16[512,2048]{1,0:T(8,128)(2,1)} %param.9, s32[]{:T(128)S(6)} %select_n.256, s32[]{:T(128)S(6)} %select_n.247), kind=kLoop, calls=%fused_computation.73 | loop fusion | bytes 4194312 | tf_op jit(solution)/shard_map/dynamic_slice | solution.py:226
  105.0 6.0 %all-gather.5.cloned.1.call-done.refs_0_.student_ref = bf16[512,1024]{1,0:T(8,128)(2,1)} async-done(((bf16[128,1024]{1,0:T(8,128)(2,1)}), bf16[512,1024]{1,0:T(8,128)(2,1)}) %all-gather.5.cloned.1.call-update) | async-done | bytes 1048592 | tf_op jit(solution)/shard_map/all_gather | solution.py:277
  111.1 2.5 %collective-permute-start.14 = (bf16[512,1024]{1,0:T(8,128)(2,1)}, bf16[512,1024]{1,0:T(8,128)(2,1)}, u32[]{:S(2)}, u32[]{:S(2)}) collective-permute-start(bf16[512,1024]{1,0:T(8,128)(2,1)} %all-gather.5.cloned.1.call-done.refs_0_.student_ref), channel_id=1, source_target_pairs={{0,24},{4,28},{8,0},{12,4},{16,8},{20,12},{24,16},{28,20},{1,25},{... | collective-permute-start | bytes 3145736 | tf_op jit(solution)/shard_map/ppermute | solution.py:38
  118.3 2.4 collective-permute-start.17
  125.7 10.7 %collective-permute-done.18 = f32[640]{0:T(1024)S(1)} collective-permute-done((f32[640]{0:T(1024)S(1)}, f32[640]{0:T(1024)S(1)}, u32[]{:S(2)}, u32[]{:S(2)}) %collective-permute-start.18) | collective-permute-done | bytes 2592 | tf_op jit(solution)/shard_map/ppermute | solution.py:38
  142.6 5.8 %teacher_first.1.sum_ref = f32[512,1024]{1,0:T(8,128)S(1)} custom-call(bf16[512,1024]{1,0:T(8,128)(2,1)S(1)} %copy-done, f32[12,512]{1,0:T(8,128)S(1)} %stack.92.small_ref, bf16[512,1024]{1,0:T(8,128)(2,1)S(1)} %copy-done.4, bf16[512,1024]{1,0:T(8,128)(2,1)} %collective-permute-done.14.refs_1_, bf16[512,1024]{1,0:T(8,128)(2,1)} %collective-permute-done.21.refs_2_), custom_call_target="tpu_custom_call" | custom-call | flops 3221225472 | bytes 7340032 | tf_op jit(solution)/shard_map/teacher_first/pallas_call | solution.py:112
  148.4 2.5 %collective-permute-done.22.refs_0_ = bf16[512,1024]{1,0:T(8,128)(2,1)S(1)} collective-permute-done((bf16[512,1024]{1,0:T(8,128)(2,1)}, bf16[512,1024]{1,0:T(8,128)(2,1)S(1)}, u32[]{:S(2)}, u32[]{:S(2)}) %collective-permute-start.22) | collective-permute-done | bytes 1048608 | tf_op jit(solution)/shard_map/ppermute | solution.py:38
  156.2 2.5 %fusion.52 = f32[1024,1024]{1,0:T(8,128)S(1)} fusion(bf16[512,1024]{1,0:T(8,128)(2,1)} %get-tuple-element.38, bf16[512,1024]{1,0:T(8,128)(2,1)S(1)} %teacher_last.1), kind=kOutput, calls=%fused_computation.121 | convolution fusion | flops 1073741824 | bytes 6291456 | tf_op jit(solution)/shard_map/dot_general | solution.py:29
  160.2 2.8 %fusion.53 = f32[1024,1024]{1,0:T(8,128)S(1)} fusion(bf16[512,1024]{1,0:T(8,128)(2,1)} %collective-permute-done.24, bf16[512,1024]{1,0:T(8,128)(2,1)} %collective-permute-done.23), kind=kOutput, calls=%fused_computation.122 | convolution fusion | flops 1073741824 | bytes 6291456 | tf_op jit(solution)/shard_map/dot_general | solution.py:29
  164.7 2.9 %collective-permute-start.25 = (bf16[256,1024]{1,0:T(8,128)(2,1)S(1)}, bf16[256,1024]{1,0:T(8,128)(2,1)S(1)}, u32[]{:S(2)}, u32[]{:S(2)}) collective-permute-start(bf16[256,1024]{1,0:T(8,128)(2,1)S(1)} %get-tuple-element.82), channel_id=1, source_target_pairs={{0,8},{4,12},{8,16},{12,20},{16,24},{20,28},{24,0},{28,4},{1,9},{5... | collective-permute-start | bytes 1572872 | tf_op jit(solution)/shard_map/ppermute | solution.py:38
  171.9 20.3 %collective-permute-done.28 = f32[128]{0:T(128)S(1)} collective-permute-done((f32[128]{0:T(128)S(1)}, f32[128]{0:T(128)S(1)}, u32[]{:S(2)}, u32[]{:S(2)}) %collective-permute-start.28) | collective-permute-done | bytes 544 | tf_op jit(solution)/shard_map/ppermute | solution.py:38
  196.0 8.7 %all-gather.9.cloned.1.call-done = bf16[1536,1024]{1,0:T(8,128)(2,1)} async-done(((bf16[384,1024]{1,0:T(8,128)(2,1)}), bf16[1536,1024]{1,0:T(8,128)(2,1)}) %all-gather.9.cloned.1.call-update) | async-done | bytes 3145744 | tf_op jit(solution)/shard_map/all_gather | solution.py:316
  207.1 9.1 %student_side.1 = bf16[512,1024]{1,0:T(8,128)(2,1)S(1)} custom-call(bf16[512,1024]{1,0:T(8,128)(2,1)S(1)} %copy-done.5, f32[512,1024]{1,0:T(8,128)S(1)} %get-tuple-element.79.full_ref, f32[512,9]{1,0:T(8,128)S(1)} %copy.69.scalar_ref, bf16[512,1024]{1,0:T(8,128)(2,1)S(1)} %copy-done.1, bf16[4,384,1024]{2,1,0:T(8,128)(2,1)} %bitcast.133), custom_call_target="tpu_custom_call" | custom-call | flops 4294967296 | bytes 8388608 | tf_op jit(solution)/shard_map/student_side/pallas_call | solution.py:158
  217.2 6.9 %convolution_convert_fusion = bf16[512,2048]{1,0:T(8,128)(2,1)} fusion(bf16[2048,1024]{1,0:T(8,128)(2,1)} %param.8, bf16[512,1024]{1,0:T(8,128)(2,1)} %copy-done.6, s32[512]{0:T(512)S(1)} %iota_add_fusion, s32[512]{0:T(512)S(1)} %bitcast.129, s32[512]{0:T(512)S(1)} %bitcast.113), kind=kOutput, calls=%fused_computation | convolution fusion | flops 2686713856 | bytes 7346176 | tf_op jit(solution)/shard_map/dot_general | solution.py:33
  227.0 6.5 %assemble.1 = f32[2048,1024]{1,0:T(8,128)} custom-call(s32[8]{0:T(128)S(1)} %stack.103.order_ref, bf16[256,1024]{1,0:T(8,128)(2,1)S(1)} %add_convert_fusion.refs_0_, bf16[256,1024]{1,0:T(8,128)(2,1)} %collective-permute-done.29.refs_1_, bf16[256,1024]{1,0:T(8,128)(2,1)} %collective-permute-done.30.refs_2_, ...), custom_call_target="tpu_custom_call" | custom-call | flops 2097152 | bytes 12582912 | tf_op jit(solution)/shard_map/assemble/pallas_call | solution.py:191
  (181 shorter events, 65.2 us)
Async XLA Ops:
  7.2 70.2 %reduce-scatter.2.cloned.1.call-start = ((), (), s32[]{:S(2)}) async-start(), calls=%async_computation.1 | async-start | bytes 2621440 | tf_op jit(solution)/shard_map/reduce_scatter | solution.py:239
  13.7 97.3 %all-gather.5.cloned.1.call-start = ((), (), s32[]{:S(2)}) async-start(), calls=%async_computation.2 | async-start | bytes 1310720 | tf_op jit(solution)/shard_map/all_gather | solution.py:277
  14.6 15.8 %collective-permute-start = (bf16[16,2048]{1,0:T(8,128)(2,1)S(1)}, bf16[16,2048]{1,0:T(8,128)(2,1)S(1)}, u32[]{:S(2)}, u32[]{:S(2)}) collective-permute-start(bf16[16,2048]{1,0:T(8,128)(2,1)S(1)} %get-tuple-element.85), channel_id=1, source_target_pairs={{0,1},{1,2},{2,3},{4,5},{5,6},{6,7},{8,9},{9,10},{10,11},{12,13},{... | collective-permute-start | bytes 196616 | tf_op jit(solution)/shard_map/ppermute | solution.py:231
  38.6 17.9 %collective-permute-start.2 = (bf16[128,1024]{1,0:T(8,128)(2,1)}, bf16[128,1024]{1,0:T(8,128)(2,1)}, u32[]{:S(2)}, u32[]{:S(2)}) collective-permute-start(bf16[128,1024]{1,0:T(8,128)(2,1)} %get-tuple-element.87), channel_id=1, source_target_pairs={{0,1},{1,2},{2,3},{3,0},{4,5},{5,6},{6,7},{7,4},{8,9},{9,10},{10,1... | collective-permute-start | bytes 786440 | tf_op jit(solution)/shard_map/ppermute | solution.py:73
  41.3 33.9 %collective-permute-start.3 = (bf16[128,1024]{1,0:T(8,128)(2,1)}, bf16[128,1024]{1,0:T(8,128)(2,1)}, u32[]{:S(2)}, u32[]{:S(2)}) collective-permute-start(bf16[128,1024]{1,0:T(8,128)(2,1)} %get-tuple-element.89), channel_id=1, source_target_pairs={{0,2},{1,3},{2,0},{3,1},{4,6},{5,7},{6,4},{7,5},{8,10},{9,11},{10,... | collective-permute-start | bytes 786440 | tf_op jit(solution)/shard_map/ppermute | solution.py:73
  43.9 31.5 %collective-permute-start.4 = (bf16[128,1024]{1,0:T(8,128)(2,1)S(1)}, bf16[128,1024]{1,0:T(8,128)(2,1)}, u32[]{:S(2)}, u32[]{:S(2)}) collective-permute-start(bf16[128,1024]{1,0:T(8,128)(2,1)S(1)} %get-tuple-element.88), channel_id=1, source_target_pairs={{0,3},{1,0},{2,1},{3,2},{4,7},{5,4},{6,5},{7,6},{8,11},{9,8},{10,9... | collective-permute-start | bytes 786440 | tf_op jit(solution)/shard_map/ppermute | solution.py:73
  77.4 62.7 %all-gather.7.cloned.1.call-start = ((), (), s32[]{:S(2)}) async-start(), calls=%async_computation.3 | async-start | bytes 1310720 | tf_op jit(solution)/shard_map/all_gather | solution.py:290
  79.8 20.5 %collective-permute-start.5 = (bf16[128,1024]{1,0:T(8,128)(2,1)S(1)}, bf16[128,1024]{1,0:T(8,128)(2,1)S(1)}, u32[]{:S(2)}, u32[]{:S(2)}) collective-permute-start(bf16[128,1024]{1,0:T(8,128)(2,1)S(1)} %multiply_convert_fusion), channel_id=1, source_target_pairs={{0,4},{4,8},{8,12},{12,16},{16,20},{20,24},{24,28},{28,0},{1,5},{5... | collective-permute-start | bytes 786440 | tf_op jit(solution)/shard_map/ppermute | solution.py:38
  80.0 21.0 %collective-permute-start.6 = (bf16[128,1024]{1,0:T(8,128)(2,1)S(1)}, bf16[128,1024]{1,0:T(8,128)(2,1)S(1)}, u32[]{:S(2)}, u32[]{:S(2)}) collective-permute-start(bf16[128,1024]{1,0:T(8,128)(2,1)S(1)} %multiply_convert_fusion), channel_id=1, source_target_pairs={{0,8},{4,12},{8,16},{12,20},{16,24},{20,28},{24,0},{28,4},{1,9},{5... | collective-permute-start | bytes 786440 | tf_op jit(solution)/shard_map/ppermute | solution.py:38
  81.4 20.3 %collective-permute-start.7 = (bf16[128,1024]{1,0:T(8,128)(2,1)S(1)}, bf16[128,1024]{1,0:T(8,128)(2,1)}, u32[]{:S(2)}, u32[]{:S(2)}) collective-permute-start(bf16[128,1024]{1,0:T(8,128)(2,1)S(1)} %multiply_convert_fusion), channel_id=1, source_target_pairs={{0,12},{4,16},{8,20},{12,24},{16,28},{20,0},{24,4},{28,8},{1,13},{... | collective-permute-start | bytes 786440 | tf_op jit(solution)/shard_map/ppermute | solution.py:38
  111.0 93.6 %all-gather.9.cloned.1.call-start = ((), (), s32[]{:S(2)}) async-start(), calls=%async_computation.4 | async-start | bytes 3932160 | tf_op jit(solution)/shard_map/all_gather | solution.py:316
  111.1 25.2 %collective-permute-start.14 = (bf16[512,1024]{1,0:T(8,128)(2,1)}, bf16[512,1024]{1,0:T(8,128)(2,1)}, u32[]{:S(2)}, u32[]{:S(2)}) collective-permute-start(bf16[512,1024]{1,0:T(8,128)(2,1)} %all-gather.5.cloned.1.call-done.refs_0_.student_ref), channel_id=1, source_target_pairs={{0,24},{4,28},{8,0},{12,4},{16,8},{20,12},{24,16},{28,20},{1,25},{... | collective-permute-start | bytes 3145736 | tf_op jit(solution)/shard_map/ppermute | solution.py:38
  123.5 12.9 %collective-permute-start.18 = (f32[640]{0:T(1024)S(1)}, f32[640]{0:T(1024)S(1)}, u32[]{:S(2)}, u32[]{:S(2)}) collective-permute-start(f32[640]{0:T(1024)S(1)} %concatenate.20), channel_id=1, source_target_pairs={{0,24},{4,28},{8,0},{12,4},{16,8},{20,12},{24,16},{28,20},{1,25},{... | collective-permute-start | bytes 7688 | tf_op jit(solution)/shard_map/ppermute | solution.py:38
  124.1 12.3 %collective-permute-start.19 = (f32[640]{0:T(1024)S(1)}, f32[640]{0:T(1024)S(1)}, u32[]{:S(2)}, u32[]{:S(2)}) collective-permute-start(f32[640]{0:T(1024)S(1)} %concatenate.20), channel_id=1, source_target_pairs={{0,20},{4,0},{8,28},{12,8},{16,4},{20,16},{24,12},{28,24},{1,21},{... | collective-permute-start | bytes 7688 | tf_op jit(solution)/shard_map/ppermute | solution.py:38
  124.1 12.3 %collective-permute-start.20 = (f32[640]{0:T(1024)S(1)}, f32[640]{0:T(1024)S(1)}, u32[]{:S(2)}, u32[]{:S(2)}) collective-permute-start(f32[640]{0:T(1024)S(1)} %concatenate.20), channel_id=1, source_target_pairs={{0,28},{4,24},{8,4},{12,0},{16,12},{20,8},{24,20},{28,16},{1,29},{... | collective-permute-start | bytes 7688 | tf_op jit(solution)/shard_map/ppermute | solution.py:38
  136.6 14.3 %collective-permute-start.22 = (bf16[512,1024]{1,0:T(8,128)(2,1)}, bf16[512,1024]{1,0:T(8,128)(2,1)S(1)}, u32[]{:S(2)}, u32[]{:S(2)}) collective-permute-start(bf16[512,1024]{1,0:T(8,128)(2,1)} %all-gather.5.cloned.1.call-done.refs_0_.student_ref), channel_id=1, source_target_pairs={{0,20},{4,0},{8,28},{12,8},{16,4},{20,16},{24,12},{28,24},{1,21},{... | collective-permute-start | bytes 3145736 | tf_op jit(solution)/shard_map/ppermute | solution.py:38
  164.7 27.6 %collective-permute-start.25 = (bf16[256,1024]{1,0:T(8,128)(2,1)S(1)}, bf16[256,1024]{1,0:T(8,128)(2,1)S(1)}, u32[]{:S(2)}, u32[]{:S(2)}) collective-permute-start(bf16[256,1024]{1,0:T(8,128)(2,1)S(1)} %get-tuple-element.82), channel_id=1, source_target_pairs={{0,8},{4,12},{8,16},{12,20},{16,24},{20,28},{24,0},{28,4},{1,9},{5... | collective-permute-start | bytes 1572872 | tf_op jit(solution)/shard_map/ppermute | solution.py:38
  167.5 24.7 %collective-permute-start.26 = (bf16[256,1024]{1,0:T(8,128)(2,1)S(1)}, bf16[256,1024]{1,0:T(8,128)(2,1)S(1)}, u32[]{:S(2)}, u32[]{:S(2)}) collective-permute-start(bf16[256,1024]{1,0:T(8,128)(2,1)S(1)} %get-tuple-element.81), channel_id=1, source_target_pairs={{0,16},{4,20},{8,24},{12,28},{16,0},{20,4},{24,8},{28,12},{1,17},{... | collective-permute-start | bytes 1572872 | tf_op jit(solution)/shard_map/ppermute | solution.py:38
  169.0 23.2 %collective-permute-start.27 = (bf16[256,1024]{1,0:T(8,128)(2,1)S(1)}, bf16[256,1024]{1,0:T(8,128)(2,1)S(1)}, u32[]{:S(2)}, u32[]{:S(2)}) collective-permute-start(bf16[256,1024]{1,0:T(8,128)(2,1)S(1)} %get-tuple-element.80), channel_id=1, source_target_pairs={{0,24},{4,28},{8,0},{12,4},{16,8},{20,12},{24,16},{28,20},{1,25},{... | collective-permute-start | bytes 1572872 | tf_op jit(solution)/shard_map/ppermute | solution.py:38
  169.2 23.0 %collective-permute-start.28 = (f32[128]{0:T(128)S(1)}, f32[128]{0:T(128)S(1)}, u32[]{:S(2)}, u32[]{:S(2)}) collective-permute-start(f32[128]{0:T(128)S(1)} %compare_select_fusion.10), channel_id=1, source_target_pairs={{0,16},{4,20},{8,24},{12,28},{16,0},{20,4},{24,8},{28,12},{1,17},{... | collective-permute-start | bytes 1544 | tf_op jit(solution)/shard_map/ppermute | solution.py:38
  192.5 24.6 %collective-permute-start.34 = (bf16[256,1024]{1,0:T(8,128)(2,1)S(1)}, bf16[256,1024]{1,0:T(8,128)(2,1)S(1)}, u32[]{:S(2)}, u32[]{:S(2)}) collective-permute-start(bf16[256,1024]{1,0:T(8,128)(2,1)S(1)} %add_convert_fusion.refs_0_), channel_id=1, source_target_pairs={{0,24},{4,28},{8,0},{12,4},{16,8},{20,12},{24,16},{28,20},{1,25},{... | collective-permute-start | bytes 1572872 | tf_op jit(solution)/shard_map/ppermute | solution.py:38
  194.5 29.5 %collective-permute-start.32 = (bf16[256,1024]{1,0:T(8,128)(2,1)S(1)}, bf16[256,1024]{1,0:T(8,128)(2,1)}, u32[]{:S(2)}, u32[]{:S(2)}) collective-permute-start(bf16[256,1024]{1,0:T(8,128)(2,1)S(1)} %add_convert_fusion.refs_0_), channel_id=1, source_target_pairs={{0,16},{4,20},{8,24},{12,28},{16,0},{20,4},{24,8},{28,12},{1,17},{... | collective-permute-start | bytes 1572872 | tf_op jit(solution)/shard_map/ppermute | solution.py:38
  196.0 28.6 %collective-permute-start.30 = (bf16[256,1024]{1,0:T(8,128)(2,1)S(1)}, bf16[256,1024]{1,0:T(8,128)(2,1)}, u32[]{:S(2)}, u32[]{:S(2)}) collective-permute-start(bf16[256,1024]{1,0:T(8,128)(2,1)S(1)} %add_convert_fusion.refs_0_), channel_id=1, source_target_pairs={{0,8},{4,12},{8,16},{12,20},{16,24},{20,28},{24,0},{28,4},{1,9},{5... | collective-permute-start | bytes 1572872 | tf_op jit(solution)/shard_map/ppermute | solution.py:38
  196.0 30.0 %collective-permute-start.29 = (bf16[256,1024]{1,0:T(8,128)(2,1)S(1)}, bf16[256,1024]{1,0:T(8,128)(2,1)}, u32[]{:S(2)}, u32[]{:S(2)}) collective-permute-start(bf16[256,1024]{1,0:T(8,128)(2,1)S(1)} %add_convert_fusion.refs_0_), channel_id=1, source_target_pairs={{0,4},{4,0},{8,12},{12,8},{16,20},{20,16},{24,28},{28,24},{1,5},{5... | collective-permute-start | bytes 1572872 | tf_op jit(solution)/shard_map/ppermute | solution.py:38
  (31 other events, 206.8 us)
Sparse Core Ops, SparseCore 0:
  13.8 63.0 reduce-scatter.1
  78.6 32.3 all-gather.4
  112.7 27.3 all-gather.6
  141.6 62.9 all-gather.8
